TPU v7x, 32 devices: a whole 2x2x4 slice. The times are simulated.
32 devices in a mesh: groups: 2 (over y), span: 8 (over z, x), sub: 2 (over core).
Axes of the slice: x: 2, y: 2, z: 4, core: 2. Of those that a mesh axis runs over, the one named last changes fastest.
Arguments:
- child_weight: float32 [4096, 128], P(('groups', 'span', 'sub')), parts along dimension 0, may hold values from 0.02 to 1
- child_mean: float32 [3, 4096, 128], P(None, ('groups', 'span', 'sub')), parts along dimension 1, may hold values from -6 to 6
- child_factor: float32 [6, 4096, 128], P(None, ('groups', 'span', 'sub')), parts along dimension 1, may hold values from 0.2 to 1
- child_colour: bfloat16 [48, 4096, 128], P(None, ('groups', 'span', 'sub')), parts along dimension 1, may hold values from -6 to 6
- child_dest: int32 [4096], P(('groups', 'span', 'sub')), parts along dimension 0, may hold values from 0 to 7, as said below
- child_slot: int32 [4096], P(('groups', 'span', 'sub')), parts along dimension 0, may hold values from 0 to 63
- child_row: int32 [4096, 128], P(('groups', 'span', 'sub')), parts along dimension 0, may hold values from 0 to 127
- live_blocks: int32 [32], P(('groups', 'span', 'sub')), parts along dimension 0, may hold values from 96 to 128, as said below
- parent_owner: int32 [1024], P(('groups', 'span', 'sub')), parts along dimension 0, may hold values from 0 to 7, as said below
- parent_slot: int32 [1024], P(('groups', 'span', 'sub')), parts along dimension 0, may hold values from 0 to 15
- parent_row: int32 [1024, 128], P(('groups', 'span', 'sub')), parts along dimension 0, may hold values from 0 to 127
Outputs:
- level_one: float32 [58, 1024, 128], P(None, ('groups', 'span', 'sub')), parts along dimension 1
- level_two: float32 [58, 256, 128], P(None, ('groups', 'span', 'sub')), parts along dimension 1
There are 2 independent parts, one for each index of `groups`. A program takes and returns all parts, laid end to end along the dimension named above; each array names one. Nothing has to cross between parts.
Inputs may be any that keep to these rules, and one draw needn't show every extreme that they name: `child_dest`: among the live blocks of one device at most 32 name the same owner span. `live_blocks`: the live child blocks of a device are its first ones; the others are ignored. `parent_owner`: among the level-one blocks of one device at most 4 name the same owner span.
All inputs are finite; a program needn't handle non-finite values.
Results may differ from a plain program's by a relative error of at most 0.0003.
Values sent between devices are 32-bit elements; how exact they have to be, the bound alone decides.
No kernel may reach another device: no remote copies, remote signals or barrier semaphores. Data moves between devices by JAX's collectives and lax.ppermute only.
A program may use at most 64 MiB of HBM per device.

v0:
```python
import math

import jax
import jax.numpy as jnp
from jax import lax
from jax.sharding import PartitionSpec as P

PB_DEV = 32
GB_DEV = 8


PAIRS = ((0, 0), (0, 1), (0, 2), (1, 1), (1, 2), (2, 2))
WEIGHT_FLOOR = 0.1


def covariance(factor):
    return jnp.stack(
        [
            factor[0] * factor[0],
            factor[0] * factor[1],
            factor[0] * factor[3],
            factor[1] * factor[1] + factor[2] * factor[2],
            factor[1] * factor[3] + factor[2] * factor[4],
            factor[3] * factor[3] + factor[4] * factor[4] + factor[5] * factor[5],
        ]
    )


def moment_sums(weight, centres, factor, colour):
    outer = jnp.stack([centres[first] * centres[second] for first, second in PAIRS])
    return jnp.concatenate(
        [
            weight[None],
            weight * centres,
            weight * (covariance(factor) + outer),
            weight * colour.astype(jnp.float32),
        ],
        0,
    )


def match_moments(sums):
    whole_weight = sums[0]
    divisor = jnp.maximum(whole_weight, WEIGHT_FLOOR)
    centre = sums[1:4] / divisor
    centre_outer = jnp.stack([centre[first] * centre[second] for first, second in PAIRS])
    spread = sums[4:10] / divisor - centre_outer
    colour_mean = sums[10:] / divisor
    return jnp.concatenate([whole_weight[None], centre, spread, colour_mean], 0)


def earlier_same(owners):
    position = jnp.arange(owners.shape[0], dtype=jnp.int32)
    same_owner = (owners[:, None] == owners[None, :]) & (position[None, :] < position[:, None])
    return jnp.sum(same_owner.astype(jnp.int32), 1)


def fold_rows(values, row_picks):
    block_total = values.shape[1]
    width = values.shape[2]
    group_size = math.gcd(block_total, 16)
    row_labels = jnp.arange(width, dtype=jnp.int32)

    def fold_step(turn_index, result):
        start = turn_index * group_size
        block_part = lax.dynamic_slice_in_dim(values, start, group_size, 1)
        picks_part = lax.dynamic_slice_in_dim(row_picks, start, group_size, 0)
        row_table = (picks_part[:, :, None] == row_labels).astype(jnp.float32)
        folded_part = jnp.einsum(
            "cbr,brj->cbj", block_part, row_table, precision=lax.Precision.HIGHEST
        )
        return lax.dynamic_update_slice_in_dim(result, folded_part, start, 1)

    return lax.fori_loop(
        0, block_total // group_size, fold_step, jnp.zeros(values.shape, jnp.float32)
    )


def place_blocks(values, block_picks, block_count):
    block_table = (block_picks[:, None] == jnp.arange(block_count, dtype=jnp.int32)).astype(
        jnp.float32
    )
    return jnp.einsum("csj,sp->cpj", values, block_table, precision=lax.Precision.HIGHEST)


def seam(partial_value, per_device):
    whole_sum = lax.psum(partial_value, "sub")
    return lax.dynamic_slice_in_dim(whole_sum, lax.axis_index("sub") * per_device, per_device, 1)


def body(
    child_weight,
    child_mean,
    child_factor,
    child_colour,
    child_dest,
    child_slot,
    child_row,
    live_blocks,
    parent_owner,
    parent_slot,
    parent_row,
):
    spans = lax.axis_size("span")
    sub_count = lax.axis_size("sub")
    block_count = child_weight.shape[0]
    row_count = child_weight.shape[1]
    components = 10 + child_colour.shape[0]
    cap_one = max(2, (2 * block_count + spans - 1) // spans)
    slot_total = spans * cap_one
    parent_span = PB_DEV * sub_count
    moments = moment_sums(child_weight, child_mean, child_factor, child_colour)
    position = jnp.arange(block_count, dtype=jnp.int32)
    is_live = position < live_blocks[0]
    slot_index = jnp.where(is_live, child_dest * cap_one + earlier_same(child_dest), slot_total)
    outgoing_shape = (components, slot_total, row_count)
    outgoing = jnp.zeros(outgoing_shape, jnp.float32).at[:, slot_index].set(moments, mode="drop")
    targets = child_slot[:, None] * row_count + child_row
    target_rows = (
        jnp.zeros((1, slot_total, row_count), jnp.int32).at[0, slot_index].set(targets, mode="drop")
    )
    received, received_rows = (
        lax.all_to_all(outgoing, "span", split_axis=1, concat_axis=1, tiled=True),
        lax.all_to_all(target_rows, "span", split_axis=1, concat_axis=1, tiled=True),
    )
    incoming_rows = received_rows[0]
    folded = fold_rows(received, incoming_rows % row_count)
    collected = place_blocks(folded, incoming_rows[:, 0] // row_count, parent_span)
    own_sums = seam(collected, PB_DEV)
    level_one = match_moments(own_sums)
    cap_two = max(1, (PB_DEV + spans - 1) // spans)
    slot_two = parent_owner * cap_two + earlier_same(parent_owner)
    outgoing_two = (
        jnp.zeros((components, spans * cap_two, row_count), jnp.float32)
        .at[:, slot_two]
        .set(own_sums)
    )
    targets_two = parent_slot[:, None] * row_count + parent_row
    rows_two = (
        jnp.zeros((1, spans * cap_two, row_count), jnp.int32).at[0, slot_two].set(targets_two)
    )
    received_two, received_rows_two = (
        lax.all_to_all(outgoing_two, "span", split_axis=1, concat_axis=1, tiled=True),
        lax.all_to_all(rows_two, "span", split_axis=1, concat_axis=1, tiled=True),
    )
    grand_span = GB_DEV * sub_count
    incoming_two = received_rows_two[0]
    folded_two = fold_rows(received_two, incoming_two % row_count)
    collected_two = place_blocks(folded_two, incoming_two[:, 0] // row_count, grand_span)
    level_two = match_moments(seam(collected_two, GB_DEV))
    return (level_one, level_two)


def solution(mesh):
    placed = (
        P(("groups", "span", "sub"), None),
        P(None, ("groups", "span", "sub"), None),
        P(None, ("groups", "span", "sub"), None),
        P(None, ("groups", "span", "sub"), None),
        P(("groups", "span", "sub")),
        P(("groups", "span", "sub")),
        P(("groups", "span", "sub"), None),
        P(("groups", "span", "sub")),
        P(("groups", "span", "sub")),
        P(("groups", "span", "sub")),
        P(("groups", "span", "sub"), None),
    )
    return jax.shard_map(
        body,
        mesh=mesh,
        in_specs=placed,
        out_specs=(
            P(None, ("groups", "span", "sub"), None),
            P(None, ("groups", "span", "sub"), None),
        ),
        check_vma=False,
    )
```

profile of v0, /device:TPU:0, one launch (start us, length us, event | category | flops | bytes accessed | tf_op | source)
XLA Modules:
  0.0 397.7 jit_solution(10594547297773773612)
XLA Ops:
  9.5 1.9 scatter_custom_fusion
  11.4 7.3 %all-to-all-start = ((s32[1,256,128]{2,0,1:T(1,128)}), s32[1,256,128]{2,0,1:T(1,128)S(1)}, u32[]{:S(2)}, u32[]{:S(2)}) async-start(s32[1,256,128]{2,0,1:T(1,128)} %bitcast.1), calls=%async_computation | async-start | bytes 262144 | tf_op jit(solution)/shard_map/all_to_all | solution.py:124
  28.5 1.2 convert_multiply_fusion
  30.3 4.2 %copy.25 = f32[128,58,128]{2,1,0:T(8,128)} copy(f32[128,58,128]{2,0,1:T(8,128)S(1)} %maximum_bitcast_fusion) | data formatting | bytes 7602176 | tf_op jit(solution)/shard_map/concatenate | solution.py:31
  34.4 4.3 %broadcast.77 = f32[58,256,128]{2,0,1:T(8,128)} broadcast(f32[]{:T(128)} %constant.128.clone.1), dimensions={} | broadcast | bytes 7602180 | tf_op jit(solution)/shard_map/broadcast.15
  38.7 19.5 %scatter_fusion = f32[58,256,128]{2,0,1:T(8,128)} fusion(f32[58,256,128]{2,0,1:T(8,128)} %broadcast.77, s32[128]{0:T(128)S(1)} %get-tuple-element.232, f32[128,58,128]{2,1,0:T(8,128)} %copy.25), kind=kCustom, calls=%fused_computation.1 | custom fusion | bytes 11403776 | tf_op jit(solution)/shard_map/scatter | solution.py:117
  58.2 6.3 %all-to-all-start.1 = ((f32[58,256,128]{2,0,1:T(8,128)}), f32[58,256,128]{2,0,1:T(8,128)}, u32[]{:S(2)}, u32[]{:S(2)}) async-start(f32[58,256,128]{2,0,1:T(8,128)} %scatter_fusion), calls=%async_computation.1 | async-start | bytes 16777216 | tf_op jit(solution)/shard_map/all_to_all | solution.py:123
  64.8 182.0 %all-to-all-done.1 = f32[58,256,128]{2,0,1:T(8,128)} async-done(((f32[58,256,128]{2,0,1:T(8,128)}), f32[58,256,128]{2,0,1:T(8,128)}, u32[]{:S(2)}, u32[]{:S(2)}) %all-to-all-start.1) | async-done | bytes 7602208 | tf_op jit(solution)/shard_map/all_to_all | solution.py:123
  246.7 4.0 %broadcast.77.clone = f32[58,256,128]{2,1,0:T(8,128)} broadcast(f32[]{:T(128)} %constant.128.clone.1), dimensions={} | broadcast | bytes 7602180 | tf_op jit(solution)/shard_map/broadcast.15
  250.7 47.2 %while.28 = (s32[]{:T(128)}, f32[58,256,128]{2,1,0:T(8,128)}, s32[256,128]{1,0:T(8,128)S(1)}, f32[58,256,128]{2,0,1:T(8,128)}, s32[]{:T(128)}, /*index=5*/s32[]{:T(128)}, s32[]{:T(128)}, s32[]{:T(128)}) while((s32[]{:T(128)}, f32[58,256,128]{2,1,0:T(8,128)}, s32[256,128]{1,0:T(8,128)S(1)}, f32[58,256,128]{2,0,1:T(8,128)}, ...), condition=%wide.region_4.5_spmd.clone, body=%wide.region_3.4_spmd.clone.sunk | while | flops 182714368 | bytes 1974415 | solution.py:74
  250.7 1.8 convolution_bitcast_fusion.6
  252.6 1.2 copy_dynamic-update-slice_fusion.4
  253.7 1.8 convolution_bitcast_fusion.6
  255.6 1.2 copy_dynamic-update-slice_fusion.4
  256.7 1.8 convolution_bitcast_fusion.6
  258.5 1.1 copy_dynamic-update-slice_fusion.4
  259.7 1.8 convolution_bitcast_fusion.6
  262.6 1.8 convolution_bitcast_fusion.6
  264.4 1.1 copy_dynamic-update-slice_fusion.4
  265.6 1.8 convolution_bitcast_fusion.6
  267.4 1.1 copy_dynamic-update-slice_fusion.4
  268.5 1.8 convolution_bitcast_fusion.6
  271.5 1.8 convolution_bitcast_fusion.6
  273.3 1.1 copy_dynamic-update-slice_fusion.4
  274.4 1.8 convolution_bitcast_fusion.6
  276.2 1.1 copy_dynamic-update-slice_fusion.4
  277.4 1.8 convolution_bitcast_fusion.6
  280.3 1.8 convolution_bitcast_fusion.6
  283.2 1.8 convolution_bitcast_fusion.6
  286.1 1.8 convolution_bitcast_fusion.6
  289.1 1.8 convolution_bitcast_fusion.6
  292.0 1.8 convolution_bitcast_fusion.6
  293.8 1.1 copy_dynamic-update-slice_fusion.4
  294.9 1.8 convolution_bitcast_fusion.6
  296.8 1.1 copy_dynamic-update-slice_fusion.4
  297.9 7.4 %convolution_bitcast_fusion.2 = f32[58,64,128]{2,1,0:T(8,128)} fusion(f32[58,256,128]{2,1,0:T(8,128)} %get-tuple-element.190, s32[256]{0:T(256)S(1)} %fusion.11), kind=kOutput, calls=%fused_computation.22 | convolution fusion | flops 1459634176 | bytes 9503744 | tf_op jit(solution)/shard_map/csj,sp->cpj/dot_general | solution.py:83
  305.6 1.3 scatter_custom_fusion.2
  306.9 3.6 all-to-all-start.2
  310.5 6.6 %all-to-all-done.2 = s32[1,32,128]{2,0,1:T(1,128)S(1)} async-done(((s32[1,32,128]{2,0,1:T(1,128)}), s32[1,32,128]{2,0,1:T(1,128)S(1)}, u32[]{:S(2)}, u32[]{:S(2)}) %all-to-all-start.2) | async-done | bytes 16416 | tf_op jit(solution)/shard_map/all_to_all | solution.py:144
  317.2 8.3 %all-reduce.5.cloned.1.call-done = f32[58,64,128]{2,1,0:T(8,128)} async-done(((f32[58,64,128]{2,1,0:T(8,128)}), f32[58,64,128]{2,1,0:T(8,128)}) %all-reduce.5.cloned.1.call-update) | async-done | bytes 1900560 | tf_op jit(solution)/shard_map/psum | solution.py:87
  325.6 1.3 dynamic-slice_bitcast_fusion
  328.5 4.6 %scatter_fusion.1 = f32[58,32,128]{2,0,1:T(8,128)} fusion(f32[58,32,128]{2,0,1:T(8,128)} %broadcast.82, s32[32]{0:T(128)S(1)} %compare_select_fusion, f32[32,58,128]{2,1,0:T(8,128)S(1)} %copy.27), kind=kCustom, calls=%fused_computation.3 | custom fusion | bytes 2850944 | tf_op jit(solution)/shard_map/scatter | solution.py:136
  333.1 5.8 %all-to-all-start.3 = ((f32[58,32,128]{2,0,1:T(8,128)}), f32[58,32,128]{2,0,1:T(8,128)S(1)}, u32[]{:S(2)}, u32[]{:S(2)}) async-start(f32[58,32,128]{2,0,1:T(8,128)} %scatter_fusion.1), calls=%async_computation.3 | async-start | bytes 2097152 | tf_op jit(solution)/shard_map/all_to_all | solution.py:143
  340.5 24.6 %all-to-all-done.3 = f32[58,32,128]{2,0,1:T(8,128)S(1)} async-done(((f32[58,32,128]{2,0,1:T(8,128)}), f32[58,32,128]{2,0,1:T(8,128)S(1)}, u32[]{:S(2)}, u32[]{:S(2)}) %all-to-all-start.3) | async-done | bytes 950304 | tf_op jit(solution)/shard_map/all_to_all | solution.py:143
  365.2 2.8 while.29
  368.0 1.2 convolution_bitcast_fusion.3
  370.2 1.2 dynamic-slice_divide_fusion
  372.4 14.6 %all-reduce.7.cloned.1.call-done = f32[58,16,128]{2,1,0:T(8,128)} async-done(((f32[58,16,128]{2,1,0:T(8,128)}), f32[58,16,128]{2,1,0:T(8,128)}) %all-reduce.7.cloned.1.call-update) | async-done | bytes 475152 | tf_op jit(solution)/shard_map/psum | solution.py:87
  (93 shorter events, 32.0 us)
Async XLA Ops:
  7.2 22.6 %copy-start.2 = (f32[128,128]{1,0:T(8,128)S(1)}, f32[128,128]{1,0:T(8,128)}, u32[]{:S(2)}) copy-start(f32[128,128]{1,0:T(8,128)} %param.15) | copy-start | bytes 196612
  7.2 21.3 %copy-start.1 = (bf16[48,128,128]{2,1,0:T(8,128)(2,1)S(1)}, bf16[48,128,128]{2,1,0:T(8,128)(2,1)}, u32[]{:S(2)}) copy-start(bf16[48,128,128]{2,1,0:T(8,128)(2,1)} %param.18) | copy-start | bytes 4718596
  11.4 46.8 %all-to-all-start = ((s32[1,256,128]{2,0,1:T(1,128)}), s32[1,256,128]{2,0,1:T(1,128)S(1)}, u32[]{:S(2)}, u32[]{:S(2)}) async-start(s32[1,256,128]{2,0,1:T(1,128)} %bitcast.1), calls=%async_computation | async-start | bytes 262144 | tf_op jit(solution)/shard_map/all_to_all | solution.py:124
  22.2 7.6 %copy-start = (f32[3,128,128]{2,1,0:T(8,128)S(1)}, f32[3,128,128]{2,1,0:T(8,128)}, u32[]{:S(2)}) copy-start(f32[3,128,128]{2,1,0:T(8,128)} %param.16) | copy-start | bytes 589828
  58.2 188.6 %all-to-all-start.1 = ((f32[58,256,128]{2,0,1:T(8,128)}), f32[58,256,128]{2,0,1:T(8,128)}, u32[]{:S(2)}, u32[]{:S(2)}) async-start(f32[58,256,128]{2,0,1:T(8,128)} %scatter_fusion), calls=%async_computation.1 | async-start | bytes 16777216 | tf_op jit(solution)/shard_map/all_to_all | solution.py:123
  64.5 261.1 %all-reduce.5.cloned.1.call-start = ((), (), s32[]{:S(2)}) async-start(), calls=%async_computation.4 | async-start | bytes 3801088 | tf_op jit(solution)/shard_map/psum | solution.py:87
  297.9 7.5 %copy-start.5 = (s32[32]{0:T(128)S(1)}, s32[32]{0:T(128)}, u32[]{:S(2)}) copy-start(s32[32]{0:T(128)} %param.23) | copy-start | bytes 388
  297.9 7.6 %copy-start.4 = (s32[32]{0:T(128)S(1)}, s32[32]{0:T(128)}, u32[]{:S(2)}) copy-start(s32[32]{0:T(128)} %param.24) | copy-start | bytes 388
  297.9 7.7 %copy-start.3 = (s32[32,128]{1,0:T(8,128)S(1)}, s32[32,128]{1,0:T(8,128)}, u32[]{:S(2)}) copy-start(s32[32,128]{1,0:T(8,128)} %param.25) | copy-start | bytes 49156
  306.9 10.2 %all-to-all-start.2 = ((s32[1,32,128]{2,0,1:T(1,128)}), s32[1,32,128]{2,0,1:T(1,128)S(1)}, u32[]{:S(2)}, u32[]{:S(2)}) async-start(s32[1,32,128]{2,0,1:T(1,128)} %bitcast.8), calls=%async_computation.2 | async-start | bytes 32768 | tf_op jit(solution)/shard_map/all_to_all | solution.py:144
  333.1 32.0 %all-to-all-start.3 = ((f32[58,32,128]{2,0,1:T(8,128)}), f32[58,32,128]{2,0,1:T(8,128)S(1)}, u32[]{:S(2)}, u32[]{:S(2)}) async-start(f32[58,32,128]{2,0,1:T(8,128)} %scatter_fusion.1), calls=%async_computation.3 | async-start | bytes 2097152 | tf_op jit(solution)/shard_map/all_to_all | solution.py:143
  338.9 48.2 %all-reduce.7.cloned.1.call-start = ((), (), s32[]{:S(2)}) async-start(), calls=%async_computation.5 | async-start | bytes 950272 | tf_op jit(solution)/shard_map/psum | solution.py:87
Sparse Core Ops, SparseCore 0:
  305.5 20.0 all-reduce.4
  369.4 17.6 all-reduce.6
where the time goes:
time: 400 us; the launch traced here: 398 us
  waiting for transfers between devices  236 us (59%)
  local copies, waits for them, and re-layouts  58 us (14%)
  matrix products  39.8 us (10%)
  other arithmetic  25.3 us (6%)
  starting transfers between devices  23 us (6%)
  between operations  15.1 us (4%)
    all_to_all x1, waiting for transfers between devices, body(): lax.all_to_all(outgoing, 'span', split_axis=1, concat_axis=1, tiled=True)  182 us
    dot_general x18, matrix products, fold_step(): jnp.einsum('cbr,brj->cbj', block_part, row_table, precision=lax.Precision...  31.2 us
    all_to_all x1, waiting for transfers between devices, body(): lax.all_to_all(outgoing_two, 'span', split_axis=1, concat_axis=1, tiled=T...  24.6 us
    psum x2, waiting for transfers between devices, seam(): whole_sum = lax.psum(partial_value, 'sub')  23 us
    scatter x1, local copies, waits for them, and re-layouts, body(): jnp.zeros(outgoing_shape, jnp.float32).at[:, slot_index]  19.5 us
    dynamic_update_slice x18, local copies, waits for them, and re-layouts, fold_step(): return lax.dynamic_update_slice_in_dim(result, folded_part, start, 1)  18.4 us
    another operation x4, local copies, waits for them, and re-layouts  9.49 us
    unnamed x20, other arithmetic  8.87 us
  transfers between devices with their start and end apart: 6, of which 5 were waited for; matrix products, arithmetic and copies ran while one was open for 12% of the time, Pallas kernels for 0%

commit v1 on v0

--- a/solution.py
+++ b/solution.py
@@ -3,6 +3,8 @@
 import jax
 import jax.numpy as jnp
 from jax import lax
+from jax.experimental import pallas as pl
+from jax.experimental.pallas import tpu as pltpu
 from jax.sharding import PartitionSpec as P
 
 PB_DEV = 32
@@ -88,7 +90,7 @@
     return lax.dynamic_slice_in_dim(whole_sum, lax.axis_index("sub") * per_device, per_device, 1)
 
 
-def body(
+def plain_body(
     child_weight,
     child_mean,
     child_factor,
@@ -151,6 +153,409 @@
     return (level_one, level_two)
 
 
+TILE = 8
+UNROLL = 8
+
+
+def tile_count(width, slots):
+    return (width // TILE) * slots + (slots * (width % TILE) + TILE - 1) // TILE
+
+
+def split_pair(values):
+    high = values.astype(jnp.bfloat16)
+    low = (values - high.astype(jnp.float32)).astype(jnp.bfloat16)
+    return jnp.concatenate([high, low], 1)
+
+
+def row_table(rows):
+    width = rows.shape[1]
+    labels = lax.broadcasted_iota(jnp.int32, (width, width), 0)
+    picks = jnp.where(labels == rows, 1.0, 0.0).astype(jnp.bfloat16)
+    return jnp.concatenate([picks, picks], 1)
+
+
+def fold_block(values, rows):
+    return lax.dot_general(
+        split_pair(values),
+        row_table(rows),
+        (((1,), (1,)), ((), ())),
+        preferred_element_type=jnp.float32,
+    )
+
+
+def group_mask(extra, group):
+    return lax.broadcasted_iota(jnp.int32, (TILE, 1), 0) // extra == group
+
+
+def child_kernel(first, width, regions, slots, *refs):
+    geometry = first == 0
+    (pos_ref, live_ref, rows_ref, weight_ref, mean_ref, factor_ref, colour_ref) = refs[:7]
+    keep_ref, send_ref = refs[7:9]
+    moments, totals, colours, load_sem, keep_sem, send_sem = refs[9:]
+    block_count, row_count = rows_ref.shape
+    full, extra = width // TILE, width % TILE
+    per_region = tile_count(width, slots)
+    group = 16
+    first_colour = max(first, 10) - 10
+    colour_total = colours.shape[0]
+    load = None
+    if first + width > 10:
+        load = pltpu.make_async_copy(
+            colour_ref.at[pl.ds(first_colour, colour_total)], colours, load_sem
+        )
+        load.start()
+
+    def clear(step, carry):
+        totals[pl.ds(step * 16, 16)] = jnp.zeros((16, TILE, row_count), jnp.float32)
+        return carry
+
+    lax.fori_loop(0, totals.shape[0] // 16, clear, 0)
+    if load is not None:
+        load.wait()
+
+    def prepare(step, carry):
+        start = pl.multiple_of(step * group, group)
+        part = pl.ds(start, group)
+        weight = weight_ref[part, :]
+        values = {}
+        if geometry:
+            centre = [mean_ref[axis, part, :] for axis in range(3)]
+            factor = [factor_ref[entry, part, :] for entry in range(6)]
+            spread = [
+                factor[0] * factor[0],
+                factor[0] * factor[1],
+                factor[0] * factor[3],
+                factor[1] * factor[1] + factor[2] * factor[2],
+                factor[1] * factor[3] + factor[2] * factor[4],
+                factor[3] * factor[3] + factor[4] * factor[4] + factor[5] * factor[5],
+            ]
+            values[0] = weight
+            for axis in range(3):
+                values[1 + axis] = weight * centre[axis]
+            for entry, (left, right) in enumerate(PAIRS):
+                values[4 + entry] = weight * (spread[entry] + centre[left] * centre[right])
+        for entry in range(colour_total):
+            values[10 + first_colour + entry] = weight * colours[entry, part, :].astype(jnp.float32)
+        for place in range(full * TILE + (TILE if extra else 0)):
+            component = first + (place if place < full * TILE else full * TILE + place % extra)
+            moments[pl.ds(place * block_count + start, group), :] = values[component]
+        return carry
+
+    lax.fori_loop(0, block_count // group, prepare, 0)
+    live = live_ref[0]
+
+    def fold(step, carry):
+        folded = []
+        for turn in range(UNROLL):
+            block = step * UNROLL + turn
+            place = pos_ref[block]
+            region, slot = place // slots, place % slots
+            lines = [
+                moments[pl.ds(tile * TILE * block_count + block, TILE, stride=block_count), :]
+                for tile in range(full)
+            ]
+            if extra:
+                line = moments[pl.ds(full * TILE * block_count + block, TILE, stride=block_count), :]
+                lines.append(jnp.where(group_mask(extra, slot % (TILE // extra)), line, 0.0))
+            rows = jnp.where(block < live, rows_ref[pl.ds(block, 1), :], -1)
+            folded.append((region * per_region, slot, fold_block(jnp.concatenate(lines, 0), rows)))
+        for base, slot, result in folded:
+            for tile in range(full):
+                totals[base + tile * slots + slot] += result[tile * TILE : (tile + 1) * TILE]
+            if extra:
+                totals[base + full * slots + slot // (TILE // extra)] += result[full * TILE :]
+        return carry
+
+    lax.fori_loop(0, (live + UNROLL - 1) // UNROLL, fold, 0)
+    half = regions * per_region
+    keep = pltpu.make_async_copy(totals.at[pl.ds(0, half)], keep_ref, keep_sem)
+    send = pltpu.make_async_copy(totals.at[pl.ds(half, half)], send_ref, send_sem)
+    send.start()
+    keep.start()
+    send.wait()
+    keep.wait()
+
+
+def fold_children(place, live, rows, weight, mean, factor, colour, first, width, regions, slots):
+    block_count, row_count = rows.shape
+    per_region = tile_count(width, slots)
+    colour_total = max(first + width - max(first, 10), 0)
+    padded = width // TILE * TILE + (TILE if width % TILE else 0)
+    half = jax.ShapeDtypeStruct((regions * per_region, TILE, row_count), jnp.float32)
+    whole = pl.BlockSpec(memory_space=pltpu.VMEM)
+    scalars = pl.BlockSpec(memory_space=pltpu.SMEM)
+    outside = pl.BlockSpec(memory_space=pl.ANY)
+
+    def kernel(*refs):
+        child_kernel(first, width, regions, slots, *refs)
+
+    return pl.pallas_call(
+        kernel,
+        out_shape=(half, half),
+        in_specs=[scalars, scalars, whole, whole, whole if first == 0 else outside]
+        + [whole if first == 0 else outside, outside],
+        out_specs=(outside, outside),
+        scratch_shapes=[
+            pltpu.VMEM((padded * block_count, row_count), jnp.float32),
+            pltpu.VMEM((2 * regions * per_region, TILE, row_count), jnp.float32),
+            pltpu.VMEM((max(colour_total, 1), block_count, row_count), jnp.bfloat16),
+            pltpu.SemaphoreType.DMA,
+            pltpu.SemaphoreType.DMA,
+            pltpu.SemaphoreType.DMA,
+        ],
+        compiler_params=pltpu.CompilerParams(vmem_limit_bytes=48 * 1024 * 1024),
+        cost_estimate=pl.CostEstimate(
+            flops=4 * block_count * padded * row_count * row_count,
+            bytes_accessed=16 * regions * per_region * TILE * row_count,
+            transcendentals=0,
+        ),
+        name="fold_children",
+    )(place, live, rows, weight, mean, factor, colour)
+
+
+def parent_kernel(width, regions, cap, *refs):
+    place_ref, rows_ref, sums_ref = refs[:3]
+    out_refs, totals = refs[3:-1], refs[-1]
+    block_count = rows_ref.shape[0]
+    full, extra = width // TILE, width % TILE
+    per_region = tile_count(width, cap)
+    totals[...] = jnp.zeros(totals.shape, jnp.float32)
+    for start in range(0, block_count, UNROLL):
+        folded = []
+        for block in range(start, start + UNROLL):
+            place = place_ref[block]
+            region, rank = place // cap, place % cap
+            lines = [sums_ref[tile * block_count + block] for tile in range(full)]
+            if extra:
+                share = TILE // extra
+                line = sums_ref[full * block_count + block // share]
+                line = jnp.where(group_mask(extra, block % share), line, 0.0)
+                line = sum(
+                    (pltpu.roll(line, turn * extra, 0) for turn in range(1, share)), start=line
+                )
+                lines.append(jnp.where(group_mask(extra, rank % share), line, 0.0))
+            rows = rows_ref[pl.ds(block, 1), :]
+            folded.append((region * per_region, rank, fold_block(jnp.concatenate(lines, 0), rows)))
+        for base, rank, result in folded:
+            for tile in range(full):
+                totals[base + tile * cap + rank] += result[tile * TILE : (tile + 1) * TILE]
+            if extra:
+                totals[base + full * cap + rank // (TILE // extra)] += result[full * TILE :]
+    for region, out_ref in enumerate(out_refs):
+        out_ref[...] = totals[region * per_region : (region + 1) * per_region]
+
+
+def fold_parents(place, rows, sums, width, regions, cap):
+    row_count = rows.shape[1]
+    per_region = tile_count(width, cap)
+    whole = pl.BlockSpec(memory_space=pltpu.VMEM)
+
+    def kernel(*refs):
+        parent_kernel(width, regions, cap, *refs)
+
+    return pl.pallas_call(
+        kernel,
+        out_shape=[jax.ShapeDtypeStruct((per_region, TILE, row_count), jnp.float32)] * regions,
+        in_specs=[pl.BlockSpec(memory_space=pltpu.SMEM), whole, whole],
+        out_specs=[whole] * regions,
+        scratch_shapes=[pltpu.VMEM((regions * per_region, TILE, row_count), jnp.float32)],
+        compiler_params=pltpu.CompilerParams(vmem_limit_bytes=24 * 1024 * 1024),
+        cost_estimate=pl.CostEstimate(
+            flops=4 * rows.shape[0] * width * row_count * row_count,
+            bytes_accessed=8 * regions * per_region * TILE * row_count,
+            transcendentals=0,
+        ),
+        name="fold_parents",
+    )(place, rows, sums)
+
+
+def place_kernel(width, regions, cap, slots, *refs):
+    code_ref, in_refs = refs[0], refs[1 : 1 + regions]
+    keep_ref, send_ref, totals = refs[1 + regions :]
+    full, extra = width // TILE, width % TILE
+    per_half = tile_count(width, slots)
+    totals[...] = jnp.zeros(totals.shape, jnp.float32)
+    for region, in_ref in enumerate(in_refs):
+        for rank in range(cap):
+            code = code_ref[region * cap + rank]
+            half, slot = code // slots, code % slots
+            for tile in range(full):
+                totals[half * per_half + tile * slots + slot] += in_ref[tile * cap + rank]
+            if extra:
+                share = TILE // extra
+                line = in_ref[full * cap + rank // share]
+                line = jnp.where(group_mask(extra, rank % share), line, 0.0)
+                line = sum(
+                    (pltpu.roll(line, turn * extra, 0) for turn in range(1, share)), start=line
+                )
+                line = jnp.where(group_mask(extra, slot % share), line, 0.0)
+                totals[half * per_half + full * slots + slot // share] += line
+    keep_ref[...] = totals[:per_half]
+    send_ref[...] = totals[per_half:]
+
+
+def place_parents(codes, parts, width, cap, slots):
+    row_count = parts[0].shape[2]
+    per_half = tile_count(width, slots)
+    whole = pl.BlockSpec(memory_space=pltpu.VMEM)
+    half = jax.ShapeDtypeStruct((per_half, TILE, row_count), jnp.float32)
+
+    def kernel(*refs):
+        place_kernel(width, len(parts), cap, slots, *refs)
+
+    return pl.pallas_call(
+        kernel,
+        out_shape=(half, half),
+        in_specs=[pl.BlockSpec(memory_space=pltpu.SMEM)] + [whole] * len(parts),
+        out_specs=(whole, whole),
+        scratch_shapes=[pltpu.VMEM((2 * per_half, TILE, row_count), jnp.float32)],
+        compiler_params=pltpu.CompilerParams(vmem_limit_bytes=24 * 1024 * 1024),
+        cost_estimate=pl.CostEstimate(
+            flops=per_half * TILE * row_count,
+            bytes_accessed=16 * per_half * TILE * row_count,
+            transcendentals=0,
+        ),
+        name="place_parents",
+    )(codes, *parts)
+
+
+def unpack(tiles, width, slots):
+    full, extra = width // TILE, width % TILE
+    row_count = tiles.shape[2]
+    whole = tiles[: full * slots].reshape(full, slots, TILE, row_count)
+    whole = whole.transpose(0, 2, 1, 3).reshape(full * TILE, slots, row_count)
+    if not extra:
+        return whole
+    rest = tiles[full * slots :].reshape(slots, extra, row_count).transpose(1, 0, 2)
+    return jnp.concatenate([whole, rest], 0)
+
+
+def merged_parts(parts):
+    sums = parts[0]
+    divisor = jnp.maximum(sums[0], WEIGHT_FLOOR)
+    centre = sums[1:4] / divisor
+    centre_outer = jnp.stack([centre[first] * centre[second] for first, second in PAIRS])
+    spread = sums[4:10] / divisor - centre_outer
+    rest = [part / divisor for part in [sums[10:]] + parts[1:] if part.shape[0]]
+    return jnp.concatenate([sums[:1], centre, spread] + rest, 0)
+
+
+def cut_components(components):
+    chunks = [(0, 10, True)]
+    start = 10
+    while start < components:
+        width = min(16, components - start)
+        chunks.append((start, width, True))
+        start += width
+    return chunks
+
+
+def span_body(
+    child_weight,
+    child_mean,
+    child_factor,
+    child_colour,
+    child_dest,
+    child_slot,
+    child_row,
+    live_blocks,
+    parent_owner,
+    parent_slot,
+    parent_row,
+):
+    spans = lax.axis_size("span")
+    columns = 2
+    lines = spans // columns
+    components = 10 + child_colour.shape[0]
+    span_at, sub_at = lax.axis_index("span"), lax.axis_index("sub")
+    cap_two = max(1, (PB_DEV + spans - 1) // spans)
+
+    def region_of(owner):
+        column = (owner % columns - span_at % columns) % columns
+        line = (owner // columns - span_at // columns) % lines
+        return column * lines + line
+
+    def code_of(slot, per_device):
+        return (slot // per_device - sub_at) % 2 * per_device + slot % per_device
+
+    def shift(values, column, line):
+        pairs = [
+            (at, (at // columns + line) % lines * columns + (at + column) % columns)
+            for at in range(spans)
+        ]
+        return lax.ppermute(values, "span", pairs)
+
+    def swap(values):
+        return lax.ppermute(values, "sub", [(0, 1), (1, 0)])
+
+    code_one = code_of(child_slot, PB_DEV)
+    place_one = (code_one // PB_DEV * spans + region_of(child_dest)) * PB_DEV + code_one % PB_DEV
+    place_two = region_of(parent_owner) * cap_two + earlier_same(parent_owner)
+    taken = place_two[None, :] == jnp.arange(spans * cap_two, dtype=jnp.int32)[:, None]
+    codes = jnp.sum(jnp.where(taken, code_of(parent_slot, GB_DEV)[None, :], 0), 1)
+    codes = codes.reshape(spans, cap_two)
+    codes = jnp.concatenate(
+        [codes[:1]]
+        + [
+            shift(codes[region : region + 1], region // lines, region % lines)
+            for region in range(1, spans)
+        ],
+        0,
+    ).reshape(-1)
+
+    level_one, level_two = [], []
+    for first, width, column_first in cut_components(components):
+        keep, send = fold_children(
+            place_one,
+            live_blocks,
+            child_row,
+            child_weight,
+            child_mean,
+            child_factor,
+            child_colour,
+            first,
+            width,
+            spans,
+            PB_DEV,
+        )
+        size = tile_count(width, PB_DEV)
+        other = swap(send)
+        if column_first:
+            across = shift(keep[lines * size :] + other[lines * size :], 1, 0)
+
+            def term(line):
+                part = slice(line * size, (line + 1) * size)
+                return keep[part] + other[part] + across[part]
+
+            total = term(lines - 1)
+            for line in range(lines - 2, -1, -1):
+                total = shift(total, 0, 1) + term(line)
+        else:
+            both = (keep + other).reshape((columns, lines, size) + keep.shape[1:])
+            total = both[:, lines - 1]
+            for line in range(lines - 2, -1, -1):
+                total = shift(total, 0, 1) + both[:, line]
+            total = total[0] + shift(total[1], 1, 0)
+        level_one.append(unpack(total, width, PB_DEV))
+        parts = fold_parents(place_two, parent_row, total, width, spans, cap_two)
+        parts = [parts[0]] + [
+            shift(parts[region], region // lines, region % lines) for region in range(1, spans)
+        ]
+        keep_two, send_two = place_parents(codes, parts, width, cap_two, GB_DEV)
+        level_two.append(unpack(keep_two + swap(send_two), width, GB_DEV))
+    return (merged_parts(level_one), merged_parts(level_two))
+
+
+def body(*arrays):
+    spans, subs = lax.axis_size("span"), lax.axis_size("sub")
+    blocks = arrays[0].shape[0]
+    dense = spans * subs * PB_DEV
+    fits = subs == 2 and spans % 2 == 0 and dense <= 4 * blocks and PB_DEV % (4 * spans) == 0
+    if fits and blocks % 16 == 0:
+        return span_body(*arrays)
+    return plain_body(*arrays)
+
+
 def solution(mesh):
     placed = (
         P(("groups", "span", "sub"), None),

time: 400 us -> 254 us (0.64)
  waiting for transfers between devices: 236 us -> 116 us
  local copies, waits for them, and re-layouts: 58 us -> 12.8 us
  starting transfers between devices: 23 us -> 63.9 us
  matrix products: 39.8 us -> 0 us
  Pallas kernels: 0 us -> 31.2 us
  between operations: 15.1 us -> 1.98 us
    all_to_all x4 -> x0, waiting for transfers between devices: 213 us -> none  [the longest x1 182 us: body(): lax.all_to_all(outgoing, 'span', split_axis=1, concat_axis=1, tiled=True)]
    ppermute x0 -> x59, waiting for transfers between devices: none -> 116 us  [the longest x51 114 us: shift(): return lax.ppermute(values, 'span', pairs)]
    ppermute x0 -> x59, starting transfers between devices: none -> 63.9 us  [the longest x51 62 us: shift(): return lax.ppermute(values, 'span', pairs)]
    dot_general x20 -> x0, matrix products: 39.8 us -> none  [the longest x18 31.2 us: fold_step(): jnp.einsum('cbr,brj->cbj', block_part, row_table, precision=lax.Precision...]
    pallas_call x0 -> x12, Pallas kernels: none -> 31.2 us  [the longest x4 23.1 us: fold_children(): pl.pallas_call(kernel, out_shape=(half, half), in_specs=[scalars, scalars...]
    add x0 -> x27, other arithmetic: none -> 27 us  [the longest x12 13.4 us: span_body(): total = shift(total, 0, 1) + term(line)]
    scatter x2 -> x0, local copies, waits for them, and re-layouts: 24.1 us -> none  [the longest x1 19.5 us: body(): jnp.zeros(outgoing_shape, jnp.float32).at[:, slot_index]]
    all_to_all x4 -> x0, starting transfers between devices: 23 us -> none  [the longest x1 7.25 us: body(): lax.all_to_all(target_rows, 'span', split_axis=1, concat_axis=1, tiled=True)]
  transfers between devices with their start and end apart: 6 -> 59, of which waited for: 5 -> 20; matrix products, arithmetic and copies ran while one was open for 12% -> 12% of each run, Pallas kernels for 0% -> 10%
where the time goes in v1:
time: 254 us
  waiting for transfers between devices  116 us (46%)
  starting transfers between devices  63.9 us (25%)
  Pallas kernels  31.2 us (12%)
  other arithmetic  27.7 us (11%)
  local copies, waits for them, and re-layouts  12.8 us (5%)
    ppermute x51, waiting for transfers between devices, shift(): return lax.ppermute(values, 'span', pairs)  114 us
    ppermute x51, starting transfers between devices, shift(): return lax.ppermute(values, 'span', pairs)  62 us
    pallas_call x4, Pallas kernels, fold_children(): pl.pallas_call(kernel, out_shape=(half, half), in_specs=[scalars, scalars...  23.1 us
    add x12, other arithmetic, span_body(): total = shift(total, 0, 1) + term(line)  13.4 us
    unnamed x42, local copies, waits for them, and re-layouts  12.1 us
    add x4, other arithmetic, span_body(): across = shift(keep[lines * size:] + other[lines * size:], 1, 0)  8.56 us
  transfers between devices with their start and end apart: 59, of which 20 were waited for; matrix products, arithmetic and copies ran while one was open for 12% of the time, Pallas kernels for 10%

profile of v1, /device:TPU:0, one launch (start us, length us, event | category | flops | bytes accessed | tf_op | source)
XLA Modules:
  0.0 253.5 jit_solution(8981340723994470352)
XLA Ops:
  7.0 4.9 %fold_children.4 = (f32[320,8,128]{2,1,0:T(8,128)S(1)}, f32[320,8,128]{2,1,0:T(8,128)S(1)}) custom-call(s32[128]{0:T(128)S(1)} %fusion.21.refs_0_, s32[1]{0:T(128)S(6)} %copy.57.refs_1_, s32[128,128]{1,0:T(8,128)S(1)} %copy-done.6, f32[128,128]{1,0:T(8,128)S(1)} %copy-done.7, f32[3,128,128]{2,1,0:T(8,128)S(1)} %copy-done.2, f32[6,128,128]{2,1,0:T(8,128)S(1)} %copy-done.1, ...), custom_call_target="tpu_custom_call" | custom-call | flops 134217728 | bytes 5242880 | tf_op jit(solution)/shard_map/fold_children/pallas_call | solution.py:292
  12.4 6.1 %fold_children.5 = (f32[512,8,128]{2,1,0:T(8,128)S(1)}, f32[512,8,128]{2,1,0:T(8,128)}) custom-call(s32[128]{0:T(128)S(1)} %fusion.21.refs_0_, s32[1]{0:T(128)S(6)} %copy.57.refs_1_, s32[128,128]{1,0:T(8,128)S(1)} %copy-done.6, f32[128,128]{1,0:T(8,128)S(1)} %copy-done.7, f32[3,128,128]{2,1,0:T(8,128)S(1)} %copy-done.2, f32[6,128,128]{2,1,0:T(8,128)S(1)} %copy-done.1, ...), custom_call_target="tpu_custom_call" | custom-call | flops 134217728 | bytes 8388608 | tf_op jit(solution)/shard_map/fold_children/pallas_call | solution.py:292
  19.9 6.0 %fold_children.6 = (f32[512,8,128]{2,1,0:T(8,128)S(1)}, f32[512,8,128]{2,1,0:T(8,128)}) custom-call(s32[128]{0:T(128)S(1)} %fusion.21.refs_0_, s32[1]{0:T(128)S(6)} %copy.57.refs_1_, s32[128,128]{1,0:T(8,128)S(1)} %copy-done.6, f32[128,128]{1,0:T(8,128)S(1)} %copy-done.7, f32[3,128,128]{2,1,0:T(8,128)S(1)} %copy-done.2, f32[6,128,128]{2,1,0:T(8,128)S(1)} %copy-done.1, ...), custom_call_target="tpu_custom_call" | custom-call | flops 134217728 | bytes 8388608 | tf_op jit(solution)/shard_map/fold_children/pallas_call | solution.py:292
  27.7 6.0 %fold_children.7 = (f32[512,8,128]{2,1,0:T(8,128)S(1)}, f32[512,8,128]{2,1,0:T(8,128)}) custom-call(s32[128]{0:T(128)S(1)} %fusion.21.refs_0_, s32[1]{0:T(128)S(6)} %copy.57.refs_1_, s32[128,128]{1,0:T(8,128)S(1)} %copy-done.6, f32[128,128]{1,0:T(8,128)S(1)} %copy-done.7, f32[3,128,128]{2,1,0:T(8,128)S(1)} %copy-done.2, f32[6,128,128]{2,1,0:T(8,128)S(1)} %copy-done.1, ...), custom_call_target="tpu_custom_call" | custom-call | flops 134217728 | bytes 8388608 | tf_op jit(solution)/shard_map/fold_children/pallas_call | solution.py:292
  35.0 3.5 %collective-permute-start.1 = (f32[160,8,128]{2,1,0:T(8,128)}, f32[160,8,128]{2,1,0:T(8,128)}, u32[]{:S(2)}, u32[]{:S(2)}) collective-permute-start(f32[160,8,128]{2,1,0:T(8,128)} %slice_add_fusion.3), channel_id=1, source_target_pairs={{0,2},{2,0},{4,6},{6,4},{8,10},{10,8},{12,14},{14,12},{1,3},{3,1},... | collective-permute-start | bytes 1966088 | tf_op jit(solution)/shard_map/ppermute | solution.py:486
  38.9 2.2 collective-permute-start.20
  41.1 3.5 %collective-permute-done.20 = s32[1,4]{1,0:T(1,128)S(1)} collective-permute-done((s32[1,4]{1,0:T(1,128)S(1)}, s32[1,4]{1,0:T(1,128)S(1)}, u32[]{:S(2)}, u32[]{:S(2)}) %collective-permute-start.20) | collective-permute-done | bytes 48 | tf_op jit(solution)/shard_map/ppermute | solution.py:486
  45.6 3.4 %collective-permute-done.21 = s32[1,4]{1,0:T(1,128)S(1)} collective-permute-done((s32[1,4]{1,0:T(1,128)S(1)}, s32[1,4]{1,0:T(1,128)S(1)}, u32[]{:S(2)}, u32[]{:S(2)}) %collective-permute-start.21) | collective-permute-done | bytes 48 | tf_op jit(solution)/shard_map/ppermute | solution.py:486
  49.0 2.0 collective-permute-start.22
  51.1 1.5 collective-permute-done.22
  52.8 3.3 %collective-permute-done.23 = s32[1,4]{1,0:T(1,128)S(1)} collective-permute-done((s32[1,4]{1,0:T(1,128)S(1)}, s32[1,4]{1,0:T(1,128)S(1)}, u32[]{:S(2)}, u32[]{:S(2)}) %collective-permute-start.23) | collective-permute-done | bytes 48 | tf_op jit(solution)/shard_map/ppermute | solution.py:486
  57.5 4.8 %collective-permute-done.24 = s32[1,4]{1,0:T(1,128)S(1)} collective-permute-done((s32[1,4]{1,0:T(1,128)S(1)}, s32[1,4]{1,0:T(1,128)S(1)}, u32[]{:S(2)}, u32[]{:S(2)}) %collective-permute-start.24) | collective-permute-done | bytes 48 | tf_op jit(solution)/shard_map/ppermute | solution.py:486
  63.0 4.7 %collective-permute-done.25 = s32[1,4]{1,0:T(1,128)S(1)} collective-permute-done((s32[1,4]{1,0:T(1,128)S(1)}, s32[1,4]{1,0:T(1,128)S(1)}, u32[]{:S(2)}, u32[]{:S(2)}) %collective-permute-start.25) | collective-permute-done | bytes 48 | tf_op jit(solution)/shard_map/ppermute | solution.py:486
  67.7 1.7 collective-permute-start.26
  69.4 2.7 %collective-permute-done.26 = s32[1,4]{1,0:T(1,128)S(1)} collective-permute-done((s32[1,4]{1,0:T(1,128)S(1)}, s32[1,4]{1,0:T(1,128)S(1)}, u32[]{:S(2)}, u32[]{:S(2)}) %collective-permute-start.26) | collective-permute-done | bytes 48 | tf_op jit(solution)/shard_map/ppermute | solution.py:486
  73.4 2.8 %slice_add_fusion.2 = f32[256,8,128]{2,1,0:T(8,128)} fusion(f32[512,8,128]{2,1,0:T(8,128)} %collective-permute-done.5, f32[512,8,128]{2,1,0:T(8,128)} %copy-done.5), kind=kLoop, calls=%fused_computation.2 | loop fusion | flops 262144 | bytes 3145728 | tf_op jit(solution)/shard_map/add | solution.py:524
  76.2 4.7 %collective-permute-done.2 = f32[40,8,128]{2,1,0:T(8,128)S(1)} collective-permute-done((f32[40,8,128]{2,1,0:T(8,128)S(1)}, f32[40,8,128]{2,1,0:T(8,128)S(1)}, u32[]{:S(2)}, u32[]{:S(2)}) %collective-permute-start.2) | collective-permute-done | bytes 163872 | tf_op jit(solution)/shard_map/ppermute | solution.py:486
  82.0 2.3 slice_add_fusion.1
  84.3 6.3 %collective-permute-done.3 = f32[40,8,128]{2,1,0:T(8,128)S(1)} collective-permute-done((f32[40,8,128]{2,1,0:T(8,128)S(1)}, f32[40,8,128]{2,1,0:T(8,128)S(1)}, u32[]{:S(2)}, u32[]{:S(2)}) %collective-permute-start.3) | collective-permute-done | bytes 163872 | tf_op jit(solution)/shard_map/ppermute | solution.py:486
  91.7 2.4 slice_add_fusion
  94.1 5.4 %collective-permute-done.4 = f32[40,8,128]{2,1,0:T(8,128)S(1)} collective-permute-done((f32[40,8,128]{2,1,0:T(8,128)S(1)}, f32[40,8,128]{2,1,0:T(8,128)S(1)}, u32[]{:S(2)}, u32[]{:S(2)}) %collective-permute-start.4) | collective-permute-done | bytes 163872 | tf_op jit(solution)/shard_map/ppermute | solution.py:486
  102.0 3.7 %collective-permute-start.29 = (f32[5,8,128]{2,1,0:T(8,128)S(1)}, f32[5,8,128]{2,1,0:T(8,128)S(1)}, u32[]{:S(2)}, u32[]{:S(2)}) collective-permute-start(f32[5,8,128]{2,1,0:T(8,128)S(1)} %get-tuple-element.61), channel_id=1, source_target_pairs={{0,12},{2,14},{4,0},{6,2},{8,4},{10,6},{12,8},{14,10},{1,13},{3,15... | collective-permute-start | bytes 61448 | tf_op jit(solution)/shard_map/ppermute | solution.py:486
  105.7 2.0 collective-permute-start.31
  108.7 1.5 collective-permute-start.32
  110.2 3.8 %collective-permute-start.33 = (f32[5,8,128]{2,1,0:T(8,128)S(1)}, f32[5,8,128]{2,1,0:T(8,128)S(1)}, u32[]{:S(2)}, u32[]{:S(2)}) collective-permute-start(f32[5,8,128]{2,1,0:T(8,128)S(1)} %get-tuple-element.65), channel_id=1, source_target_pairs={{0,14},{2,12},{4,2},{6,0},{8,6},{10,4},{12,10},{14,8},{1,15},{3,13... | collective-permute-start | bytes 61448 | tf_op jit(solution)/shard_map/ppermute | solution.py:486
  114.6 2.0 collective-permute-start.11
  120.9 20.1 %collective-permute-done.6 = f32[256,8,128]{2,1,0:T(8,128)} collective-permute-done((f32[256,8,128]{2,1,0:T(8,128)}, f32[256,8,128]{2,1,0:T(8,128)}, u32[]{:S(2)}, u32[]{:S(2)}) %collective-permute-start.6) | collective-permute-done | bytes 1048608 | tf_op jit(solution)/shard_map/ppermute | solution.py:486
  142.2 21.3 %collective-permute-done.11 = f32[256,8,128]{2,1,0:T(8,128)} collective-permute-done((f32[256,8,128]{2,1,0:T(8,128)}, f32[256,8,128]{2,1,0:T(8,128)}, u32[]{:S(2)}, u32[]{:S(2)}) %collective-permute-start.11) | collective-permute-done | bytes 1048608 | tf_op jit(solution)/shard_map/ppermute | solution.py:486
  164.7 10.2 %collective-permute-done.16 = f32[256,8,128]{2,1,0:T(8,128)S(1)} collective-permute-done((f32[256,8,128]{2,1,0:T(8,128)}, f32[256,8,128]{2,1,0:T(8,128)S(1)}, u32[]{:S(2)}, u32[]{:S(2)}) %collective-permute-start.16) | collective-permute-done | bytes 1048608 | tf_op jit(solution)/shard_map/ppermute | solution.py:486
  177.2 1.8 collective-permute-start.8
  180.3 6.8 %collective-permute-done.17 = f32[64,8,128]{2,1,0:T(8,128)S(1)} collective-permute-done((f32[64,8,128]{2,1,0:T(8,128)S(1)}, f32[64,8,128]{2,1,0:T(8,128)S(1)}, u32[]{:S(2)}, u32[]{:S(2)}) %collective-permute-start.17) | collective-permute-done | bytes 262176 | tf_op jit(solution)/shard_map/ppermute | solution.py:486
  188.1 4.5 %collective-permute-done.8 = f32[64,8,128]{2,1,0:T(8,128)S(1)} collective-permute-done((f32[64,8,128]{2,1,0:T(8,128)S(1)}, f32[64,8,128]{2,1,0:T(8,128)S(1)}, u32[]{:S(2)}, u32[]{:S(2)}) %collective-permute-start.8) | collective-permute-done | bytes 262176 | tf_op jit(solution)/shard_map/ppermute | solution.py:486
  193.9 4.4 %collective-permute-done.13 = f32[64,8,128]{2,1,0:T(8,128)S(1)} collective-permute-done((f32[64,8,128]{2,1,0:T(8,128)S(1)}, f32[64,8,128]{2,1,0:T(8,128)S(1)}, u32[]{:S(2)}, u32[]{:S(2)}) %collective-permute-start.13) | collective-permute-done | bytes 262176 | tf_op jit(solution)/shard_map/ppermute | solution.py:486
  199.6 4.4 %collective-permute-done.18 = f32[64,8,128]{2,1,0:T(8,128)S(1)} collective-permute-done((f32[64,8,128]{2,1,0:T(8,128)S(1)}, f32[64,8,128]{2,1,0:T(8,128)S(1)}, u32[]{:S(2)}, u32[]{:S(2)}) %collective-permute-start.18) | collective-permute-done | bytes 262176 | tf_op jit(solution)/shard_map/ppermute | solution.py:486
  205.1 2.1 collective-permute-done.9
  209.8 2.2 collective-permute-start.36
  212.0 1.6 collective-permute-start.37
  215.2 1.6 collective-permute-start.39
  216.8 1.5 collective-permute-start.40
  220.9 3.8 %collective-permute-start.41 = (f32[8,8,128]{2,1,0:T(8,128)S(1)}, f32[8,8,128]{2,1,0:T(8,128)S(1)}, u32[]{:S(2)}, u32[]{:S(2)}) collective-permute-start(f32[8,8,128]{2,1,0:T(8,128)S(1)} %get-tuple-element.75), channel_id=1, source_target_pairs={{0,14},{2,12},{4,2},{6,0},{8,6},{10,4},{12,10},{14,8},{1,15},{3,13... | collective-permute-start | bytes 98312 | tf_op jit(solution)/shard_map/ppermute | solution.py:486
  225.6 2.9 %collective-permute-start.45 = (f32[8,8,128]{2,1,0:T(8,128)S(1)}, f32[8,8,128]{2,1,0:T(8,128)S(1)}, u32[]{:S(2)}, u32[]{:S(2)}) collective-permute-start(f32[8,8,128]{2,1,0:T(8,128)S(1)} %get-tuple-element.81), channel_id=1, source_target_pairs={{0,12},{2,14},{4,0},{6,2},{8,4},{10,6},{12,8},{14,10},{1,13},{3,15... | collective-permute-start | bytes 98312 | tf_op jit(solution)/shard_map/ppermute | solution.py:486
  230.4 1.6 collective-permute-start.47
  232.0 1.5 collective-permute-start.48
  233.5 3.7 %collective-permute-start.49 = (f32[8,8,128]{2,1,0:T(8,128)S(1)}, f32[8,8,128]{2,1,0:T(8,128)S(1)}, u32[]{:S(2)}, u32[]{:S(2)}) collective-permute-start(f32[8,8,128]{2,1,0:T(8,128)S(1)} %get-tuple-element.85), channel_id=1, source_target_pairs={{0,14},{2,12},{4,2},{6,0},{8,6},{10,4},{12,10},{14,8},{1,15},{3,13... | collective-permute-start | bytes 98312 | tf_op jit(solution)/shard_map/ppermute | solution.py:486
  238.3 2.9 %collective-permute-start.53 = (f32[8,8,128]{2,1,0:T(8,128)S(1)}, f32[8,8,128]{2,1,0:T(8,128)S(1)}, u32[]{:S(2)}, u32[]{:S(2)}) collective-permute-start(f32[8,8,128]{2,1,0:T(8,128)S(1)} %get-tuple-element.91), channel_id=1, source_target_pairs={{0,12},{2,14},{4,0},{6,2},{8,4},{10,6},{12,8},{14,10},{1,13},{3,15... | collective-permute-start | bytes 98312 | tf_op jit(solution)/shard_map/ppermute | solution.py:486
  241.7 1.6 collective-permute-start.55
  243.3 1.4 collective-permute-start.56
  244.7 3.8 %collective-permute-start.57 = (f32[8,8,128]{2,1,0:T(8,128)S(1)}, f32[8,8,128]{2,1,0:T(8,128)S(1)}, u32[]{:S(2)}, u32[]{:S(2)}) collective-permute-start(f32[8,8,128]{2,1,0:T(8,128)S(1)} %get-tuple-element.95), channel_id=1, source_target_pairs={{0,14},{2,12},{4,2},{6,0},{8,6},{10,4},{12,10},{14,8},{1,15},{3,13... | collective-permute-start | bytes 98312 | tf_op jit(solution)/shard_map/ppermute | solution.py:486
  (180 shorter events, 52.3 us)
Async XLA Ops:
  11.9 22.1 %collective-permute-start = (f32[320,8,128]{2,1,0:T(8,128)S(1)}, f32[320,8,128]{2,1,0:T(8,128)S(1)}, u32[]{:S(2)}, u32[]{:S(2)}) collective-permute-start(f32[320,8,128]{2,1,0:T(8,128)S(1)} %get-tuple-element.51), channel_id=1, source_target_pairs={{0,1},{1,0},{2,3},{3,2},{4,5},{5,4},{6,7},{7,6},{8,9},{9,8},{10,11... | collective-permute-start | bytes 3932168 | tf_op jit(solution)/shard_map/ppermute | solution.py:489
  19.9 53.5 %collective-permute-start.5 = (f32[512,8,128]{2,1,0:T(8,128)}, f32[512,8,128]{2,1,0:T(8,128)}, u32[]{:S(2)}, u32[]{:S(2)}) collective-permute-start(f32[512,8,128]{2,1,0:T(8,128)} %get-tuple-element.53), channel_id=1, source_target_pairs={{0,1},{1,0},{2,3},{3,2},{4,5},{5,4},{6,7},{7,6},{8,9},{9,8},{10,11... | collective-permute-start | bytes 6291464 | tf_op jit(solution)/shard_map/ppermute | solution.py:489
  27.3 54.7 %collective-permute-start.10 = (f32[512,8,128]{2,1,0:T(8,128)}, f32[512,8,128]{2,1,0:T(8,128)}, u32[]{:S(2)}, u32[]{:S(2)}) collective-permute-start(f32[512,8,128]{2,1,0:T(8,128)} %get-tuple-element.55), channel_id=1, source_target_pairs={{0,1},{1,0},{2,3},{3,2},{4,5},{5,4},{6,7},{7,6},{8,9},{9,8},{10,11... | collective-permute-start | bytes 6291464 | tf_op jit(solution)/shard_map/ppermute | solution.py:489
  33.8 57.9 %collective-permute-start.15 = (f32[512,8,128]{2,1,0:T(8,128)}, f32[512,8,128]{2,1,0:T(8,128)}, u32[]{:S(2)}, u32[]{:S(2)}) collective-permute-start(f32[512,8,128]{2,1,0:T(8,128)} %get-tuple-element.57), channel_id=1, source_target_pairs={{0,1},{1,0},{2,3},{3,2},{4,5},{5,4},{6,7},{7,6},{8,9},{9,8},{10,11... | collective-permute-start | bytes 6291464 | tf_op jit(solution)/shard_map/ppermute | solution.py:489
  35.0 37.2 %collective-permute-start.1 = (f32[160,8,128]{2,1,0:T(8,128)}, f32[160,8,128]{2,1,0:T(8,128)}, u32[]{:S(2)}, u32[]{:S(2)}) collective-permute-start(f32[160,8,128]{2,1,0:T(8,128)} %slice_add_fusion.3), channel_id=1, source_target_pairs={{0,2},{2,0},{4,6},{6,4},{8,10},{10,8},{12,14},{14,12},{1,3},{3,1},... | collective-permute-start | bytes 1966088 | tf_op jit(solution)/shard_map/ppermute | solution.py:486
  56.1 6.2 %collective-permute-start.24 = (s32[1,4]{1,0:T(1,128)S(1)}, s32[1,4]{1,0:T(1,128)S(1)}, u32[]{:S(2)}, u32[]{:S(2)}) collective-permute-start(s32[1,4]{1,0:T(1,128)S(1)} %get-tuple-element.126), channel_id=1, source_target_pairs={{0,6},{2,4},{4,10},{6,8},{8,14},{10,12},{12,2},{14,0},{1,7},{3,5},... | collective-permute-start | bytes 56 | tf_op jit(solution)/shard_map/ppermute | solution.py:486
  73.3 7.6 %collective-permute-start.2 = (f32[40,8,128]{2,1,0:T(8,128)S(1)}, f32[40,8,128]{2,1,0:T(8,128)S(1)}, u32[]{:S(2)}, u32[]{:S(2)}) collective-permute-start(f32[40,8,128]{2,1,0:T(8,128)S(1)} %slice_add_fusion.34), channel_id=1, source_target_pairs={{0,4},{2,6},{4,8},{6,10},{8,12},{10,14},{12,0},{14,2},{1,5},{3,7},... | collective-permute-start | bytes 491528 | tf_op jit(solution)/shard_map/ppermute | solution.py:486
  81.9 8.7 %collective-permute-start.3 = (f32[40,8,128]{2,1,0:T(8,128)S(1)}, f32[40,8,128]{2,1,0:T(8,128)S(1)}, u32[]{:S(2)}, u32[]{:S(2)}) collective-permute-start(f32[40,8,128]{2,1,0:T(8,128)S(1)} %fusion.11), channel_id=1, source_target_pairs={{0,4},{2,6},{4,8},{6,10},{8,12},{10,14},{12,0},{14,2},{1,5},{3,7},... | collective-permute-start | bytes 491528 | tf_op jit(solution)/shard_map/ppermute | solution.py:486
  91.6 7.9 %collective-permute-start.4 = (f32[40,8,128]{2,1,0:T(8,128)S(1)}, f32[40,8,128]{2,1,0:T(8,128)S(1)}, u32[]{:S(2)}, u32[]{:S(2)}) collective-permute-start(f32[40,8,128]{2,1,0:T(8,128)S(1)} %fusion.10), channel_id=1, source_target_pairs={{0,4},{2,6},{4,8},{6,10},{8,12},{10,14},{12,0},{14,2},{1,5},{3,7},... | collective-permute-start | bytes 491528 | tf_op jit(solution)/shard_map/ppermute | solution.py:486
  101.8 6.9 %collective-permute-start.27 = (f32[5,8,128]{2,1,0:T(8,128)S(1)}, f32[5,8,128]{2,1,0:T(8,128)S(1)}, u32[]{:S(2)}, u32[]{:S(2)}) collective-permute-start(f32[5,8,128]{2,1,0:T(8,128)S(1)} %get-tuple-element.59), channel_id=1, source_target_pairs={{0,4},{2,6},{4,8},{6,10},{8,12},{10,14},{12,0},{14,2},{1,5},{3,7},... | collective-permute-start | bytes 61448 | tf_op jit(solution)/shard_map/ppermute | solution.py:486
  101.9 8.3 %collective-permute-start.28 = (f32[5,8,128]{2,1,0:T(8,128)S(1)}, f32[5,8,128]{2,1,0:T(8,128)S(1)}, u32[]{:S(2)}, u32[]{:S(2)}) collective-permute-start(f32[5,8,128]{2,1,0:T(8,128)S(1)} %get-tuple-element.60), channel_id=1, source_target_pairs={{0,8},{2,10},{4,12},{6,14},{8,0},{10,2},{12,4},{14,6},{1,9},{3,11}... | collective-permute-start | bytes 61448 | tf_op jit(solution)/shard_map/ppermute | solution.py:486
  102.0 12.6 %collective-permute-start.29 = (f32[5,8,128]{2,1,0:T(8,128)S(1)}, f32[5,8,128]{2,1,0:T(8,128)S(1)}, u32[]{:S(2)}, u32[]{:S(2)}) collective-permute-start(f32[5,8,128]{2,1,0:T(8,128)S(1)} %get-tuple-element.61), channel_id=1, source_target_pairs={{0,12},{2,14},{4,0},{6,2},{8,4},{10,6},{12,8},{14,10},{1,13},{3,15... | collective-permute-start | bytes 61448 | tf_op jit(solution)/shard_map/ppermute | solution.py:486
  105.7 8.9 %collective-permute-start.30 = (f32[5,8,128]{2,1,0:T(8,128)S(1)}, f32[5,8,128]{2,1,0:T(8,128)S(1)}, u32[]{:S(2)}, u32[]{:S(2)}) collective-permute-start(f32[5,8,128]{2,1,0:T(8,128)S(1)} %get-tuple-element.62), channel_id=1, source_target_pairs={{0,2},{2,0},{4,6},{6,4},{8,10},{10,8},{12,14},{14,12},{1,3},{3,1},... | collective-permute-start | bytes 61448 | tf_op jit(solution)/shard_map/ppermute | solution.py:486
  105.7 10.9 %collective-permute-start.31 = (f32[5,8,128]{2,1,0:T(8,128)S(1)}, f32[5,8,128]{2,1,0:T(8,128)S(1)}, u32[]{:S(2)}, u32[]{:S(2)}) collective-permute-start(f32[5,8,128]{2,1,0:T(8,128)S(1)} %get-tuple-element.63), channel_id=1, source_target_pairs={{0,6},{2,4},{4,10},{6,8},{8,14},{10,12},{12,2},{14,0},{1,7},{3,5},... | collective-permute-start | bytes 61448 | tf_op jit(solution)/shard_map/ppermute | solution.py:486
  108.7 8.0 %collective-permute-start.32 = (f32[5,8,128]{2,1,0:T(8,128)S(1)}, f32[5,8,128]{2,1,0:T(8,128)S(1)}, u32[]{:S(2)}, u32[]{:S(2)}) collective-permute-start(f32[5,8,128]{2,1,0:T(8,128)S(1)} %get-tuple-element.64), channel_id=1, source_target_pairs={{0,10},{2,8},{4,14},{6,12},{8,2},{10,0},{12,6},{14,4},{1,11},{3,9}... | collective-permute-start | bytes 61448 | tf_op jit(solution)/shard_map/ppermute | solution.py:486
  110.2 6.6 %collective-permute-start.33 = (f32[5,8,128]{2,1,0:T(8,128)S(1)}, f32[5,8,128]{2,1,0:T(8,128)S(1)}, u32[]{:S(2)}, u32[]{:S(2)}) collective-permute-start(f32[5,8,128]{2,1,0:T(8,128)S(1)} %get-tuple-element.65), channel_id=1, source_target_pairs={{0,14},{2,12},{4,2},{6,0},{8,6},{10,4},{12,10},{14,8},{1,15},{3,13... | collective-permute-start | bytes 61448 | tf_op jit(solution)/shard_map/ppermute | solution.py:486
  114.6 26.4 %collective-permute-start.6 = (f32[256,8,128]{2,1,0:T(8,128)}, f32[256,8,128]{2,1,0:T(8,128)}, u32[]{:S(2)}, u32[]{:S(2)}) collective-permute-start(f32[256,8,128]{2,1,0:T(8,128)} %slice_add_fusion.2), channel_id=1, source_target_pairs={{0,2},{2,0},{4,6},{6,4},{8,10},{10,8},{12,14},{14,12},{1,3},{3,1},... | collective-permute-start | bytes 3145736 | tf_op jit(solution)/shard_map/ppermute | solution.py:486
  114.6 48.9 %collective-permute-start.11 = (f32[256,8,128]{2,1,0:T(8,128)}, f32[256,8,128]{2,1,0:T(8,128)}, u32[]{:S(2)}, u32[]{:S(2)}) collective-permute-start(f32[256,8,128]{2,1,0:T(8,128)} %slice_add_fusion.1), channel_id=1, source_target_pairs={{0,2},{2,0},{4,6},{6,4},{8,10},{10,8},{12,14},{14,12},{1,3},{3,1},... | collective-permute-start | bytes 3145736 | tf_op jit(solution)/shard_map/ppermute | solution.py:486
  116.7 58.3 %collective-permute-start.16 = (f32[256,8,128]{2,1,0:T(8,128)}, f32[256,8,128]{2,1,0:T(8,128)S(1)}, u32[]{:S(2)}, u32[]{:S(2)}) collective-permute-start(f32[256,8,128]{2,1,0:T(8,128)} %slice_add_fusion), channel_id=1, source_target_pairs={{0,2},{2,0},{4,6},{6,4},{8,10},{10,8},{12,14},{14,12},{1,3},{3,1},... | collective-permute-start | bytes 3145736 | tf_op jit(solution)/shard_map/ppermute | solution.py:486
  142.2 33.8 %collective-permute-start.7 = (f32[64,8,128]{2,1,0:T(8,128)S(1)}, f32[64,8,128]{2,1,0:T(8,128)S(1)}, u32[]{:S(2)}, u32[]{:S(2)}) collective-permute-start(f32[64,8,128]{2,1,0:T(8,128)S(1)} %slice_add_fusion.26), channel_id=1, source_target_pairs={{0,4},{2,6},{4,8},{6,10},{8,12},{10,14},{12,0},{14,2},{1,5},{3,7},... | collective-permute-start | bytes 786440 | tf_op jit(solution)/shard_map/ppermute | solution.py:486
  164.7 14.3 %collective-permute-start.12 = (f32[64,8,128]{2,1,0:T(8,128)S(1)}, f32[64,8,128]{2,1,0:T(8,128)S(1)}, u32[]{:S(2)}, u32[]{:S(2)}) collective-permute-start(f32[64,8,128]{2,1,0:T(8,128)S(1)} %slice_add_fusion.18), channel_id=1, source_target_pairs={{0,4},{2,6},{4,8},{6,10},{8,12},{10,14},{12,0},{14,2},{1,5},{3,7},... | collective-permute-start | bytes 786440 | tf_op jit(solution)/shard_map/ppermute | solution.py:486
  176.0 11.1 %collective-permute-start.17 = (f32[64,8,128]{2,1,0:T(8,128)S(1)}, f32[64,8,128]{2,1,0:T(8,128)S(1)}, u32[]{:S(2)}, u32[]{:S(2)}) collective-permute-start(f32[64,8,128]{2,1,0:T(8,128)S(1)} %slice_add_fusion.10), channel_id=1, source_target_pairs={{0,4},{2,6},{4,8},{6,10},{8,12},{10,14},{12,0},{14,2},{1,5},{3,7},... | collective-permute-start | bytes 786440 | tf_op jit(solution)/shard_map/ppermute | solution.py:486
  177.2 15.4 %collective-permute-start.8 = (f32[64,8,128]{2,1,0:T(8,128)S(1)}, f32[64,8,128]{2,1,0:T(8,128)S(1)}, u32[]{:S(2)}, u32[]{:S(2)}) collective-permute-start(f32[64,8,128]{2,1,0:T(8,128)S(1)} %fusion.8), channel_id=1, source_target_pairs={{0,4},{2,6},{4,8},{6,10},{8,12},{10,14},{12,0},{14,2},{1,5},{3,7},... | collective-permute-start | bytes 786440 | tf_op jit(solution)/shard_map/ppermute | solution.py:486
  180.2 18.2 %collective-permute-start.13 = (f32[64,8,128]{2,1,0:T(8,128)S(1)}, f32[64,8,128]{2,1,0:T(8,128)S(1)}, u32[]{:S(2)}, u32[]{:S(2)}) collective-permute-start(f32[64,8,128]{2,1,0:T(8,128)S(1)} %fusion.5), channel_id=1, source_target_pairs={{0,4},{2,6},{4,8},{6,10},{8,12},{10,14},{12,0},{14,2},{1,5},{3,7},... | collective-permute-start | bytes 786440 | tf_op jit(solution)/shard_map/ppermute | solution.py:486
  188.1 16.0 %collective-permute-start.18 = (f32[64,8,128]{2,1,0:T(8,128)S(1)}, f32[64,8,128]{2,1,0:T(8,128)S(1)}, u32[]{:S(2)}, u32[]{:S(2)}) collective-permute-start(f32[64,8,128]{2,1,0:T(8,128)S(1)} %fusion.2), channel_id=1, source_target_pairs={{0,4},{2,6},{4,8},{6,10},{8,12},{10,14},{12,0},{14,2},{1,5},{3,7},... | collective-permute-start | bytes 786440 | tf_op jit(solution)/shard_map/ppermute | solution.py:486
  193.9 13.4 %collective-permute-start.9 = (f32[64,8,128]{2,1,0:T(8,128)S(1)}, f32[64,8,128]{2,1,0:T(8,128)S(1)}, u32[]{:S(2)}, u32[]{:S(2)}) collective-permute-start(f32[64,8,128]{2,1,0:T(8,128)S(1)} %fusion.7), channel_id=1, source_target_pairs={{0,4},{2,6},{4,8},{6,10},{8,12},{10,14},{12,0},{14,2},{1,5},{3,7},... | collective-permute-start | bytes 786440 | tf_op jit(solution)/shard_map/ppermute | solution.py:486
  199.5 14.1 %collective-permute-start.14 = (f32[64,8,128]{2,1,0:T(8,128)S(1)}, f32[64,8,128]{2,1,0:T(8,128)S(1)}, u32[]{:S(2)}, u32[]{:S(2)}) collective-permute-start(f32[64,8,128]{2,1,0:T(8,128)S(1)} %fusion.4), channel_id=1, source_target_pairs={{0,4},{2,6},{4,8},{6,10},{8,12},{10,14},{12,0},{14,2},{1,5},{3,7},... | collective-permute-start | bytes 786440 | tf_op jit(solution)/shard_map/ppermute | solution.py:486
  205.1 10.2 %collective-permute-start.19 = (f32[64,8,128]{2,1,0:T(8,128)S(1)}, f32[64,8,128]{2,1,0:T(8,128)S(1)}, u32[]{:S(2)}, u32[]{:S(2)}) collective-permute-start(f32[64,8,128]{2,1,0:T(8,128)S(1)} %fusion.1), channel_id=1, source_target_pairs={{0,4},{2,6},{4,8},{6,10},{8,12},{10,14},{12,0},{14,2},{1,5},{3,7},... | collective-permute-start | bytes 786440 | tf_op jit(solution)/shard_map/ppermute | solution.py:486
  209.7 7.1 %collective-permute-start.35 = (f32[8,8,128]{2,1,0:T(8,128)S(1)}, f32[8,8,128]{2,1,0:T(8,128)S(1)}, u32[]{:S(2)}, u32[]{:S(2)}) collective-permute-start(f32[8,8,128]{2,1,0:T(8,128)S(1)} %get-tuple-element.69), channel_id=1, source_target_pairs={{0,4},{2,6},{4,8},{6,10},{8,12},{10,14},{12,0},{14,2},{1,5},{3,7},... | collective-permute-start | bytes 98312 | tf_op jit(solution)/shard_map/ppermute | solution.py:486
  209.8 11.1 %collective-permute-start.36 = (f32[8,8,128]{2,1,0:T(8,128)S(1)}, f32[8,8,128]{2,1,0:T(8,128)S(1)}, u32[]{:S(2)}, u32[]{:S(2)}) collective-permute-start(f32[8,8,128]{2,1,0:T(8,128)S(1)} %get-tuple-element.70), channel_id=1, source_target_pairs={{0,8},{2,10},{4,12},{6,14},{8,0},{10,2},{12,4},{14,6},{1,9},{3,11}... | collective-permute-start | bytes 98312 | tf_op jit(solution)/shard_map/ppermute | solution.py:486
  212.0 12.7 %collective-permute-start.37 = (f32[8,8,128]{2,1,0:T(8,128)S(1)}, f32[8,8,128]{2,1,0:T(8,128)S(1)}, u32[]{:S(2)}, u32[]{:S(2)}) collective-permute-start(f32[8,8,128]{2,1,0:T(8,128)S(1)} %get-tuple-element.71), channel_id=1, source_target_pairs={{0,12},{2,14},{4,0},{6,2},{8,4},{10,6},{12,8},{14,10},{1,13},{3,15... | collective-permute-start | bytes 98312 | tf_op jit(solution)/shard_map/ppermute | solution.py:486
  213.6 11.1 %collective-permute-start.38 = (f32[8,8,128]{2,1,0:T(8,128)S(1)}, f32[8,8,128]{2,1,0:T(8,128)S(1)}, u32[]{:S(2)}, u32[]{:S(2)}) collective-permute-start(f32[8,8,128]{2,1,0:T(8,128)S(1)} %get-tuple-element.72), channel_id=1, source_target_pairs={{0,2},{2,0},{4,6},{6,4},{8,10},{10,8},{12,14},{14,12},{1,3},{3,1},... | collective-permute-start | bytes 98312 | tf_op jit(solution)/shard_map/ppermute | solution.py:486
  215.2 10.4 %collective-permute-start.39 = (f32[8,8,128]{2,1,0:T(8,128)S(1)}, f32[8,8,128]{2,1,0:T(8,128)S(1)}, u32[]{:S(2)}, u32[]{:S(2)}) collective-permute-start(f32[8,8,128]{2,1,0:T(8,128)S(1)} %get-tuple-element.73), channel_id=1, source_target_pairs={{0,6},{2,4},{4,10},{6,8},{8,14},{10,12},{12,2},{14,0},{1,7},{3,5},... | collective-permute-start | bytes 98312 | tf_op jit(solution)/shard_map/ppermute | solution.py:486
  216.8 11.7 %collective-permute-start.40 = (f32[8,8,128]{2,1,0:T(8,128)S(1)}, f32[8,8,128]{2,1,0:T(8,128)S(1)}, u32[]{:S(2)}, u32[]{:S(2)}) collective-permute-start(f32[8,8,128]{2,1,0:T(8,128)S(1)} %get-tuple-element.74), channel_id=1, source_target_pairs={{0,10},{2,8},{4,14},{6,12},{8,2},{10,0},{12,6},{14,4},{1,11},{3,9}... | collective-permute-start | bytes 98312 | tf_op jit(solution)/shard_map/ppermute | solution.py:486
  220.9 9.5 %collective-permute-start.41 = (f32[8,8,128]{2,1,0:T(8,128)S(1)}, f32[8,8,128]{2,1,0:T(8,128)S(1)}, u32[]{:S(2)}, u32[]{:S(2)}) collective-permute-start(f32[8,8,128]{2,1,0:T(8,128)S(1)} %get-tuple-element.75), channel_id=1, source_target_pairs={{0,14},{2,12},{4,2},{6,0},{8,6},{10,4},{12,10},{14,8},{1,15},{3,13... | collective-permute-start | bytes 98312 | tf_op jit(solution)/shard_map/ppermute | solution.py:486
  224.7 7.3 %collective-permute-start.43 = (f32[8,8,128]{2,1,0:T(8,128)S(1)}, f32[8,8,128]{2,1,0:T(8,128)S(1)}, u32[]{:S(2)}, u32[]{:S(2)}) collective-permute-start(f32[8,8,128]{2,1,0:T(8,128)S(1)} %get-tuple-element.79), channel_id=1, source_target_pairs={{0,4},{2,6},{4,8},{6,10},{8,12},{10,14},{12,0},{14,2},{1,5},{3,7},... | collective-permute-start | bytes 98312 | tf_op jit(solution)/shard_map/ppermute | solution.py:486
  224.7 8.8 %collective-permute-start.44 = (f32[8,8,128]{2,1,0:T(8,128)S(1)}, f32[8,8,128]{2,1,0:T(8,128)S(1)}, u32[]{:S(2)}, u32[]{:S(2)}) collective-permute-start(f32[8,8,128]{2,1,0:T(8,128)S(1)} %get-tuple-element.80), channel_id=1, source_target_pairs={{0,8},{2,10},{4,12},{6,14},{8,0},{10,2},{12,4},{14,6},{1,9},{3,11}... | collective-permute-start | bytes 98312 | tf_op jit(solution)/shard_map/ppermute | solution.py:486
  225.6 11.6 %collective-permute-start.45 = (f32[8,8,128]{2,1,0:T(8,128)S(1)}, f32[8,8,128]{2,1,0:T(8,128)S(1)}, u32[]{:S(2)}, u32[]{:S(2)}) collective-permute-start(f32[8,8,128]{2,1,0:T(8,128)S(1)} %get-tuple-element.81), channel_id=1, source_target_pairs={{0,12},{2,14},{4,0},{6,2},{8,4},{10,6},{12,8},{14,10},{1,13},{3,15... | collective-permute-start | bytes 98312 | tf_op jit(solution)/shard_map/ppermute | solution.py:486
  228.6 8.7 %collective-permute-start.46 = (f32[8,8,128]{2,1,0:T(8,128)S(1)}, f32[8,8,128]{2,1,0:T(8,128)S(1)}, u32[]{:S(2)}, u32[]{:S(2)}) collective-permute-start(f32[8,8,128]{2,1,0:T(8,128)S(1)} %get-tuple-element.82), channel_id=1, source_target_pairs={{0,2},{2,0},{4,6},{6,4},{8,10},{10,8},{12,14},{14,12},{1,3},{3,1},... | collective-permute-start | bytes 98312 | tf_op jit(solution)/shard_map/ppermute | solution.py:486
  230.4 7.9 %collective-permute-start.47 = (f32[8,8,128]{2,1,0:T(8,128)S(1)}, f32[8,8,128]{2,1,0:T(8,128)S(1)}, u32[]{:S(2)}, u32[]{:S(2)}) collective-permute-start(f32[8,8,128]{2,1,0:T(8,128)S(1)} %get-tuple-element.83), channel_id=1, source_target_pairs={{0,6},{2,4},{4,10},{6,8},{8,14},{10,12},{12,2},{14,0},{1,7},{3,5},... | collective-permute-start | bytes 98312 | tf_op jit(solution)/shard_map/ppermute | solution.py:486
  232.0 9.2 %collective-permute-start.48 = (f32[8,8,128]{2,1,0:T(8,128)S(1)}, f32[8,8,128]{2,1,0:T(8,128)S(1)}, u32[]{:S(2)}, u32[]{:S(2)}) collective-permute-start(f32[8,8,128]{2,1,0:T(8,128)S(1)} %get-tuple-element.84), channel_id=1, source_target_pairs={{0,10},{2,8},{4,14},{6,12},{8,2},{10,0},{12,6},{14,4},{1,11},{3,9}... | collective-permute-start | bytes 98312 | tf_op jit(solution)/shard_map/ppermute | solution.py:486
  233.5 8.2 %collective-permute-start.49 = (f32[8,8,128]{2,1,0:T(8,128)S(1)}, f32[8,8,128]{2,1,0:T(8,128)S(1)}, u32[]{:S(2)}, u32[]{:S(2)}) collective-permute-start(f32[8,8,128]{2,1,0:T(8,128)S(1)} %get-tuple-element.85), channel_id=1, source_target_pairs={{0,14},{2,12},{4,2},{6,0},{8,6},{10,4},{12,10},{14,8},{1,15},{3,13... | collective-permute-start | bytes 98312 | tf_op jit(solution)/shard_map/ppermute | solution.py:486
  237.2 6.0 %collective-permute-start.51 = (f32[8,8,128]{2,1,0:T(8,128)S(1)}, f32[8,8,128]{2,1,0:T(8,128)S(1)}, u32[]{:S(2)}, u32[]{:S(2)}) collective-permute-start(f32[8,8,128]{2,1,0:T(8,128)S(1)} %get-tuple-element.89), channel_id=1, source_target_pairs={{0,4},{2,6},{4,8},{6,10},{8,12},{10,14},{12,0},{14,2},{1,5},{3,7},... | collective-permute-start | bytes 98312 | tf_op jit(solution)/shard_map/ppermute | solution.py:486
  237.2 7.5 %collective-permute-start.52 = (f32[8,8,128]{2,1,0:T(8,128)S(1)}, f32[8,8,128]{2,1,0:T(8,128)S(1)}, u32[]{:S(2)}, u32[]{:S(2)}) collective-permute-start(f32[8,8,128]{2,1,0:T(8,128)S(1)} %get-tuple-element.90), channel_id=1, source_target_pairs={{0,8},{2,10},{4,12},{6,14},{8,0},{10,2},{12,4},{14,6},{1,9},{3,11}... | collective-permute-start | bytes 98312 | tf_op jit(solution)/shard_map/ppermute | solution.py:486
  238.3 11.7 %collective-permute-start.53 = (f32[8,8,128]{2,1,0:T(8,128)S(1)}, f32[8,8,128]{2,1,0:T(8,128)S(1)}, u32[]{:S(2)}, u32[]{:S(2)}) collective-permute-start(f32[8,8,128]{2,1,0:T(8,128)S(1)} %get-tuple-element.91), channel_id=1, source_target_pairs={{0,12},{2,14},{4,0},{6,2},{8,4},{10,6},{12,8},{14,10},{1,13},{3,15... | collective-permute-start | bytes 98312 | tf_op jit(solution)/shard_map/ppermute | solution.py:486
  241.2 8.9 %collective-permute-start.54 = (f32[8,8,128]{2,1,0:T(8,128)S(1)}, f32[8,8,128]{2,1,0:T(8,128)S(1)}, u32[]{:S(2)}, u32[]{:S(2)}) collective-permute-start(f32[8,8,128]{2,1,0:T(8,128)S(1)} %get-tuple-element.92), channel_id=1, source_target_pairs={{0,2},{2,0},{4,6},{6,4},{8,10},{10,8},{12,14},{14,12},{1,3},{3,1},... | collective-permute-start | bytes 98312 | tf_op jit(solution)/shard_map/ppermute | solution.py:486
  241.7 8.9 %collective-permute-start.55 = (f32[8,8,128]{2,1,0:T(8,128)S(1)}, f32[8,8,128]{2,1,0:T(8,128)S(1)}, u32[]{:S(2)}, u32[]{:S(2)}) collective-permute-start(f32[8,8,128]{2,1,0:T(8,128)S(1)} %get-tuple-element.93), channel_id=1, source_target_pairs={{0,6},{2,4},{4,10},{6,8},{8,14},{10,12},{12,2},{14,0},{1,7},{3,5},... | collective-permute-start | bytes 98312 | tf_op jit(solution)/shard_map/ppermute | solution.py:486
  243.3 7.4 %collective-permute-start.56 = (f32[8,8,128]{2,1,0:T(8,128)S(1)}, f32[8,8,128]{2,1,0:T(8,128)S(1)}, u32[]{:S(2)}, u32[]{:S(2)}) collective-permute-start(f32[8,8,128]{2,1,0:T(8,128)S(1)} %get-tuple-element.94), channel_id=1, source_target_pairs={{0,10},{2,8},{4,14},{6,12},{8,2},{10,0},{12,6},{14,4},{1,11},{3,9}... | collective-permute-start | bytes 98312 | tf_op jit(solution)/shard_map/ppermute | solution.py:486
  (27 other events, 138.1 us)

commit v2 on v0

--- a/solution.py
+++ b/solution.py
@@ -3,6 +3,8 @@
 import jax
 import jax.numpy as jnp
 from jax import lax
+from jax.experimental import pallas as pl
+from jax.experimental.pallas import tpu as pltpu
 from jax.sharding import PartitionSpec as P
 
 PB_DEV = 32
@@ -88,7 +90,7 @@
     return lax.dynamic_slice_in_dim(whole_sum, lax.axis_index("sub") * per_device, per_device, 1)
 
 
-def body(
+def plain_body(
     child_weight,
     child_mean,
     child_factor,
@@ -151,6 +153,489 @@
     return (level_one, level_two)
 
 
+TILE = 8
+UNROLL = 8
+WIDTHS = (16, 16, 8, 8)
+GROUPS = {6: (0, 1, 2, 3, 4)}
+WAIT_FETCH = True
+HEAD = 1
+
+
+def tile_count(width, slots):
+    return (width // TILE) * slots + (slots * (width % TILE) + TILE - 1) // TILE
+
+
+def split_pair(values):
+    high = values.astype(jnp.bfloat16)
+    low = (values - high.astype(jnp.float32)).astype(jnp.bfloat16)
+    return jnp.concatenate([high, low], 1)
+
+
+def row_table(rows):
+    width = rows.shape[1]
+    labels = lax.broadcasted_iota(jnp.int32, (width, width), 0)
+    picks = jnp.where(labels == rows, 1.0, 0.0).astype(jnp.bfloat16)
+    return jnp.concatenate([picks, picks], 1)
+
+
+def fold_block(values, rows):
+    return lax.dot_general(
+        split_pair(values),
+        row_table(rows),
+        (((1,), (1,)), ((), ())),
+        preferred_element_type=jnp.float32,
+    )
+
+
+def tile_rows():
+    return lax.broadcasted_iota(jnp.int32, (TILE, 1), 0)
+
+
+def spread_group(line, extra, group):
+    share = TILE // extra
+    line = jnp.where(tile_rows() // extra == group, line, 0.0)
+    return sum((pltpu.roll(line, turn * extra, 0) for turn in range(1, share)), start=line)
+
+
+def child_kernel(first, width, regions, slots, *refs):
+    geometry = first == 0
+    place_ref, live_ref = refs[:2]
+    count = 4 if geometry else 3
+    sources = refs[2 : 2 + count]
+    keep_ref, send_ref = refs[2 + count : 4 + count]
+    targets = refs[4 + count : 4 + 2 * count]
+    rows_ref, weight_ref = targets[:2]
+    moments, totals, load_sems, out_sems = refs[4 + 2 * count :]
+    block_count, row_count = rows_ref.shape
+    full, extra = width // TILE, width % TILE
+    per_region = tile_count(width, slots)
+    group = 16
+    first_colour = max(first, 10) - 10
+    colour_total = 0 if geometry else width
+    loads = []
+    for at, (source, target) in enumerate(zip(sources, targets, strict=True)):
+        if colour_total and at == 2:
+            source = source.at[pl.ds(first_colour, colour_total)]
+        loads.append(pltpu.make_async_copy(source, target, load_sems.at[at]))
+    if geometry:
+        mean_ref, factor_ref = targets[2:4]
+    else:
+        colours = targets[2]
+    for load in loads:
+        load.start()
+
+    def clear(step, carry):
+        totals[pl.ds(step * 16, 16)] = jnp.zeros((16, TILE, row_count), jnp.float32)
+        return carry
+
+    lax.fori_loop(0, totals.shape[0] // 16, clear, 0)
+    for load in loads:
+        load.wait()
+
+    def prepare(step, carry):
+        start = pl.multiple_of(step * group, group)
+        part = pl.ds(start, group)
+        weight = weight_ref[part, :]
+        values = {}
+        if geometry:
+            centre = [mean_ref[axis, part, :] for axis in range(3)]
+            factor = [factor_ref[entry, part, :] for entry in range(6)]
+            spread = [
+                factor[0] * factor[0],
+                factor[0] * factor[1],
+                factor[0] * factor[3],
+                factor[1] * factor[1] + factor[2] * factor[2],
+                factor[1] * factor[3] + factor[2] * factor[4],
+                factor[3] * factor[3] + factor[4] * factor[4] + factor[5] * factor[5],
+            ]
+            values[0] = weight
+            for axis in range(3):
+                values[1 + axis] = weight * centre[axis]
+            for entry, (left, right) in enumerate(PAIRS):
+                values[4 + entry] = weight * (spread[entry] + centre[left] * centre[right])
+        for entry in range(colour_total):
+            values[10 + first_colour + entry] = weight * colours[entry, part, :].astype(jnp.float32)
+        for place in range(full * TILE + (TILE if extra else 0)):
+            component = first + (place if place < full * TILE else full * TILE + place % extra)
+            moments[pl.ds(place * block_count + start, group), :] = values[component]
+        return carry
+
+    lax.fori_loop(0, block_count // group, prepare, 0)
+    live = live_ref[0]
+
+    def fold(step, carry):
+        folded = []
+        for turn in range(UNROLL):
+            block = step * UNROLL + turn
+            place = place_ref[block]
+            region, slot = place // slots, place % slots
+            lines = [
+                moments[pl.ds(tile * TILE * block_count + block, TILE, stride=block_count), :]
+                for tile in range(full)
+            ]
+            if extra:
+                line = moments[pl.ds(full * TILE * block_count + block, TILE, stride=block_count), :]
+                lines.append(jnp.where(tile_rows() // extra == slot % (TILE // extra), line, 0.0))
+            rows = jnp.where(block < live, rows_ref[pl.ds(block, 1), :], -1)
+            folded.append((region * per_region, slot, fold_block(jnp.concatenate(lines, 0), rows)))
+        for base, slot, result in folded:
+            for tile in range(full):
+                totals[base + tile * slots + slot] += result[tile * TILE : (tile + 1) * TILE]
+            if extra:
+                totals[base + full * slots + slot // (TILE // extra)] += result[full * TILE :]
+        return carry
+
+    lax.fori_loop(0, (live + UNROLL - 1) // UNROLL, fold, 0)
+    half = regions * per_region
+    send = pltpu.make_async_copy(totals.at[pl.ds(half, half)], send_ref, out_sems.at[0])
+    keep = pltpu.make_async_copy(totals.at[pl.ds(0, half)], keep_ref, out_sems.at[1])
+    send.start()
+    keep.start()
+    send.wait()
+    keep.wait()
+
+
+def fold_children(place, live, arrays, first, width, regions, slots, vmem):
+    rows, weight, mean, factor, colour = arrays
+    geometry = first == 0
+    used = [rows, weight, mean, factor] if geometry else [rows, weight, colour]
+    block_count, row_count = rows.shape
+    per_region = tile_count(width, slots)
+    padded = width // TILE * TILE + (TILE if width % TILE else 0)
+    half = jax.ShapeDtypeStruct((regions * per_region, TILE, row_count), jnp.float32)
+    scalars = pl.BlockSpec(memory_space=pltpu.SMEM)
+    outside = pl.BlockSpec(memory_space=pl.ANY)
+    targets = [
+        pltpu.VMEM(array.shape if geometry or at < 2 else (width,) + array.shape[1:], array.dtype)
+        for at, array in enumerate(used)
+    ]
+
+    def kernel(*refs):
+        child_kernel(first, width, regions, slots, *refs)
+
+    return pl.pallas_call(
+        kernel,
+        out_shape=(half, half),
+        in_specs=[scalars, scalars] + [outside] * len(used),
+        out_specs=(outside, outside),
+        scratch_shapes=targets
+        + [
+            pltpu.VMEM((padded * block_count, row_count), jnp.float32),
+            pltpu.VMEM((2 * regions * per_region, TILE, row_count), jnp.float32),
+            pltpu.SemaphoreType.DMA((len(used),)),
+            pltpu.SemaphoreType.DMA((2,)),
+        ],
+        compiler_params=pltpu.CompilerParams(vmem_limit_bytes=vmem * 1024 * 1024),
+        cost_estimate=pl.CostEstimate(flops=1024, bytes_accessed=1024, transcendentals=0),
+        name="fold_children",
+    )(place, live, *used)
+
+
+def group_sizes(widths, cap):
+    full = sum(width // TILE for width in widths)
+    extra = sum(width % TILE for width in widths)
+    return full, extra, full * cap + (1 if extra else 0)
+
+
+def parent_kernel(widths, owners, cap, coded, *refs):
+    place_ref, code_ref, rows_ref = refs[:3]
+    sums_refs = refs[3 : 3 + len(widths)]
+    totals = refs[3 + len(widths)]
+    block_count = rows_ref.shape[0]
+    full, extra, used = group_sizes(widths, cap)
+    per_owner = used + (1 if coded else 0)
+    totals[...] = jnp.zeros(totals.shape, jnp.float32)
+    for start in range(0, block_count, UNROLL):
+        folded = []
+        for block in range(start, start + UNROLL):
+            place = place_ref[block]
+            owner, rank = place // cap, place % cap
+            lines, shared = [], []
+            for width, sums_ref in zip(widths, sums_refs, strict=True):
+                tiles = width // TILE
+                lines += [sums_ref[tile * block_count + block] for tile in range(tiles)]
+                if width % TILE:
+                    share = TILE // extra
+                    line = sums_ref[tiles * block_count + block // share]
+                    line = spread_group(line, extra, block % share)
+                    shared.append(jnp.where(tile_rows() // extra == rank, line, 0.0))
+            rows = rows_ref[pl.ds(block, 1), :]
+            result = fold_block(jnp.concatenate(lines + shared, 0), rows)
+            folded.append((owner * per_owner, rank, result))
+            if coded:
+                code = code_ref[block].astype(jnp.float32)
+                totals[owner * per_owner + used] += jnp.where(tile_rows() == rank, code, 0.0)
+        for base, rank, result in folded:
+            for tile in range(full):
+                totals[base + tile * cap + rank] += result[tile * TILE : (tile + 1) * TILE]
+            if extra:
+                totals[base + full * cap] += result[full * TILE :]
+
+
+def fold_parents(place, code, rows, sums, widths, owners, cap, coded):
+    row_count = rows.shape[1]
+    per_owner = group_sizes(widths, cap)[2] + (1 if coded else 0)
+    whole = pl.BlockSpec(memory_space=pltpu.VMEM)
+    scalars = pl.BlockSpec(memory_space=pltpu.SMEM)
+
+    def kernel(*refs):
+        parent_kernel(widths, owners, cap, coded, *refs)
+
+    return pl.pallas_call(
+        kernel,
+        out_shape=jax.ShapeDtypeStruct((owners * per_owner, TILE, row_count), jnp.float32),
+        in_specs=[scalars, scalars, whole] + [whole] * len(sums),
+        out_specs=whole,
+        compiler_params=pltpu.CompilerParams(vmem_limit_bytes=16 * 1024 * 1024),
+        cost_estimate=pl.CostEstimate(flops=1024, bytes_accessed=1024, transcendentals=0),
+        name="fold_parents",
+    )(place, code, rows, *sums)
+
+
+def place_kernel(widths, owners, cap, slots, coded, *refs):
+    if coded:
+        sub_ref, in_ref, keep_ref, send_ref, codes_ref = refs
+    else:
+        codes_in, in_ref, keep_ref, send_ref = refs
+    full, extra, used = group_sizes(widths, cap)
+    per_owner = used + (1 if coded else 0)
+    if coded:
+        for owner in range(owners):
+            code = in_ref[owner * per_owner + used].astype(jnp.int32)
+            codes_ref[owner] = (code // slots + sub_ref[0]) % 2 * slots + code % slots
+        codes_in = codes_ref
+    for half, out_ref in enumerate((keep_ref, send_ref)):
+        for slot in range(slots):
+            label = half * slots + slot
+            sums = [jnp.zeros(in_ref.shape[1:], jnp.float32) for _ in range(full)]
+            for owner in range(owners):
+                for rank in range(cap):
+                    here = codes_in[owner, rank : rank + 1, :] == label
+                    for tile in range(full):
+                        line = in_ref[owner * per_owner + tile * cap + rank]
+                        sums[tile] += jnp.where(here, line, 0.0)
+            for tile in range(full):
+                out_ref[tile * slots + slot] = sums[tile]
+        if extra:
+            share = TILE // extra
+            sums = [jnp.zeros(in_ref.shape[1:], jnp.float32) for _ in range(slots // share)]
+            for owner in range(owners):
+                for rank in range(cap):
+                    line = spread_group(in_ref[owner * per_owner + full * cap], extra, rank)
+                    code = codes_in[owner, rank : rank + 1, :] - half * slots - tile_rows() // extra
+                    for tile in range(slots // share):
+                        sums[tile] += jnp.where(code == tile * share, line, 0.0)
+            for tile in range(slots // share):
+                out_ref[full * slots + tile] = sums[tile]
+
+
+def place_parents(sub_at, codes, received, widths, owners, cap, slots):
+    row_count = received.shape[2]
+    coded = codes is None
+    full, extra, _ = group_sizes(widths, cap)
+    per_half = full * slots + slots * extra // TILE
+    whole = pl.BlockSpec(memory_space=pltpu.VMEM)
+    scalars = pl.BlockSpec(memory_space=pltpu.SMEM)
+    half = jax.ShapeDtypeStruct((per_half, TILE, row_count), jnp.float32)
+    table = jax.ShapeDtypeStruct((owners, TILE, row_count), jnp.int32)
+
+    def kernel(*refs):
+        place_kernel(widths, owners, cap, slots, coded, *refs)
+
+    return pl.pallas_call(
+        kernel,
+        out_shape=(half, half, table) if coded else (half, half),
+        in_specs=[scalars if coded else whole, whole],
+        out_specs=(whole, whole, whole) if coded else (whole, whole),
+        compiler_params=pltpu.CompilerParams(vmem_limit_bytes=16 * 1024 * 1024),
+        cost_estimate=pl.CostEstimate(flops=1024, bytes_accessed=1024, transcendentals=0),
+        name="place_parents",
+    )(sub_at.reshape(1) if coded else codes, received)
+
+
+def unpack(tiles, widths, slots):
+    row_count = tiles.shape[2]
+    parts, start = [], 0
+    for width in widths:
+        full = width // TILE
+        whole = tiles[start : start + full * slots].reshape(full, slots, TILE, row_count)
+        parts.append([whole.transpose(0, 2, 1, 3).reshape(full * TILE, slots, row_count)])
+        start += full * slots
+    for part, width in zip(parts, widths, strict=True):
+        if width % TILE:
+            rest = tiles[start:].reshape(slots, width % TILE, row_count)
+            part.append(rest.transpose(1, 0, 2))
+    return [jnp.concatenate(part, 0) for part in parts]
+
+
+def merged_parts(parts):
+    sums = parts[0]
+    divisor = jnp.maximum(sums[0], WEIGHT_FLOOR)
+    centre = sums[1:4] / divisor
+    centre_outer = jnp.stack([centre[first] * centre[second] for first, second in PAIRS])
+    spread = sums[4:10] / divisor - centre_outer
+    rest = [part / divisor for part in [sums[10:]] + parts[1:] if part.shape[0]]
+    return jnp.concatenate([sums[:1], centre, spread] + rest, 0)
+
+
+def cut_components(components):
+    chunks, start = [(0, 10)], 10
+    for width in WIDTHS:
+        width = min(width, components - start)
+        if width > 0:
+            chunks.append((start, width))
+            start += width
+    if start < components:
+        chunks.append((start, components - start))
+    return chunks
+
+
+def after(values, *others):
+    return lax.optimization_barrier((values,) + others)[0]
+
+
+def span_body(
+    child_weight,
+    child_mean,
+    child_factor,
+    child_colour,
+    child_dest,
+    child_slot,
+    child_row,
+    live_blocks,
+    parent_owner,
+    parent_slot,
+    parent_row,
+):
+    spans = lax.axis_size("span")
+    levels = spans.bit_length() - 1
+    components = 10 + child_colour.shape[0]
+    span_at, sub_at = lax.axis_index("span"), lax.axis_index("sub")
+    cap_two = max(1, (PB_DEV + spans - 1) // spans)
+
+    def swap(values):
+        return lax.ppermute(values, "sub", [(0, 1), (1, 0)])
+
+    def cross(values, bit):
+        return lax.ppermute(values, "span", [(at, at ^ (1 << bit)) for at in range(spans)])
+
+    away = child_dest ^ span_at
+    half = (child_slot // PB_DEV + sub_at) % 2
+
+    def place_in(order):
+        region = sum(((away >> bit) & 1) << (levels - 1 - at) for at, bit in enumerate(order))
+        return (half * spans + region) * PB_DEV + child_slot % PB_DEV
+
+    place_two = parent_owner * cap_two + earlier_same(parent_owner)
+
+    arrays = (child_row, child_weight, child_mean, child_factor, child_colour)
+    chunks = cut_components(components)
+    total = len(chunks)
+    sizes = [tile_count(width, PB_DEV) for _, width in chunks]
+    orders = [list(range(levels)) for _ in chunks]
+    terms = [[] for _ in chunks]
+    sends = [[] for _ in chunks]
+
+    def fold(at, *others):
+        place = place_in(orders[at])
+        if others:
+            place = after(place, *others)
+        keep, send = fold_children(place, live_blocks, arrays, *chunks[at], spans, PB_DEV, 56 if at < HEAD else 40)
+        terms[at] = [keep, swap(send)]
+
+    def part(at, low, high):
+        return sum(
+            (term[low * sizes[at] : high * sizes[at]] for term in terms[at][1:]),
+            start=terms[at][0][low * sizes[at] : high * sizes[at]],
+        )
+
+    def exchange(at, level, *others):
+        low = spans >> (level + 1)
+        send = part(at, low, 2 * low)
+        if others:
+            send = after(send, *others)
+        sends[at].append(send)
+        terms[at].append(cross(send, orders[at][level]))
+
+    def send_of(at, level):
+        low = spans >> (level + 1)
+        return part(at, low, 2 * low)
+
+    def depart(at, level, send):
+        terms[at].append(cross(send, orders[at][level]))
+
+    def depart_alone(at, level):
+        send = send_of(at, level)
+        depart(at, level, send)
+        return send
+
+    level_two, codes, fetched = [], [None], []
+
+    def raise_level(group, *others):
+        widths = [chunks[at][1] for at in group]
+        parts = fold_parents(
+            after(place_two, *others) if others else place_two,
+            parent_slot,
+            parent_row,
+            [sums[at] for at in group],
+            widths,
+            spans,
+            cap_two,
+            codes[0] is None,
+        )
+        parts = lax.all_to_all(parts, "span", split_axis=0, concat_axis=0, tiled=True)
+        fetched.append(parts)
+        placed = place_parents(sub_at, codes[0], parts, widths, spans, cap_two, GB_DEV)
+        if codes[0] is None:
+            codes[0] = placed[2]
+        level_two.extend(unpack(placed[0] + swap(placed[1]), widths, GB_DEV))
+
+    fold(0)
+    fold(1, terms[0][0])
+    first_send = depart_alone(0, 0)
+    fold(2, terms[1][0], first_send)
+    second_send = depart_alone(1, 0)
+    for at in range(3, total):
+        fold(at, terms[at - 1][0], second_send)
+    sums = [None] * total
+    for phase in range(total + levels - 2):
+        moves, done = [], []
+        if phase + 2 < total:
+            moves.append((phase + 2, 0))
+        for turn in range(levels - 1):
+            if 0 <= phase - turn < total:
+                moves.append((phase - turn, turn + 1))
+        if phase >= levels - 1:
+            done.append(terms[phase - levels + 1][-1])
+        if phase == 0:
+            done.append(terms[total - 1][1])
+        if WAIT_FETCH:
+            done += fetched[-1:]
+        ready = [send_of(at, level) for at, level in moves]
+        ready = lax.optimization_barrier(tuple(ready + done))[: len(ready)]
+        for (at, level), send in zip(moves, ready, strict=True):
+            depart(at, level, send)
+            if level == levels - 1:
+                sums[at] = part(at, 0, 1)
+        if phase in GROUPS:
+            raise_level(GROUPS[phase], *ready)
+    raise_level(GROUPS[total + levels - 2])
+    level_one = []
+    for at in range(total):
+        level_one += unpack(sums[at], [chunks[at][1]], PB_DEV)
+    return (merged_parts(level_one), merged_parts(level_two))
+
+
+def body(*arrays):
+    spans, subs = lax.axis_size("span"), lax.axis_size("sub")
+    blocks = arrays[0].shape[0]
+    dense = spans * subs * PB_DEV
+    fits = subs == 2 and spans & (spans - 1) == 0 and dense <= 4 * blocks
+    if fits and PB_DEV == 4 * spans and blocks % 16 == 0:
+        return span_body(*arrays)
+    return plain_body(*arrays)
+
+
 def solution(mesh):
     placed = (
         P(("groups", "span", "sub"), None),

time: 400 us -> 175 us (0.44); the launches traced: 398 us -> 178 us
  waiting for transfers between devices: 236 us -> 97.4 us
  local copies, waits for them, and re-layouts: 58 us -> 5 us
  matrix products: 39.8 us -> 0 us
  Pallas kernels: 0 us -> 33.7 us
  other arithmetic: 25.3 us -> 2.84 us
  starting transfers between devices: 23 us -> 36.7 us
  between operations: 15.1 us -> 1.87 us
    all_to_all x4 -> x1, waiting for transfers between devices: 213 us -> 23.1 us  [raise_level(): lax.all_to_all(parts, 'span', split_axis=0, concat_axis=0, tiled=True)]
    ppermute x0 -> x21, waiting for transfers between devices: none -> 74.3 us  [the longest x15 72.9 us: cross(): lax.ppermute(values, 'span', [(at, at ^ 1 << bit) for at in range(spans)])]
    dot_general x20 -> x0, matrix products: 39.8 us -> none  [the longest x18 31.2 us: fold_step(): jnp.einsum('cbr,brj->cbj', block_part, row_table, precision=lax.Precision...]
    pallas_call x0 -> x7, Pallas kernels: none -> 33.7 us  [the longest x5 29.8 us: fold_children(): pl.pallas_call(kernel, out_shape=(half, half), in_specs=[scalars, scalars...]
    ppermute x0 -> x21, starting transfers between devices: none -> 29.6 us  [the longest x15 28.7 us: cross(): lax.ppermute(values, 'span', [(at, at ^ 1 << bit) for at in range(spans)])]
    scatter x2 -> x0, local copies, waits for them, and re-layouts: 24.1 us -> none  [the longest x1 19.5 us: body(): jnp.zeros(outgoing_shape, jnp.float32).at[:, slot_index]]
    psum x2 -> x0, waiting for transfers between devices: 23 us -> none  [seam(): whole_sum = lax.psum(partial_value, 'sub')]
    dynamic_update_slice x18 -> x0, local copies, waits for them, and re-layouts: 18.4 us -> none  [fold_step(): return lax.dynamic_update_slice_in_dim(result, folded_part, start, 1)]
  transfers between devices with their start and end apart: 6 -> 22, of which waited for: 5 -> 12; matrix products, arithmetic and copies ran while one was open for 12% -> 1% of each run, Pallas kernels for 0% -> 12%
where the time goes in v2:
time: 175 us; the launch traced here: 178 us
  waiting for transfers between devices  97.4 us (56%)
  starting transfers between devices  36.7 us (21%)
  Pallas kernels  33.7 us (19%)
  local copies, waits for them, and re-layouts  5 us (3%)
  other arithmetic  2.84 us (2%)
  between operations  1.87 us (1%)
    ppermute x15, waiting for transfers between devices, cross(): lax.ppermute(values, 'span', [(at, at ^ 1 << bit) for at in range(spans)])  72.9 us
    pallas_call x5, Pallas kernels, fold_children(): pl.pallas_call(kernel, out_shape=(half, half), in_specs=[scalars, scalars...  29.8 us
    ppermute x15, starting transfers between devices, cross(): lax.ppermute(values, 'span', [(at, at ^ 1 << bit) for at in range(spans)])  28.7 us
    all_to_all x1, waiting for transfers between devices, raise_level(): lax.all_to_all(parts, 'span', split_axis=0, concat_axis=0, tiled=True)  23.1 us
    all_to_all x1, starting transfers between devices, raise_level(): lax.all_to_all(parts, 'span', split_axis=0, concat_axis=0, tiled=True)  7.13 us
    unnamed x34, local copies, waits for them, and re-layouts  4.59 us
  transfers between devices with their start and end apart: 22, of which 12 were waited for; matrix products, arithmetic and copies ran while one was open for 1% of the time, Pallas kernels for 12%

profile of v2, /device:TPU:0, one launch (start us, length us, event | category | flops | bytes accessed | tf_op | source)
XLA Modules:
  0.0 177.5 jit_solution(6154143258544089023)
XLA Ops:
  1.3 1.2 fusion.14.refs_0_
  2.5 7.8 %fold_children.5 = (f32[320,8,128]{2,1,0:T(8,128)}, f32[320,8,128]{2,1,0:T(8,128)}) custom-call(s32[128]{0:T(128)} %fusion.14.refs_0_, s32[1]{0:T(128)S(6)} %copy.57.refs_1_, s32[128,128]{1,0:T(8,128)} %refs_2_.10, f32[128,128]{1,0:T(8,128)} %refs_3_.9, f32[3,128,128]{2,1,0:T(8,128)} %refs_4_.5, f32[6,128,128]{2,1,0:T(8,128)} %refs_5_.1), custom_call_target="tpu_custom_call" | custom-call | flops 1024 | bytes 1024 | tf_op jit(solution)/shard_map/fold_children/pallas_call | solution.py:316
  10.4 1.4 copy-done
  11.8 0.8 copy-done.1
  12.6 0.8 copy-done.2
  13.4 0.7 copy-done.4
  14.1 5.7 %fold_children.6 = (f32[512,8,128]{2,1,0:T(8,128)S(1)}, f32[512,8,128]{2,1,0:T(8,128)S(1)}) custom-call(s32[128]{0:T(128)S(1)} %copy-done.4, s32[1]{0:T(128)S(6)} %copy.57.refs_1_, s32[128,128]{1,0:T(8,128)S(1)} %copy-done.1, f32[128,128]{1,0:T(8,128)S(1)} %copy-done.2, bf16[48,128,128]{2,1,0:T(8,128)(2,1)S(1)} %copy-done), custom_call_target="tpu_custom_call" | custom-call | flops 1024 | bytes 1024 | tf_op jit(solution)/shard_map/fold_children/pallas_call | solution.py:316
  19.8 0.1 collective-permute-start.3
  20.0 5.7 %fold_children.7 = (f32[512,8,128]{2,1,0:T(8,128)S(1)}, f32[512,8,128]{2,1,0:T(8,128)S(1)}) custom-call(s32[128]{0:T(128)S(1)} %copy-done.4, s32[1]{0:T(128)S(6)} %copy.57.refs_1_, s32[128,128]{1,0:T(8,128)S(1)} %copy-done.1, f32[128,128]{1,0:T(8,128)S(1)} %copy-done.2, bf16[48,128,128]{2,1,0:T(8,128)(2,1)S(1)} %copy-done), custom_call_target="tpu_custom_call" | custom-call | flops 1024 | bytes 1024 | tf_op jit(solution)/shard_map/fold_children/pallas_call | solution.py:316
  25.7 2.9 %collective-permute-start.1 = (f32[160,8,128]{2,1,0:T(8,128)S(1)}, f32[160,8,128]{2,1,0:T(8,128)S(1)}, u32[]{:S(2)}, u32[]{:S(2)}) collective-permute-start(f32[160,8,128]{2,1,0:T(8,128)S(1)} %slice_add_fusion.2), channel_id=1, source_target_pairs={{0,2},{2,0},{4,6},{6,4},{8,10},{10,8},{12,14},{14,12},{1,3},{3,1},... | collective-permute-start | bytes 1966088 | tf_op jit(solution)/shard_map/ppermute | solution.py:520
  28.6 0.1 slice_add_fusion
  28.8 5.3 %fold_children.8 = (f32[256,8,128]{2,1,0:T(8,128)S(1)}, f32[256,8,128]{2,1,0:T(8,128)S(1)}) custom-call(s32[128]{0:T(128)S(1)} %copy-done.4, s32[1]{0:T(128)S(6)} %copy.57.refs_1_, s32[128,128]{1,0:T(8,128)S(1)} %copy-done.1, f32[128,128]{1,0:T(8,128)S(1)} %copy-done.2, bf16[48,128,128]{2,1,0:T(8,128)(2,1)S(1)} %copy-done), custom_call_target="tpu_custom_call" | custom-call | flops 1024 | bytes 1024 | tf_op jit(solution)/shard_map/fold_children/pallas_call | solution.py:316
  34.1 5.3 %fold_children.9 = (f32[256,8,128]{2,1,0:T(8,128)S(1)}, f32[256,8,128]{2,1,0:T(8,128)S(1)}) custom-call(s32[128]{0:T(128)S(1)} %copy-done.4, s32[1]{0:T(128)S(6)} %copy.57.refs_1_, s32[128,128]{1,0:T(8,128)S(1)} %copy-done.1, f32[128,128]{1,0:T(8,128)S(1)} %copy-done.2, bf16[48,128,128]{2,1,0:T(8,128)(2,1)S(1)} %copy-done), custom_call_target="tpu_custom_call" | custom-call | flops 1024 | bytes 1024 | tf_op jit(solution)/shard_map/fold_children/pallas_call | solution.py:316
  39.5 0.5 collective-permute-start.6
  40.0 4.2 %collective-permute-done.1 = f32[160,8,128]{2,1,0:T(8,128)S(1)} collective-permute-done((f32[160,8,128]{2,1,0:T(8,128)S(1)}, f32[160,8,128]{2,1,0:T(8,128)S(1)}, u32[]{:S(2)}, u32[]{:S(2)}) %collective-permute-start.1) | collective-permute-done | bytes 655392 | tf_op jit(solution)/shard_map/ppermute | solution.py:520
  44.2 0.1 slice_add_fusion.1
  44.4 2.3 %collective-permute-start.5 = (f32[80,8,128]{2,1,0:T(8,128)S(1)}, f32[80,8,128]{2,1,0:T(8,128)S(1)}, u32[]{:S(2)}, u32[]{:S(2)}) collective-permute-start(f32[80,8,128]{2,1,0:T(8,128)S(1)} %slice_add_fusion.9), channel_id=1, source_target_pairs={{0,4},{2,6},{4,0},{6,2},{8,12},{10,14},{12,8},{14,10},{1,5},{3,7},... | collective-permute-start | bytes 983048 | tf_op jit(solution)/shard_map/ppermute | solution.py:520
  46.7 19.4 %collective-permute-done.7 = f32[256,8,128]{2,1,0:T(8,128)S(1)} collective-permute-done((f32[256,8,128]{2,1,0:T(8,128)S(1)}, f32[256,8,128]{2,1,0:T(8,128)S(1)}, u32[]{:S(2)}, u32[]{:S(2)}) %collective-permute-start.7) | collective-permute-done | bytes 1048608 | tf_op jit(solution)/shard_map/ppermute | solution.py:520
  66.1 0.1 slice_add_fusion.6
  66.2 1.8 %collective-permute-start.10 = (f32[256,8,128]{2,1,0:T(8,128)S(1)}, f32[256,8,128]{2,1,0:T(8,128)S(1)}, u32[]{:S(2)}, u32[]{:S(2)}) collective-permute-start(f32[256,8,128]{2,1,0:T(8,128)S(1)} %slice_add_fusion.1), channel_id=1, source_target_pairs={{0,2},{2,0},{4,6},{6,4},{8,10},{10,8},{12,14},{14,12},{1,3},{3,1},... | collective-permute-start | bytes 3145736 | tf_op jit(solution)/shard_map/ppermute | solution.py:520
  68.0 0.9 collective-permute-start.9
  68.9 0.2 convert_reduce_fusion
  69.2 4.3 %collective-permute-start.8 = (f32[40,8,128]{2,1,0:T(8,128)S(1)}, f32[40,8,128]{2,1,0:T(8,128)S(1)}, u32[]{:S(2)}, u32[]{:S(2)}) collective-permute-start(f32[40,8,128]{2,1,0:T(8,128)S(1)} %slice_add_fusion.27), channel_id=1, source_target_pairs={{0,8},{2,10},{4,12},{6,14},{8,0},{10,2},{12,4},{14,6},{1,9},{3,11}... | collective-permute-start | bytes 491528 | tf_op jit(solution)/shard_map/ppermute | solution.py:520
  73.5 0.3 collective-permute-start.13
  73.8 10.6 %collective-permute-done.9 = f32[128,8,128]{2,1,0:T(8,128)S(1)} collective-permute-done((f32[128,8,128]{2,1,0:T(8,128)S(1)}, f32[128,8,128]{2,1,0:T(8,128)S(1)}, u32[]{:S(2)}, u32[]{:S(2)}) %collective-permute-start.9) | collective-permute-done | bytes 524320 | tf_op jit(solution)/shard_map/ppermute | solution.py:520
  84.4 7.9 %collective-permute-done.10 = f32[256,8,128]{2,1,0:T(8,128)S(1)} collective-permute-done((f32[256,8,128]{2,1,0:T(8,128)S(1)}, f32[256,8,128]{2,1,0:T(8,128)S(1)}, u32[]{:S(2)}, u32[]{:S(2)}) %collective-permute-start.10) | collective-permute-done | bytes 1048608 | tf_op jit(solution)/shard_map/ppermute | solution.py:520
  92.3 0.1 slice_add_fusion.3
  92.4 2.4 %collective-permute-start.12 = (f32[128,8,128]{2,1,0:T(8,128)S(1)}, f32[128,8,128]{2,1,0:T(8,128)S(1)}, u32[]{:S(2)}, u32[]{:S(2)}) collective-permute-start(f32[128,8,128]{2,1,0:T(8,128)S(1)} %slice_add_fusion.3), channel_id=1, source_target_pairs={{0,4},{2,6},{4,0},{6,2},{8,12},{10,14},{12,8},{14,10},{1,5},{3,7},... | collective-permute-start | bytes 1572872 | tf_op jit(solution)/shard_map/ppermute | solution.py:520
  94.9 2.9 %collective-permute-start.11 = (f32[64,8,128]{2,1,0:T(8,128)S(1)}, f32[64,8,128]{2,1,0:T(8,128)S(1)}, u32[]{:S(2)}, u32[]{:S(2)}) collective-permute-start(f32[64,8,128]{2,1,0:T(8,128)S(1)} %slice_add_fusion.21), channel_id=1, source_target_pairs={{0,8},{2,10},{4,12},{6,14},{8,0},{10,2},{12,4},{14,6},{1,9},{3,11}... | collective-permute-start | bytes 786440 | tf_op jit(solution)/shard_map/ppermute | solution.py:520
  97.7 1.7 collective-permute-start.16
  99.5 4.1 %collective-permute-done.13 = f32[128,8,128]{2,1,0:T(8,128)S(1)} collective-permute-done((f32[128,8,128]{2,1,0:T(8,128)S(1)}, f32[128,8,128]{2,1,0:T(8,128)S(1)}, u32[]{:S(2)}, u32[]{:S(2)}) %collective-permute-start.13) | collective-permute-done | bytes 524320 | tf_op jit(solution)/shard_map/ppermute | solution.py:520
  103.6 6.3 %collective-permute-done.12 = f32[128,8,128]{2,1,0:T(8,128)S(1)} collective-permute-done((f32[128,8,128]{2,1,0:T(8,128)S(1)}, f32[128,8,128]{2,1,0:T(8,128)S(1)}, u32[]{:S(2)}, u32[]{:S(2)}) %collective-permute-start.12) | collective-permute-done | bytes 524320 | tf_op jit(solution)/shard_map/ppermute | solution.py:520
  110.0 3.0 %collective-permute-start.15 = (f32[64,8,128]{2,1,0:T(8,128)S(1)}, f32[64,8,128]{2,1,0:T(8,128)S(1)}, u32[]{:S(2)}, u32[]{:S(2)}) collective-permute-start(f32[64,8,128]{2,1,0:T(8,128)S(1)} %slice_add_fusion.16), channel_id=1, source_target_pairs={{0,4},{2,6},{4,0},{6,2},{8,12},{10,14},{12,8},{14,10},{1,5},{3,7},... | collective-permute-start | bytes 786440 | tf_op jit(solution)/shard_map/ppermute | solution.py:520
  113.0 1.6 collective-permute-start.14
  114.7 6.6 %collective-permute-done.15 = f32[64,8,128]{2,1,0:T(8,128)S(1)} collective-permute-done((f32[64,8,128]{2,1,0:T(8,128)S(1)}, f32[64,8,128]{2,1,0:T(8,128)S(1)}, u32[]{:S(2)}, u32[]{:S(2)}) %collective-permute-start.15) | collective-permute-done | bytes 262176 | tf_op jit(solution)/shard_map/ppermute | solution.py:520
  121.3 4.4 %collective-permute-done.14 = f32[64,8,128]{2,1,0:T(8,128)S(1)} collective-permute-done((f32[64,8,128]{2,1,0:T(8,128)S(1)}, f32[64,8,128]{2,1,0:T(8,128)S(1)}, u32[]{:S(2)}, u32[]{:S(2)}) %collective-permute-start.14) | collective-permute-done | bytes 262176 | tf_op jit(solution)/shard_map/ppermute | solution.py:520
  125.9 2.3 %collective-permute-start.17 = (f32[32,8,128]{2,1,0:T(8,128)S(1)}, f32[32,8,128]{2,1,0:T(8,128)S(1)}, u32[]{:S(2)}, u32[]{:S(2)}) collective-permute-start(f32[32,8,128]{2,1,0:T(8,128)S(1)} %slice_add_fusion.39), channel_id=1, source_target_pairs={{0,8},{2,10},{4,12},{6,14},{8,0},{10,2},{12,4},{14,6},{1,9},{3,11}... | collective-permute-start | bytes 393224 | tf_op jit(solution)/shard_map/ppermute | solution.py:520
  128.2 5.3 %collective-permute-done.18 = f32[64,8,128]{2,1,0:T(8,128)S(1)} collective-permute-done((f32[64,8,128]{2,1,0:T(8,128)S(1)}, f32[64,8,128]{2,1,0:T(8,128)S(1)}, u32[]{:S(2)}, u32[]{:S(2)}) %collective-permute-start.18) | collective-permute-done | bytes 262176 | tf_op jit(solution)/shard_map/ppermute | solution.py:520
  133.6 2.2 %collective-permute-start.19 = (f32[32,8,128]{2,1,0:T(8,128)S(1)}, f32[32,8,128]{2,1,0:T(8,128)S(1)}, u32[]{:S(2)}, u32[]{:S(2)}) collective-permute-start(f32[32,8,128]{2,1,0:T(8,128)S(1)} %slice_add_fusion.33), channel_id=1, source_target_pairs={{0,8},{2,10},{4,12},{6,14},{8,0},{10,2},{12,4},{14,6},{1,9},{3,11}... | collective-permute-start | bytes 393224 | tf_op jit(solution)/shard_map/ppermute | solution.py:520
  135.9 4.1 %collective-permute-done.19 = f32[32,8,128]{2,1,0:T(8,128)S(1)} collective-permute-done((f32[32,8,128]{2,1,0:T(8,128)S(1)}, f32[32,8,128]{2,1,0:T(8,128)S(1)}, u32[]{:S(2)}, u32[]{:S(2)}) %collective-permute-start.19) | collective-permute-done | bytes 131104 | tf_op jit(solution)/shard_map/ppermute | solution.py:520
  139.9 0.1 bitcast_divide_fusion.2
  140.1 2.5 %fold_parents.1 = f32[240,8,128]{2,1,0:T(8,128)} custom-call(s32[32]{0:T(128)S(1)} %multiply_add_fusion.refs_0_, s32[32]{0:T(128)S(1)} %copy-done.6, s32[32,128]{1,0:T(8,128)S(1)} %copy-done.5, f32[40,8,128]{2,1,0:T(8,128)S(1)} %fusion.2.refs_3_, f32[64,8,128]{2,1,0:T(8,128)S(1)} %fusion.1.refs_4_, f32[64,8,128]{2,1,0:T(8,128)S(1)} %fusion.refs_5_, ...), custom_call_target="tpu_custom_call" | custom-call | flops 1024 | bytes 1024 | tf_op jit(solution)/shard_map/fold_parents/pallas_call | solution.py:384
  142.6 7.1 %all-to-all-start = ((f32[240,8,128]{2,1,0:T(8,128)}), f32[240,8,128]{2,1,0:T(8,128)S(1)}, u32[]{:S(2)}, u32[]{:S(2)}) async-start(f32[240,8,128]{2,1,0:T(8,128)} %fold_parents.1), calls=%async_computation | async-start | bytes 1966080 | tf_op jit(solution)/shard_map/all_to_all | solution.py:586
  149.8 0.2 stack.4
  150.3 23.1 %all-to-all-done.refs_1_ = f32[240,8,128]{2,1,0:T(8,128)S(1)} async-done(((f32[240,8,128]{2,1,0:T(8,128)}), f32[240,8,128]{2,1,0:T(8,128)S(1)}, u32[]{:S(2)}, u32[]{:S(2)}) %all-to-all-start) | async-done | bytes 983072 | tf_op jit(solution)/shard_map/all_to_all | solution.py:586
  173.4 1.4 place_parents.1
  175.0 1.4 collective-permute-done.20
  176.8 0.7 copy-done.9
  (85 shorter events, 1.8 us)
Async XLA Ops:
  10.3 9.6 %collective-permute-start = (f32[320,8,128]{2,1,0:T(8,128)}, f32[320,8,128]{2,1,0:T(8,128)S(1)}, u32[]{:S(2)}, u32[]{:S(2)}) collective-permute-start(f32[320,8,128]{2,1,0:T(8,128)} %get-tuple-element.32), channel_id=1, source_target_pairs={{0,1},{1,0},{2,3},{3,2},{4,5},{5,4},{6,7},{7,6},{8,9},{9,8},{10,11... | collective-permute-start | bytes 3932168 | tf_op jit(solution)/shard_map/ppermute | solution.py:517
  10.3 1.4 copy-start
  11.8 0.8 copy-start.1
  12.6 0.8 copy-start.2
  13.4 0.7 copy-start.4
  14.1 5.8 %copy-start.7 = (f32[320,8,128]{2,1,0:T(8,128)S(1)}, f32[320,8,128]{2,1,0:T(8,128)}, u32[]{:S(2)}) copy-start(f32[320,8,128]{2,1,0:T(8,128)} %get-tuple-element.31) | copy-start | bytes 3932164
  19.8 8.9 %collective-permute-start.3 = (f32[512,8,128]{2,1,0:T(8,128)S(1)}, f32[512,8,128]{2,1,0:T(8,128)S(1)}, u32[]{:S(2)}, u32[]{:S(2)}) collective-permute-start(f32[512,8,128]{2,1,0:T(8,128)S(1)} %get-tuple-element.38), channel_id=1, source_target_pairs={{0,1},{1,0},{2,3},{3,2},{4,5},{5,4},{6,7},{7,6},{8,9},{9,8},{10,11... | collective-permute-start | bytes 6291464 | tf_op jit(solution)/shard_map/ppermute | solution.py:517
  25.7 18.6 %collective-permute-start.2 = (f32[512,8,128]{2,1,0:T(8,128)S(1)}, f32[512,8,128]{2,1,0:T(8,128)S(1)}, u32[]{:S(2)}, u32[]{:S(2)}) collective-permute-start(f32[512,8,128]{2,1,0:T(8,128)S(1)} %get-tuple-element.37), channel_id=1, source_target_pairs={{0,1},{1,0},{2,3},{3,2},{4,5},{5,4},{6,7},{7,6},{8,9},{9,8},{10,11... | collective-permute-start | bytes 6291464 | tf_op jit(solution)/shard_map/ppermute | solution.py:517
  25.7 18.4 %collective-permute-start.1 = (f32[160,8,128]{2,1,0:T(8,128)S(1)}, f32[160,8,128]{2,1,0:T(8,128)S(1)}, u32[]{:S(2)}, u32[]{:S(2)}) collective-permute-start(f32[160,8,128]{2,1,0:T(8,128)S(1)} %slice_add_fusion.2), channel_id=1, source_target_pairs={{0,2},{2,0},{4,6},{6,4},{8,10},{10,8},{12,14},{14,12},{1,3},{3,1},... | collective-permute-start | bytes 1966088 | tf_op jit(solution)/shard_map/ppermute | solution.py:520
  39.4 5.0 %collective-permute-start.4 = (f32[256,8,128]{2,1,0:T(8,128)S(1)}, f32[256,8,128]{2,1,0:T(8,128)S(1)}, u32[]{:S(2)}, u32[]{:S(2)}) collective-permute-start(f32[256,8,128]{2,1,0:T(8,128)S(1)} %get-tuple-element.42), channel_id=1, source_target_pairs={{0,1},{1,0},{2,3},{3,2},{4,5},{5,4},{6,7},{7,6},{8,9},{9,8},{10,11... | collective-permute-start | bytes 3145736 | tf_op jit(solution)/shard_map/ppermute | solution.py:517
  39.5 7.2 %collective-permute-start.6 = (f32[256,8,128]{2,1,0:T(8,128)S(1)}, f32[256,8,128]{2,1,0:T(8,128)S(1)}, u32[]{:S(2)}, u32[]{:S(2)}) collective-permute-start(f32[256,8,128]{2,1,0:T(8,128)S(1)} %get-tuple-element.44), channel_id=1, source_target_pairs={{0,1},{1,0},{2,3},{3,2},{4,5},{5,4},{6,7},{7,6},{8,9},{9,8},{10,11... | collective-permute-start | bytes 3145736 | tf_op jit(solution)/shard_map/ppermute | solution.py:517
  40.0 26.1 %collective-permute-start.7 = (f32[256,8,128]{2,1,0:T(8,128)S(1)}, f32[256,8,128]{2,1,0:T(8,128)S(1)}, u32[]{:S(2)}, u32[]{:S(2)}) collective-permute-start(f32[256,8,128]{2,1,0:T(8,128)S(1)} %slice_add_fusion), channel_id=1, source_target_pairs={{0,2},{2,0},{4,6},{6,4},{8,10},{10,8},{12,14},{14,12},{1,3},{3,1},... | collective-permute-start | bytes 3145736 | tf_op jit(solution)/shard_map/ppermute | solution.py:520
  44.3 24.6 %copy-start.10 = (s32[32]{0:T(128)S(1)}, s32[32]{0:T(128)}, u32[]{:S(2)}) copy-start(s32[32]{0:T(128)} %param.19) | copy-start | bytes 388
  44.4 23.6 %collective-permute-start.5 = (f32[80,8,128]{2,1,0:T(8,128)S(1)}, f32[80,8,128]{2,1,0:T(8,128)S(1)}, u32[]{:S(2)}, u32[]{:S(2)}) collective-permute-start(f32[80,8,128]{2,1,0:T(8,128)S(1)} %slice_add_fusion.9), channel_id=1, source_target_pairs={{0,4},{2,6},{4,0},{6,2},{8,12},{10,14},{12,8},{14,10},{1,5},{3,7},... | collective-permute-start | bytes 983048 | tf_op jit(solution)/shard_map/ppermute | solution.py:520
  66.2 26.1 %collective-permute-start.10 = (f32[256,8,128]{2,1,0:T(8,128)S(1)}, f32[256,8,128]{2,1,0:T(8,128)S(1)}, u32[]{:S(2)}, u32[]{:S(2)}) collective-permute-start(f32[256,8,128]{2,1,0:T(8,128)S(1)} %slice_add_fusion.1), channel_id=1, source_target_pairs={{0,2},{2,0},{4,6},{6,4},{8,10},{10,8},{12,14},{14,12},{1,3},{3,1},... | collective-permute-start | bytes 3145736 | tf_op jit(solution)/shard_map/ppermute | solution.py:520
  68.0 16.4 %collective-permute-start.9 = (f32[128,8,128]{2,1,0:T(8,128)S(1)}, f32[128,8,128]{2,1,0:T(8,128)S(1)}, u32[]{:S(2)}, u32[]{:S(2)}) collective-permute-start(f32[128,8,128]{2,1,0:T(8,128)S(1)} %slice_add_fusion.6), channel_id=1, source_target_pairs={{0,4},{2,6},{4,0},{6,2},{8,12},{10,14},{12,8},{14,10},{1,5},{3,7},... | collective-permute-start | bytes 1572872 | tf_op jit(solution)/shard_map/ppermute | solution.py:520
  69.2 23.2 %collective-permute-start.8 = (f32[40,8,128]{2,1,0:T(8,128)S(1)}, f32[40,8,128]{2,1,0:T(8,128)S(1)}, u32[]{:S(2)}, u32[]{:S(2)}) collective-permute-start(f32[40,8,128]{2,1,0:T(8,128)S(1)} %slice_add_fusion.27), channel_id=1, source_target_pairs={{0,8},{2,10},{4,12},{6,14},{8,0},{10,2},{12,4},{14,6},{1,9},{3,11}... | collective-permute-start | bytes 491528 | tf_op jit(solution)/shard_map/ppermute | solution.py:520
  73.5 30.0 %collective-permute-start.13 = (f32[128,8,128]{2,1,0:T(8,128)S(1)}, f32[128,8,128]{2,1,0:T(8,128)S(1)}, u32[]{:S(2)}, u32[]{:S(2)}) collective-permute-start(f32[128,8,128]{2,1,0:T(8,128)S(1)} %slice_add_fusion.8), channel_id=1, source_target_pairs={{0,2},{2,0},{4,6},{6,4},{8,10},{10,8},{12,14},{14,12},{1,3},{3,1},... | collective-permute-start | bytes 1572872 | tf_op jit(solution)/shard_map/ppermute | solution.py:520
  92.4 17.5 %collective-permute-start.12 = (f32[128,8,128]{2,1,0:T(8,128)S(1)}, f32[128,8,128]{2,1,0:T(8,128)S(1)}, u32[]{:S(2)}, u32[]{:S(2)}) collective-permute-start(f32[128,8,128]{2,1,0:T(8,128)S(1)} %slice_add_fusion.3), channel_id=1, source_target_pairs={{0,4},{2,6},{4,0},{6,2},{8,12},{10,14},{12,8},{14,10},{1,5},{3,7},... | collective-permute-start | bytes 1572872 | tf_op jit(solution)/shard_map/ppermute | solution.py:520
  94.8 45.2 %copy-start.3 = (f32[40,8,128]{2,1,0:T(8,128)}, f32[40,8,128]{2,1,0:T(8,128)S(1)}, u32[]{:S(2)}) copy-start(f32[40,8,128]{2,1,0:T(8,128)S(1)} %fusion.2.refs_3_) | copy-start | bytes 491524
  94.9 15.1 %collective-permute-start.11 = (f32[64,8,128]{2,1,0:T(8,128)S(1)}, f32[64,8,128]{2,1,0:T(8,128)S(1)}, u32[]{:S(2)}, u32[]{:S(2)}) collective-permute-start(f32[64,8,128]{2,1,0:T(8,128)S(1)} %slice_add_fusion.21), channel_id=1, source_target_pairs={{0,8},{2,10},{4,12},{6,14},{8,0},{10,2},{12,4},{14,6},{1,9},{3,11}... | collective-permute-start | bytes 786440 | tf_op jit(solution)/shard_map/ppermute | solution.py:520
  97.7 16.9 %collective-permute-start.16 = (f32[128,8,128]{2,1,0:T(8,128)S(1)}, f32[128,8,128]{2,1,0:T(8,128)S(1)}, u32[]{:S(2)}, u32[]{:S(2)}) collective-permute-start(f32[128,8,128]{2,1,0:T(8,128)S(1)} %slice_add_fusion.5), channel_id=1, source_target_pairs={{0,2},{2,0},{4,6},{6,4},{8,10},{10,8},{12,14},{14,12},{1,3},{3,1},... | collective-permute-start | bytes 1572872 | tf_op jit(solution)/shard_map/ppermute | solution.py:520
  110.0 11.3 %collective-permute-start.15 = (f32[64,8,128]{2,1,0:T(8,128)S(1)}, f32[64,8,128]{2,1,0:T(8,128)S(1)}, u32[]{:S(2)}, u32[]{:S(2)}) collective-permute-start(f32[64,8,128]{2,1,0:T(8,128)S(1)} %slice_add_fusion.16), channel_id=1, source_target_pairs={{0,4},{2,6},{4,0},{6,2},{8,12},{10,14},{12,8},{14,10},{1,5},{3,7},... | collective-permute-start | bytes 786440 | tf_op jit(solution)/shard_map/ppermute | solution.py:520
  113.0 12.7 %collective-permute-start.14 = (f32[64,8,128]{2,1,0:T(8,128)S(1)}, f32[64,8,128]{2,1,0:T(8,128)S(1)}, u32[]{:S(2)}, u32[]{:S(2)}) collective-permute-start(f32[64,8,128]{2,1,0:T(8,128)S(1)} %slice_add_fusion.13), channel_id=1, source_target_pairs={{0,8},{2,10},{4,12},{6,14},{8,0},{10,2},{12,4},{14,6},{1,9},{3,11}... | collective-permute-start | bytes 786440 | tf_op jit(solution)/shard_map/ppermute | solution.py:520
  125.8 7.8 %collective-permute-start.18 = (f32[64,8,128]{2,1,0:T(8,128)S(1)}, f32[64,8,128]{2,1,0:T(8,128)S(1)}, u32[]{:S(2)}, u32[]{:S(2)}) collective-permute-start(f32[64,8,128]{2,1,0:T(8,128)S(1)} %slice_add_fusion.11), channel_id=1, source_target_pairs={{0,4},{2,6},{4,0},{6,2},{8,12},{10,14},{12,8},{14,10},{1,5},{3,7},... | collective-permute-start | bytes 786440 | tf_op jit(solution)/shard_map/ppermute | solution.py:520
  125.8 14.2 %copy-start.5 = (s32[32,128]{1,0:T(8,128)S(1)}, s32[32,128]{1,0:T(8,128)}, u32[]{:S(2)}) copy-start(s32[32,128]{1,0:T(8,128)} %refs_2_.11) | copy-start | bytes 49156
  125.8 14.2 %copy-start.6 = (s32[32]{0:T(128)S(1)}, s32[32]{0:T(128)}, u32[]{:S(2)}) copy-start(s32[32]{0:T(128)} %refs_1_.6) | copy-start | bytes 388
  125.9 7.7 %collective-permute-start.17 = (f32[32,8,128]{2,1,0:T(8,128)S(1)}, f32[32,8,128]{2,1,0:T(8,128)S(1)}, u32[]{:S(2)}, u32[]{:S(2)}) collective-permute-start(f32[32,8,128]{2,1,0:T(8,128)S(1)} %slice_add_fusion.39), channel_id=1, source_target_pairs={{0,8},{2,10},{4,12},{6,14},{8,0},{10,2},{12,4},{14,6},{1,9},{3,11}... | collective-permute-start | bytes 393224 | tf_op jit(solution)/shard_map/ppermute | solution.py:520
  133.6 6.4 %collective-permute-start.19 = (f32[32,8,128]{2,1,0:T(8,128)S(1)}, f32[32,8,128]{2,1,0:T(8,128)S(1)}, u32[]{:S(2)}, u32[]{:S(2)}) collective-permute-start(f32[32,8,128]{2,1,0:T(8,128)S(1)} %slice_add_fusion.33), channel_id=1, source_target_pairs={{0,8},{2,10},{4,12},{6,14},{8,0},{10,2},{12,4},{14,6},{1,9},{3,11}... | collective-permute-start | bytes 393224 | tf_op jit(solution)/shard_map/ppermute | solution.py:520
  142.6 7.4 %slice-start = ((f32[40,8,128]{2,1,0:T(8,128)}), f32[8,8,128]{2,1,0:T(8,128)S(1)}, s32[]{:S(2)}) async-start(f32[40,8,128]{2,1,0:T(8,128)} %copy-done.3), calls=%async_computation.1 | async-start | bytes 65536 | tf_op jit(solution)/shard_map/slice | solution.py:466
  142.6 30.9 %all-to-all-start = ((f32[240,8,128]{2,1,0:T(8,128)}), f32[240,8,128]{2,1,0:T(8,128)S(1)}, u32[]{:S(2)}, u32[]{:S(2)}) async-start(f32[240,8,128]{2,1,0:T(8,128)} %fold_parents.1), calls=%async_computation | async-start | bytes 1966080 | tf_op jit(solution)/shard_map/all_to_all | solution.py:586
  174.8 1.6 collective-permute-start.20
  175.0 1.8 %copy-start.8 = (f32[58,32,128]{2,1,0:T(8,128)}, f32[58,32,128]{2,1,0:T(8,128)S(1)}, u32[]{:S(2)}) copy-start(f32[58,32,128]{2,1,0:T(8,128)S(1)} %copy_dynamic-update-slice_fusion) | copy-start | bytes 2850820
  176.8 0.7 copy-start.9

commit v3 on v2

--- a/solution.py
+++ b/solution.py
@@ -155,9 +155,14 @@
 
 TILE = 8
 UNROLL = 8
-WIDTHS = (16, 16, 8, 8)
-GROUPS = {6: (0, 1, 2, 3, 4)}
-WAIT_FETCH = True
+WIDTHS = (8, 8, 8, 8, 8, 8)
+FOLDS = ((0,), (1, 2, 3), (4, 5, 6))
+GROUPS = {8: (0, 1, 2, 3, 4, 5, 6)}
+WAIT_FETCH = False
+LOOSE = -9
+EARLY_ONE = True
+PHASE0 = False
+TIES = 1
 HEAD = 1
 
 
@@ -197,18 +202,22 @@
     return sum((pltpu.roll(line, turn * extra, 0) for turn in range(1, share)), start=line)
 
 
-def child_kernel(first, width, regions, slots, *refs):
+def child_kernel(first, widths, regions, slots, *refs):
     geometry = first == 0
     place_ref, live_ref = refs[:2]
     count = 4 if geometry else 3
     sources = refs[2 : 2 + count]
-    keep_ref, send_ref = refs[2 + count : 4 + count]
-    targets = refs[4 + count : 4 + 2 * count]
+    refs = refs[2 + count :]
+    out_refs, refs = refs[: 2 * len(widths)], refs[2 * len(widths) :]
+    targets = refs[:count]
     rows_ref, weight_ref = targets[:2]
-    moments, totals, load_sems, out_sems = refs[4 + 2 * count :]
+    moments, totals, load_sems, out_sems = refs[count:]
     block_count, row_count = rows_ref.shape
+    width = sum(widths)
     full, extra = width // TILE, width % TILE
-    per_region = tile_count(width, slots)
+    sizes = [tile_count(part, slots) for part in widths]
+    starts = [2 * regions * sum(sizes[:at]) for at in range(len(sizes))]
+    tiles = [(at, tile) for at, part in enumerate(widths) for tile in range(part // TILE)]
     group = 16
     first_colour = max(first, 10) - 10
     colour_total = 0 if geometry else width
@@ -277,32 +286,42 @@
                 line = moments[pl.ds(full * TILE * block_count + block, TILE, stride=block_count), :]
                 lines.append(jnp.where(tile_rows() // extra == slot % (TILE // extra), line, 0.0))
             rows = jnp.where(block < live, rows_ref[pl.ds(block, 1), :], -1)
-            folded.append((region * per_region, slot, fold_block(jnp.concatenate(lines, 0), rows)))
-        for base, slot, result in folded:
-            for tile in range(full):
-                totals[base + tile * slots + slot] += result[tile * TILE : (tile + 1) * TILE]
+            folded.append((region, slot, fold_block(jnp.concatenate(lines, 0), rows)))
+        for region, slot, result in folded:
+            for line, (at, tile) in enumerate(tiles):
+                spot = starts[at] + region * sizes[at] + tile * slots + slot
+                totals[spot] += result[line * TILE : (line + 1) * TILE]
             if extra:
-                totals[base + full * slots + slot // (TILE // extra)] += result[full * TILE :]
+                spot = starts[-1] + region * sizes[-1] + (widths[-1] // TILE) * slots
+                totals[spot + slot // (TILE // extra)] += result[full * TILE :]
         return carry
 
     lax.fori_loop(0, (live + UNROLL - 1) // UNROLL, fold, 0)
-    half = regions * per_region
-    send = pltpu.make_async_copy(totals.at[pl.ds(half, half)], send_ref, out_sems.at[0])
-    keep = pltpu.make_async_copy(totals.at[pl.ds(0, half)], keep_ref, out_sems.at[1])
-    send.start()
-    keep.start()
-    send.wait()
-    keep.wait()
-
-
-def fold_children(place, live, arrays, first, width, regions, slots, vmem):
+    stores = []
+    for at, size in enumerate(sizes):
+        half = regions * size
+        for turn in (1, 0):
+            source = totals.at[pl.ds(starts[at] + turn * half, half)]
+            store = pltpu.make_async_copy(source, out_refs[2 * at + turn], out_sems.at[2 * at + turn])
+            store.start()
+            stores.append(store)
+    for store in stores:
+        store.wait()
+
+
+def fold_children(place, live, arrays, first, widths, regions, slots, vmem):
     rows, weight, mean, factor, colour = arrays
     geometry = first == 0
     used = [rows, weight, mean, factor] if geometry else [rows, weight, colour]
     block_count, row_count = rows.shape
-    per_region = tile_count(width, slots)
+    width = sum(widths)
+    sizes = [tile_count(part, slots) for part in widths]
     padded = width // TILE * TILE + (TILE if width % TILE else 0)
-    half = jax.ShapeDtypeStruct((regions * per_region, TILE, row_count), jnp.float32)
+    halves = [
+        jax.ShapeDtypeStruct((regions * size, TILE, row_count), jnp.float32)
+        for size in sizes
+        for _ in range(2)
+    ]
     scalars = pl.BlockSpec(memory_space=pltpu.SMEM)
     outside = pl.BlockSpec(memory_space=pl.ANY)
     targets = [
@@ -311,19 +330,19 @@
     ]
 
     def kernel(*refs):
-        child_kernel(first, width, regions, slots, *refs)
+        child_kernel(first, widths, regions, slots, *refs)
 
     return pl.pallas_call(
         kernel,
-        out_shape=(half, half),
+        out_shape=halves,
         in_specs=[scalars, scalars] + [outside] * len(used),
-        out_specs=(outside, outside),
+        out_specs=[outside] * len(halves),
         scratch_shapes=targets
         + [
             pltpu.VMEM((padded * block_count, row_count), jnp.float32),
-            pltpu.VMEM((2 * regions * per_region, TILE, row_count), jnp.float32),
+            pltpu.VMEM((2 * regions * sum(sizes), TILE, row_count), jnp.float32),
             pltpu.SemaphoreType.DMA((len(used),)),
-            pltpu.SemaphoreType.DMA((2,)),
+            pltpu.SemaphoreType.DMA((len(halves),)),
         ],
         compiler_params=pltpu.CompilerParams(vmem_limit_bytes=vmem * 1024 * 1024),
         cost_estimate=pl.CostEstimate(flops=1024, bytes_accessed=1024, transcendentals=0),
@@ -340,7 +359,7 @@
 def parent_kernel(widths, owners, cap, coded, *refs):
     place_ref, code_ref, rows_ref = refs[:3]
     sums_refs = refs[3 : 3 + len(widths)]
-    totals = refs[3 + len(widths)]
+    out_refs, totals = refs[3 + len(widths) : -1], refs[-1]
     block_count = rows_ref.shape[0]
     full, extra, used = group_sizes(widths, cap)
     per_owner = used + (1 if coded else 0)
@@ -370,6 +389,8 @@
                 totals[base + tile * cap + rank] += result[tile * TILE : (tile + 1) * TILE]
             if extra:
                 totals[base + full * cap] += result[full * TILE :]
+    for owner, out_ref in enumerate(out_refs):
+        out_ref[...] = totals[owner * per_owner : (owner + 1) * per_owner]
 
 
 def fold_parents(place, code, rows, sums, widths, owners, cap, coded):
@@ -383,9 +404,10 @@
 
     return pl.pallas_call(
         kernel,
-        out_shape=jax.ShapeDtypeStruct((owners * per_owner, TILE, row_count), jnp.float32),
+        out_shape=[jax.ShapeDtypeStruct((per_owner, TILE, row_count), jnp.float32)] * owners,
         in_specs=[scalars, scalars, whole] + [whole] * len(sums),
-        out_specs=whole,
+        out_specs=[whole] * owners,
+        scratch_shapes=[pltpu.VMEM((owners * per_owner, TILE, row_count), jnp.float32)],
         compiler_params=pltpu.CompilerParams(vmem_limit_bytes=16 * 1024 * 1024),
         cost_estimate=pl.CostEstimate(flops=1024, bytes_accessed=1024, transcendentals=0),
         name="fold_parents",
@@ -393,35 +415,33 @@
 
 
 def place_kernel(widths, owners, cap, slots, coded, *refs):
-    if coded:
-        sub_ref, in_ref, keep_ref, send_ref, codes_ref = refs
-    else:
-        codes_in, in_ref, keep_ref, send_ref = refs
+    first_ref, in_refs, out_refs = refs[0], refs[1 : 1 + owners], refs[1 + owners :]
+    keep_ref, send_ref = out_refs[:2]
+    shape = in_refs[0].shape[1:]
     full, extra, used = group_sizes(widths, cap)
-    per_owner = used + (1 if coded else 0)
     if coded:
         for owner in range(owners):
-            code = in_ref[owner * per_owner + used].astype(jnp.int32)
-            codes_ref[owner] = (code // slots + sub_ref[0]) % 2 * slots + code % slots
-        codes_in = codes_ref
+            code = in_refs[owner][used].astype(jnp.int32)
+            out_refs[2][owner] = (code // slots + first_ref[0]) % 2 * slots + code % slots
+    codes_in = out_refs[2] if coded else first_ref
     for half, out_ref in enumerate((keep_ref, send_ref)):
         for slot in range(slots):
             label = half * slots + slot
-            sums = [jnp.zeros(in_ref.shape[1:], jnp.float32) for _ in range(full)]
+            sums = [jnp.zeros(shape, jnp.float32) for _ in range(full)]
             for owner in range(owners):
                 for rank in range(cap):
                     here = codes_in[owner, rank : rank + 1, :] == label
                     for tile in range(full):
-                        line = in_ref[owner * per_owner + tile * cap + rank]
+                        line = in_refs[owner][tile * cap + rank]
                         sums[tile] += jnp.where(here, line, 0.0)
             for tile in range(full):
                 out_ref[tile * slots + slot] = sums[tile]
         if extra:
             share = TILE // extra
-            sums = [jnp.zeros(in_ref.shape[1:], jnp.float32) for _ in range(slots // share)]
+            sums = [jnp.zeros(shape, jnp.float32) for _ in range(slots // share)]
             for owner in range(owners):
                 for rank in range(cap):
-                    line = spread_group(in_ref[owner * per_owner + full * cap], extra, rank)
+                    line = spread_group(in_refs[owner][full * cap], extra, rank)
                     code = codes_in[owner, rank : rank + 1, :] - half * slots - tile_rows() // extra
                     for tile in range(slots // share):
                         sums[tile] += jnp.where(code == tile * share, line, 0.0)
@@ -430,7 +450,7 @@
 
 
 def place_parents(sub_at, codes, received, widths, owners, cap, slots):
-    row_count = received.shape[2]
+    row_count = received[0].shape[2]
     coded = codes is None
     full, extra, _ = group_sizes(widths, cap)
     per_half = full * slots + slots * extra // TILE
@@ -445,12 +465,12 @@
     return pl.pallas_call(
         kernel,
         out_shape=(half, half, table) if coded else (half, half),
-        in_specs=[scalars if coded else whole, whole],
+        in_specs=[scalars if coded else whole] + [whole] * owners,
         out_specs=(whole, whole, whole) if coded else (whole, whole),
         compiler_params=pltpu.CompilerParams(vmem_limit_bytes=16 * 1024 * 1024),
         cost_estimate=pl.CostEstimate(flops=1024, bytes_accessed=1024, transcendentals=0),
         name="place_parents",
-    )(sub_at.reshape(1) if coded else codes, received)
+    )(sub_at.reshape(1) if coded else codes, *received)
 
 
 def unpack(tiles, widths, slots):
@@ -526,7 +546,7 @@
         region = sum(((away >> bit) & 1) << (levels - 1 - at) for at, bit in enumerate(order))
         return (half * spans + region) * PB_DEV + child_slot % PB_DEV
 
-    place_two = parent_owner * cap_two + earlier_same(parent_owner)
+    place_two = (parent_owner ^ span_at) * cap_two + earlier_same(parent_owner)
 
     arrays = (child_row, child_weight, child_mean, child_factor, child_colour)
     chunks = cut_components(components)
@@ -536,12 +556,17 @@
     terms = [[] for _ in chunks]
     sends = [[] for _ in chunks]
 
-    def fold(at, *others):
-        place = place_in(orders[at])
+    def fold(group, *others):
+        place = place_in(orders[group[0]])
         if others:
             place = after(place, *others)
-        keep, send = fold_children(place, live_blocks, arrays, *chunks[at], spans, PB_DEV, 56 if at < HEAD else 40)
-        terms[at] = [keep, swap(send)]
+        widths = [chunks[at][1] for at in group]
+        vmem = 56 if group[0] < HEAD else 40
+        halves = fold_children(
+            place, live_blocks, arrays, chunks[group[0]][0], widths, spans, PB_DEV, vmem
+        )
+        for turn, at in enumerate(group):
+            terms[at] = [halves[2 * turn], swap(halves[2 * turn + 1])]
 
     def part(at, low, high):
         return sum(
@@ -569,7 +594,13 @@
         depart(at, level, send)
         return send
 
-    level_two, codes, fetched = [], [None], []
+    level_one, level_two, codes, fetched = [], [], [None], []
+
+    def unpack_one():
+        return [
+            unpack(sums[at], [width], PB_DEV)[0] for at, (_, width) in enumerate(chunks)
+        ]
+
 
     def raise_level(group, *others):
         widths = [chunks[at][1] for at in group]
@@ -583,20 +614,24 @@
             cap_two,
             codes[0] is None,
         )
-        parts = lax.all_to_all(parts, "span", split_axis=0, concat_axis=0, tiled=True)
-        fetched.append(parts)
+        parts = [
+            lax.ppermute(part, "span", [(at, at ^ away) for at in range(spans)]) if away else part
+            for away, part in enumerate(parts)
+        ]
+        fetched.append(parts[-1])
+        if EARLY_ONE and group[-1] == total - 1:
+            level_one.append(merged_parts(unpack_one()))
+            parts = [after(part, level_one[0]) for part in parts]
         placed = place_parents(sub_at, codes[0], parts, widths, spans, cap_two, GB_DEV)
         if codes[0] is None:
             codes[0] = placed[2]
         level_two.extend(unpack(placed[0] + swap(placed[1]), widths, GB_DEV))
 
-    fold(0)
-    fold(1, terms[0][0])
-    first_send = depart_alone(0, 0)
-    fold(2, terms[1][0], first_send)
-    second_send = depart_alone(1, 0)
-    for at in range(3, total):
-        fold(at, terms[at - 1][0], second_send)
+    fold(FOLDS[0])
+    fold(FOLDS[1], terms[FOLDS[0][0]][0])
+    ready_sends = [depart_alone(at, 0) for at in range(2)]
+    for turn in range(2, len(FOLDS)):
+        fold(FOLDS[turn], terms[FOLDS[turn - 1][0]][0], *ready_sends[: turn - 1 + TIES])
     sums = [None] * total
     for phase in range(total + levels - 2):
         moves, done = [], []
@@ -607,12 +642,13 @@
                 moves.append((phase - turn, turn + 1))
         if phase >= levels - 1:
             done.append(terms[phase - levels + 1][-1])
-        if phase == 0:
+        if phase == 0 and PHASE0:
             done.append(terms[total - 1][1])
         if WAIT_FETCH:
             done += fetched[-1:]
         ready = [send_of(at, level) for at, level in moves]
-        ready = lax.optimization_barrier(tuple(ready + done))[: len(ready)]
+        if phase < total - LOOSE:
+            ready = lax.optimization_barrier(tuple(ready + done))[: len(ready)]
         for (at, level), send in zip(moves, ready, strict=True):
             depart(at, level, send)
             if level == levels - 1:
@@ -620,10 +656,7 @@
         if phase in GROUPS:
             raise_level(GROUPS[phase], *ready)
     raise_level(GROUPS[total + levels - 2])
-    level_one = []
-    for at in range(total):
-        level_one += unpack(sums[at], [chunks[at][1]], PB_DEV)
-    return (merged_parts(level_one), merged_parts(level_two))
+    return (level_one[0] if level_one else merged_parts(unpack_one()), merged_parts(level_two))
 
 
 def body(*arrays):

time: 175 us -> 159 us (0.909); the launches traced: 178 us -> 157 us
  waiting for transfers between devices: 97.4 us -> 55.8 us
  starting transfers between devices: 36.7 us -> 61.6 us
  Pallas kernels: 33.7 us -> 24.1 us
  local copies, waits for them, and re-layouts: 5 us -> 9.49 us
    ppermute x15 -> x21, waiting for transfers between devices: 72.9 us -> 48.8 us  [cross(): lax.ppermute(values, 'span', [(at, at ^ 1 << bit) for at in range(spans)])]
    all_to_all x1 -> x0, waiting for transfers between devices: 23.1 us -> none  [raise_level(): lax.all_to_all(parts, 'span', split_axis=0, concat_axis=0, tiled=True)]
    ppermute x15 -> x21, starting transfers between devices: 28.7 us -> 46.8 us  [cross(): lax.ppermute(values, 'span', [(at, at ^ 1 << bit) for at in range(spans)])]
    ppermute x0 -> x7, starting transfers between devices: none -> 13.4 us  [raise_level(): lax.ppermute(part, 'span', [(at, at ^ away) for at in range(spans)])]
    pallas_call x6 -> x4, Pallas kernels: 32.3 us -> 22.7 us  [the longest x3 21.1 us: fold_children(): pl.pallas_call(kernel, out_shape=halves, in_specs=[scalars, scalars] + [o...]
    all_to_all x1 -> x0, starting transfers between devices: 7.13 us -> none  [raise_level(): lax.all_to_all(parts, 'span', split_axis=0, concat_axis=0, tiled=True)]
    ppermute x0 -> x7, waiting for transfers between devices: none -> 6.97 us  [raise_level(): lax.ppermute(part, 'span', [(at, at ^ away) for at in range(spans)])]
    concatenate x2, local copies, waits for them, and re-layouts: 0.03 us -> 3.17 us  [merged_parts(): return jnp.concatenate([sums[:1], centre, spread] + rest, 0)]
  transfers between devices with their start and end apart: 22 -> 36, of which waited for: 12 -> 15; matrix products, arithmetic and copies ran while one was open for 1% -> 4% of each run, Pallas kernels for 12% -> 9%
where the time goes in v3:
time: 159 us; the launch traced here: 157 us
  starting transfers between devices  61.6 us (39%)
  waiting for transfers between devices  55.8 us (35%)
  Pallas kernels  24.1 us (15%)
  local copies, waits for them, and re-layouts  9.49 us (6%)
  other arithmetic  3.85 us (2%)
  between operations  1.67 us (1%)
    ppermute x21, waiting for transfers between devices, cross(): lax.ppermute(values, 'span', [(at, at ^ 1 << bit) for at in range(spans)])  48.8 us
    ppermute x21, starting transfers between devices, cross(): lax.ppermute(values, 'span', [(at, at ^ 1 << bit) for at in range(spans)])  46.8 us
    pallas_call x3, Pallas kernels, fold_children(): pl.pallas_call(kernel, out_shape=halves, in_specs=[scalars, scalars] + [o...  21.1 us
    ppermute x7, starting transfers between devices, raise_level(): lax.ppermute(part, 'span', [(at, at ^ away) for at in range(spans)])  13.4 us
    ppermute x7, waiting for transfers between devices, raise_level(): lax.ppermute(part, 'span', [(at, at ^ away) for at in range(spans)])  6.97 us
    unnamed x18, local copies, waits for them, and re-layouts  6.08 us
  transfers between devices with their start and end apart: 36, of which 15 were waited for; matrix products, arithmetic and copies ran while one was open for 4% of the time, Pallas kernels for 9%

profile of v3, /device:TPU:0, one launch (start us, length us, event | category | flops | bytes accessed | tf_op | source)
XLA Modules:
  0.0 156.6 jit_solution(7615382963070953258)
XLA Ops:
  1.3 1.2 fusion.20.refs_0_
  2.5 7.8 %fold_children.3 = (f32[320,8,128]{2,1,0:T(8,128)}, f32[320,8,128]{2,1,0:T(8,128)}) custom-call(s32[128]{0:T(128)} %fusion.20.refs_0_, s32[1]{0:T(128)S(6)} %copy.21.refs_1_, s32[128,128]{1,0:T(8,128)} %refs_2_.6, f32[128,128]{1,0:T(8,128)} %refs_3_.5, f32[3,128,128]{2,1,0:T(8,128)} %refs_4_.3, f32[6,128,128]{2,1,0:T(8,128)} %refs_5_.1), custom_call_target="tpu_custom_call" | custom-call | flops 1024 | bytes 1024 | tf_op jit(solution)/shard_map/fold_children/pallas_call | solution.py:335
  10.4 1.4 copy-done
  14.1 6.7 %fold_children.4 = (f32[256,8,128]{2,1,0:T(8,128)S(1)}, f32[256,8,128]{2,1,0:T(8,128)S(1)}, f32[256,8,128]{2,1,0:T(8,128)S(1)}, f32[256,8,128]{2,1,0:T(8,128)S(1...) custom-call(s32[128]{0:T(128)S(1)} %copy-done.4, s32[1]{0:T(128)S(6)} %copy.21.refs_1_, ...), custom_call_target="tpu_custom_call" | custom-call | flops 1024 | bytes 1024 | tf_op jit(solution)/shard_map/fold_children/pallas_call | solution.py:335
  21.7 1.7 %collective-permute-start.1 = (f32[160,8,128]{2,1,0:T(8,128)S(1)}, f32[160,8,128]{2,1,0:T(8,128)S(1)}, u32[]{:S(2)}, u32[]{:S(2)}) collective-permute-start(f32[160,8,128]{2,1,0:T(8,128)S(1)} %slice_add_fusion), channel_id=1, source_target_pairs={{0,2},{2,0},{4,6},{6,4},{8,10},{10,8},{12,14},{14,12},{1,3},{3,1},... | collective-permute-start | bytes 1966088 | tf_op jit(solution)/shard_map/ppermute | solution.py:540
  23.6 1.5 collective-permute-start.6
  25.1 6.7 %fold_children.5 = (f32[256,8,128]{2,1,0:T(8,128)S(1)}, f32[256,8,128]{2,1,0:T(8,128)S(1)}, f32[256,8,128]{2,1,0:T(8,128)S(1)}, f32[256,8,128]{2,1,0:T(8,128)S(1...) custom-call(s32[128]{0:T(128)S(1)} %copy-done.4, s32[1]{0:T(128)S(6)} %copy.21.refs_1_, ...), custom_call_target="tpu_custom_call" | custom-call | flops 1024 | bytes 1024 | tf_op jit(solution)/shard_map/fold_children/pallas_call | solution.py:335
  31.9 7.4 %collective-permute-done.1 = f32[160,8,128]{2,1,0:T(8,128)S(1)} collective-permute-done((f32[160,8,128]{2,1,0:T(8,128)S(1)}, f32[160,8,128]{2,1,0:T(8,128)S(1)}, u32[]{:S(2)}, u32[]{:S(2)}) %collective-permute-start.1) | collective-permute-done | bytes 655392 | tf_op jit(solution)/shard_map/ppermute | solution.py:540
  39.4 3.1 %collective-permute-start.3 = (f32[80,8,128]{2,1,0:T(8,128)S(1)}, f32[80,8,128]{2,1,0:T(8,128)S(1)}, u32[]{:S(2)}, u32[]{:S(2)}) collective-permute-start(f32[80,8,128]{2,1,0:T(8,128)S(1)} %slice_add_fusion.7), channel_id=1, source_target_pairs={{0,4},{2,6},{4,0},{6,2},{8,12},{10,14},{12,8},{14,10},{1,5},{3,7},... | collective-permute-start | bytes 983048 | tf_op jit(solution)/shard_map/ppermute | solution.py:540
  43.1 7.0 %collective-permute-done.6 = f32[128,8,128]{2,1,0:T(8,128)S(1)} collective-permute-done((f32[128,8,128]{2,1,0:T(8,128)S(1)}, f32[128,8,128]{2,1,0:T(8,128)S(1)}, u32[]{:S(2)}, u32[]{:S(2)}) %collective-permute-start.6) | collective-permute-done | bytes 524320 | tf_op jit(solution)/shard_map/ppermute | solution.py:540
  50.1 1.3 collective-permute-start.10
  51.5 4.3 %collective-permute-start.7 = (f32[40,8,128]{2,1,0:T(8,128)S(1)}, f32[40,8,128]{2,1,0:T(8,128)S(1)}, u32[]{:S(2)}, u32[]{:S(2)}) collective-permute-start(f32[40,8,128]{2,1,0:T(8,128)S(1)} %slice_add_fusion.21), channel_id=1, source_target_pairs={{0,8},{2,10},{4,12},{6,14},{8,0},{10,2},{12,4},{14,6},{1,9},{3,11}... | collective-permute-start | bytes 491528 | tf_op jit(solution)/shard_map/ppermute | solution.py:540
  55.8 1.6 collective-permute-start.8
  57.5 6.1 %collective-permute-done.10 = f32[128,8,128]{2,1,0:T(8,128)S(1)} collective-permute-done((f32[128,8,128]{2,1,0:T(8,128)S(1)}, f32[128,8,128]{2,1,0:T(8,128)S(1)}, u32[]{:S(2)}, u32[]{:S(2)}) %collective-permute-start.10) | collective-permute-done | bytes 524320 | tf_op jit(solution)/shard_map/ppermute | solution.py:540
  63.6 0.9 collective-permute-start.14
  64.5 1.2 collective-permute-done.8
  65.8 1.8 %collective-permute-start.12 = (f32[64,8,128]{2,1,0:T(8,128)S(1)}, f32[64,8,128]{2,1,0:T(8,128)S(1)}, u32[]{:S(2)}, u32[]{:S(2)}) collective-permute-start(f32[64,8,128]{2,1,0:T(8,128)S(1)} %slice_add_fusion.17), channel_id=1, source_target_pairs={{0,4},{2,6},{4,0},{6,2},{8,12},{10,14},{12,8},{14,10},{1,5},{3,7},... | collective-permute-start | bytes 786440 | tf_op jit(solution)/shard_map/ppermute | solution.py:540
  67.7 3.2 %collective-permute-start.11 = (f32[32,8,128]{2,1,0:T(8,128)S(1)}, f32[32,8,128]{2,1,0:T(8,128)S(1)}, u32[]{:S(2)}, u32[]{:S(2)}) collective-permute-start(f32[32,8,128]{2,1,0:T(8,128)S(1)} %slice_add_fusion.57), channel_id=1, source_target_pairs={{0,8},{2,10},{4,12},{6,14},{8,0},{10,2},{12,4},{14,6},{1,9},{3,11}... | collective-permute-start | bytes 393224 | tf_op jit(solution)/shard_map/ppermute | solution.py:540
  71.2 4.0 %collective-permute-done.12 = f32[64,8,128]{2,1,0:T(8,128)S(1)} collective-permute-done((f32[64,8,128]{2,1,0:T(8,128)S(1)}, f32[64,8,128]{2,1,0:T(8,128)S(1)}, u32[]{:S(2)}, u32[]{:S(2)}) %collective-permute-start.12) | collective-permute-done | bytes 262176 | tf_op jit(solution)/shard_map/ppermute | solution.py:540
  75.2 3.3 %collective-permute-done.14 = f32[128,8,128]{2,1,0:T(8,128)S(1)} collective-permute-done((f32[128,8,128]{2,1,0:T(8,128)S(1)}, f32[128,8,128]{2,1,0:T(8,128)S(1)}, u32[]{:S(2)}, u32[]{:S(2)}) %collective-permute-start.14) | collective-permute-done | bytes 524320 | tf_op jit(solution)/shard_map/ppermute | solution.py:540
  78.5 3.1 %collective-permute-start.16 = (f32[64,8,128]{2,1,0:T(8,128)S(1)}, f32[64,8,128]{2,1,0:T(8,128)S(1)}, u32[]{:S(2)}, u32[]{:S(2)}) collective-permute-start(f32[64,8,128]{2,1,0:T(8,128)S(1)} %slice_add_fusion.15), channel_id=1, source_target_pairs={{0,4},{2,6},{4,0},{6,2},{8,12},{10,14},{12,8},{14,10},{1,5},{3,7},... | collective-permute-start | bytes 786440 | tf_op jit(solution)/shard_map/ppermute | solution.py:540
  81.7 2.2 %collective-permute-start.15 = (f32[32,8,128]{2,1,0:T(8,128)S(1)}, f32[32,8,128]{2,1,0:T(8,128)S(1)}, u32[]{:S(2)}, u32[]{:S(2)}) collective-permute-start(f32[32,8,128]{2,1,0:T(8,128)S(1)} %slice_add_fusion.51), channel_id=1, source_target_pairs={{0,8},{2,10},{4,12},{6,14},{8,0},{10,2},{12,4},{14,6},{1,9},{3,11}... | collective-permute-start | bytes 393224 | tf_op jit(solution)/shard_map/ppermute | solution.py:540
  83.9 1.7 %collective-permute-start.21 = (f32[128,8,128]{2,1,0:T(8,128)S(1)}, f32[128,8,128]{2,1,0:T(8,128)S(1)}, u32[]{:S(2)}, u32[]{:S(2)}) collective-permute-start(f32[128,8,128]{2,1,0:T(8,128)S(1)} %slice_add_fusion.2), channel_id=1, source_target_pairs={{0,2},{2,0},{4,6},{6,4},{8,10},{10,8},{12,14},{14,12},{1,3},{3,1},... | collective-permute-start | bytes 1572872 | tf_op jit(solution)/shard_map/ppermute | solution.py:540
  85.7 4.0 %collective-permute-done.18 = f32[128,8,128]{2,1,0:T(8,128)S(1)} collective-permute-done((f32[128,8,128]{2,1,0:T(8,128)S(1)}, f32[128,8,128]{2,1,0:T(8,128)S(1)}, u32[]{:S(2)}, u32[]{:S(2)}) %collective-permute-start.18) | collective-permute-done | bytes 524320 | tf_op jit(solution)/shard_map/ppermute | solution.py:540
  89.8 3.1 %collective-permute-start.20 = (f32[64,8,128]{2,1,0:T(8,128)S(1)}, f32[64,8,128]{2,1,0:T(8,128)S(1)}, u32[]{:S(2)}, u32[]{:S(2)}) collective-permute-start(f32[64,8,128]{2,1,0:T(8,128)S(1)} %slice_add_fusion.13), channel_id=1, source_target_pairs={{0,4},{2,6},{4,0},{6,2},{8,12},{10,14},{12,8},{14,10},{1,5},{3,7},... | collective-permute-start | bytes 786440 | tf_op jit(solution)/shard_map/ppermute | solution.py:540
  93.0 2.2 %collective-permute-start.19 = (f32[32,8,128]{2,1,0:T(8,128)S(1)}, f32[32,8,128]{2,1,0:T(8,128)S(1)}, u32[]{:S(2)}, u32[]{:S(2)}) collective-permute-start(f32[32,8,128]{2,1,0:T(8,128)S(1)} %slice_add_fusion.45), channel_id=1, source_target_pairs={{0,8},{2,10},{4,12},{6,14},{8,0},{10,2},{12,4},{14,6},{1,9},{3,11}... | collective-permute-start | bytes 393224 | tf_op jit(solution)/shard_map/ppermute | solution.py:540
  95.2 1.7 %collective-permute-start.24 = (f32[128,8,128]{2,1,0:T(8,128)S(1)}, f32[128,8,128]{2,1,0:T(8,128)S(1)}, u32[]{:S(2)}, u32[]{:S(2)}) collective-permute-start(f32[128,8,128]{2,1,0:T(8,128)S(1)} %slice_add_fusion.1), channel_id=1, source_target_pairs={{0,2},{2,0},{4,6},{6,4},{8,10},{10,8},{12,14},{14,12},{1,3},{3,1},... | collective-permute-start | bytes 1572872 | tf_op jit(solution)/shard_map/ppermute | solution.py:540
  96.9 4.0 %collective-permute-done.21 = f32[128,8,128]{2,1,0:T(8,128)S(1)} collective-permute-done((f32[128,8,128]{2,1,0:T(8,128)S(1)}, f32[128,8,128]{2,1,0:T(8,128)S(1)}, u32[]{:S(2)}, u32[]{:S(2)}) %collective-permute-start.21) | collective-permute-done | bytes 524320 | tf_op jit(solution)/shard_map/ppermute | solution.py:540
  101.1 3.1 %collective-permute-start.23 = (f32[64,8,128]{2,1,0:T(8,128)S(1)}, f32[64,8,128]{2,1,0:T(8,128)S(1)}, u32[]{:S(2)}, u32[]{:S(2)}) collective-permute-start(f32[64,8,128]{2,1,0:T(8,128)S(1)} %slice_add_fusion.11), channel_id=1, source_target_pairs={{0,4},{2,6},{4,0},{6,2},{8,12},{10,14},{12,8},{14,10},{1,5},{3,7},... | collective-permute-start | bytes 786440 | tf_op jit(solution)/shard_map/ppermute | solution.py:540
  104.2 2.2 %collective-permute-start.22 = (f32[32,8,128]{2,1,0:T(8,128)S(1)}, f32[32,8,128]{2,1,0:T(8,128)S(1)}, u32[]{:S(2)}, u32[]{:S(2)}) collective-permute-start(f32[32,8,128]{2,1,0:T(8,128)S(1)} %slice_add_fusion.39), channel_id=1, source_target_pairs={{0,8},{2,10},{4,12},{6,14},{8,0},{10,2},{12,4},{14,6},{1,9},{3,11}... | collective-permute-start | bytes 393224 | tf_op jit(solution)/shard_map/ppermute | solution.py:540
  106.4 3.5 %collective-permute-done.24 = f32[128,8,128]{2,1,0:T(8,128)S(1)} collective-permute-done((f32[128,8,128]{2,1,0:T(8,128)S(1)}, f32[128,8,128]{2,1,0:T(8,128)S(1)}, u32[]{:S(2)}, u32[]{:S(2)}) %collective-permute-start.24) | collective-permute-done | bytes 524320 | tf_op jit(solution)/shard_map/ppermute | solution.py:540
  110.1 3.0 %collective-permute-start.26 = (f32[64,8,128]{2,1,0:T(8,128)S(1)}, f32[64,8,128]{2,1,0:T(8,128)S(1)}, u32[]{:S(2)}, u32[]{:S(2)}) collective-permute-start(f32[64,8,128]{2,1,0:T(8,128)S(1)} %slice_add_fusion.9), channel_id=1, source_target_pairs={{0,4},{2,6},{4,0},{6,2},{8,12},{10,14},{12,8},{14,10},{1,5},{3,7},... | collective-permute-start | bytes 786440 | tf_op jit(solution)/shard_map/ppermute | solution.py:540
  113.2 2.0 %collective-permute-start.25 = (f32[32,8,128]{2,1,0:T(8,128)S(1)}, f32[32,8,128]{2,1,0:T(8,128)S(1)}, u32[]{:S(2)}, u32[]{:S(2)}) collective-permute-start(f32[32,8,128]{2,1,0:T(8,128)S(1)} %slice_add_fusion.33), channel_id=1, source_target_pairs={{0,8},{2,10},{4,12},{6,14},{8,0},{10,2},{12,4},{14,6},{1,9},{3,11}... | collective-permute-start | bytes 393224 | tf_op jit(solution)/shard_map/ppermute | solution.py:540
  115.2 5.0 %collective-permute-done.26 = f32[64,8,128]{2,1,0:T(8,128)S(1)} collective-permute-done((f32[64,8,128]{2,1,0:T(8,128)S(1)}, f32[64,8,128]{2,1,0:T(8,128)S(1)}, u32[]{:S(2)}, u32[]{:S(2)}) %collective-permute-start.26) | collective-permute-done | bytes 262176 | tf_op jit(solution)/shard_map/ppermute | solution.py:540
  120.3 2.6 %collective-permute-start.27 = (f32[32,8,128]{2,1,0:T(8,128)S(1)}, f32[32,8,128]{2,1,0:T(8,128)S(1)}, u32[]{:S(2)}, u32[]{:S(2)}) collective-permute-start(f32[32,8,128]{2,1,0:T(8,128)S(1)} %slice_add_fusion.27), channel_id=1, source_target_pairs={{0,8},{2,10},{4,12},{6,14},{8,0},{10,2},{12,4},{14,6},{1,9},{3,11}... | collective-permute-start | bytes 393224 | tf_op jit(solution)/shard_map/ppermute | solution.py:540
  123.1 3.1 %collective-permute-done.27 = f32[32,8,128]{2,1,0:T(8,128)S(1)} collective-permute-done((f32[32,8,128]{2,1,0:T(8,128)S(1)}, f32[32,8,128]{2,1,0:T(8,128)S(1)}, u32[]{:S(2)}, u32[]{:S(2)}) %collective-permute-start.27) | collective-permute-done | bytes 131104 | tf_op jit(solution)/shard_map/ppermute | solution.py:540
  127.0 1.6 fold_parents.1
  128.6 1.7 %collective-permute-start.28 = (f32[30,8,128]{2,1,0:T(8,128)S(1)}, f32[30,8,128]{2,1,0:T(8,128)S(1)}, u32[]{:S(2)}, u32[]{:S(2)}) collective-permute-start(f32[30,8,128]{2,1,0:T(8,128)S(1)} %get-tuple-element.92), channel_id=1, source_target_pairs={{0,2},{2,0},{4,6},{6,4},{8,10},{10,8},{12,14},{14,12},{1,3},{3,1},... | collective-permute-start | bytes 368648 | tf_op jit(solution)/shard_map/ppermute | solution.py:618
  130.3 2.6 %collective-permute-start.29 = (f32[30,8,128]{2,1,0:T(8,128)S(1)}, f32[30,8,128]{2,1,0:T(8,128)S(1)}, u32[]{:S(2)}, u32[]{:S(2)}) collective-permute-start(f32[30,8,128]{2,1,0:T(8,128)S(1)} %get-tuple-element.94), channel_id=1, source_target_pairs={{0,4},{2,6},{4,0},{6,2},{8,12},{10,14},{12,8},{14,10},{1,5},{3,7},... | collective-permute-start | bytes 368648 | tf_op jit(solution)/shard_map/ppermute | solution.py:618
  133.2 2.4 %collective-permute-start.31 = (f32[30,8,128]{2,1,0:T(8,128)S(1)}, f32[30,8,128]{2,1,0:T(8,128)S(1)}, u32[]{:S(2)}, u32[]{:S(2)}) collective-permute-start(f32[30,8,128]{2,1,0:T(8,128)S(1)} %get-tuple-element.98), channel_id=1, source_target_pairs={{0,8},{2,10},{4,12},{6,14},{8,0},{10,2},{12,4},{14,6},{1,9},{3,11}... | collective-permute-start | bytes 368648 | tf_op jit(solution)/shard_map/ppermute | solution.py:618
  135.6 1.4 collective-permute-start.32
  137.0 3.8 %collective-permute-start.33 = (f32[30,8,128]{2,1,0:T(8,128)S(1)}, f32[30,8,128]{2,1,0:T(8,128)S(1)}, u32[]{:S(2)}, u32[]{:S(2)}) collective-permute-start(f32[30,8,128]{2,1,0:T(8,128)S(1)} %get-tuple-element.102), channel_id=1, source_target_pairs={{0,12},{2,14},{4,8},{6,10},{8,4},{10,6},{12,0},{14,2},{1,13},{3,15... | collective-permute-start | bytes 368648 | tf_op jit(solution)/shard_map/ppermute | solution.py:618
  140.8 1.5 collective-permute-start.34
  142.3 2.4 %concatenate.13 = f32[58,32,128]{2,0,1:T(8,128)S(1)} concatenate(f32[1,32,128]{2,0,1:T(1,128)S(1)} %get-tuple-element.135, f32[3,32,128]{2,0,1:T(4,128)S(1)} %fusion.9, f32[6,32,128]{2,0,1:T(8,128)S(1)} %fusion.8, f32[8,32,128]{2,0,1:T(8,128)S(1)} %get-tuple-element.156, f32[8,32,128]{2,0,1:T(8,128)S(1)} %get-tuple-element.150, f32[8,32,128]{2,0,1:T(8,128)} %get-tuple-element.152, ...), dimensions={0} | concatenate | bytes 1900544 | tf_op jit(solution)/shard_map/concatenate | solution.py:498
  144.7 3.2 %collective-permute-done.31.refs_5_ = f32[30,8,128]{2,1,0:T(8,128)S(1)} collective-permute-done((f32[30,8,128]{2,1,0:T(8,128)S(1)}, f32[30,8,128]{2,1,0:T(8,128)S(1)}, u32[]{:S(2)}, u32[]{:S(2)}) %collective-permute-start.31) | collective-permute-done | bytes 122912 | tf_op jit(solution)/shard_map/ppermute | solution.py:618
  148.0 3.7 %collective-permute-done.32.refs_6_ = f32[30,8,128]{2,1,0:T(8,128)S(1)} collective-permute-done((f32[30,8,128]{2,1,0:T(8,128)S(1)}, f32[30,8,128]{2,1,0:T(8,128)S(1)}, u32[]{:S(2)}, u32[]{:S(2)}) %collective-permute-start.32) | collective-permute-done | bytes 122912 | tf_op jit(solution)/shard_map/ppermute | solution.py:618
  151.7 1.4 place_parents.1
  153.2 1.5 copy.19
  (92 shorter events, 8.8 us)
Async XLA Ops:
  0.6 20.8 %copy-start.7 = (s32[32]{0:T(128)S(1)}, s32[32]{0:T(128)}, u32[]{:S(2)}) copy-start(s32[32]{0:T(128)} %param.19) | copy-start | bytes 388
  10.3 11.3 %collective-permute-start = (f32[320,8,128]{2,1,0:T(8,128)}, f32[320,8,128]{2,1,0:T(8,128)S(1)}, u32[]{:S(2)}, u32[]{:S(2)}) collective-permute-start(f32[320,8,128]{2,1,0:T(8,128)} %get-tuple-element.56), channel_id=1, source_target_pairs={{0,1},{1,0},{2,3},{3,2},{4,5},{5,4},{6,7},{7,6},{8,9},{9,8},{10,11... | collective-permute-start | bytes 3932168 | tf_op jit(solution)/shard_map/ppermute | solution.py:537
  10.4 1.4 copy-start
  11.8 0.8 copy-start.1
  12.6 0.8 copy-start.2
  13.5 0.7 copy-start.4
  14.1 7.5 %copy-start.6 = (f32[320,8,128]{2,1,0:T(8,128)S(1)}, f32[320,8,128]{2,1,0:T(8,128)}, u32[]{:S(2)}) copy-start(f32[320,8,128]{2,1,0:T(8,128)} %get-tuple-element.55) | copy-start | bytes 3932164
  20.8 2.7 %collective-permute-start.5 = (f32[256,8,128]{2,1,0:T(8,128)S(1)}, f32[256,8,128]{2,1,0:T(8,128)S(1)}, u32[]{:S(2)}, u32[]{:S(2)}) collective-permute-start(f32[256,8,128]{2,1,0:T(8,128)S(1)} %get-tuple-element.64), channel_id=1, source_target_pairs={{0,1},{1,0},{2,3},{3,2},{4,5},{5,4},{6,7},{7,6},{8,9},{9,8},{10,11... | collective-permute-start | bytes 3145736 | tf_op jit(solution)/shard_map/ppermute | solution.py:537
  20.9 10.9 %collective-permute-start.2 = (f32[256,8,128]{2,1,0:T(8,128)S(1)}, f32[256,8,128]{2,1,0:T(8,128)S(1)}, u32[]{:S(2)}, u32[]{:S(2)}) collective-permute-start(f32[256,8,128]{2,1,0:T(8,128)S(1)} %get-tuple-element.59), channel_id=1, source_target_pairs={{0,1},{1,0},{2,3},{3,2},{4,5},{5,4},{6,7},{7,6},{8,9},{9,8},{10,11... | collective-permute-start | bytes 3145736 | tf_op jit(solution)/shard_map/ppermute | solution.py:537
  21.4 21.1 %collective-permute-start.4 = (f32[256,8,128]{2,1,0:T(8,128)S(1)}, f32[256,8,128]{2,1,0:T(8,128)S(1)}, u32[]{:S(2)}, u32[]{:S(2)}) collective-permute-start(f32[256,8,128]{2,1,0:T(8,128)S(1)} %get-tuple-element.62), channel_id=1, source_target_pairs={{0,1},{1,0},{2,3},{3,2},{4,5},{5,4},{6,7},{7,6},{8,9},{9,8},{10,11... | collective-permute-start | bytes 3145736 | tf_op jit(solution)/shard_map/ppermute | solution.py:537
  21.7 17.6 %collective-permute-start.1 = (f32[160,8,128]{2,1,0:T(8,128)S(1)}, f32[160,8,128]{2,1,0:T(8,128)S(1)}, u32[]{:S(2)}, u32[]{:S(2)}) collective-permute-start(f32[160,8,128]{2,1,0:T(8,128)S(1)} %slice_add_fusion), channel_id=1, source_target_pairs={{0,2},{2,0},{4,6},{6,4},{8,10},{10,8},{12,14},{14,12},{1,3},{3,1},... | collective-permute-start | bytes 1966088 | tf_op jit(solution)/shard_map/ppermute | solution.py:540
  23.6 26.5 %collective-permute-start.6 = (f32[128,8,128]{2,1,0:T(8,128)S(1)}, f32[128,8,128]{2,1,0:T(8,128)S(1)}, u32[]{:S(2)}, u32[]{:S(2)}) collective-permute-start(f32[128,8,128]{2,1,0:T(8,128)S(1)} %slice_add_fusion.4), channel_id=1, source_target_pairs={{0,2},{2,0},{4,6},{6,4},{8,10},{10,8},{12,14},{14,12},{1,3},{3,1},... | collective-permute-start | bytes 1572872 | tf_op jit(solution)/shard_map/ppermute | solution.py:540
  31.7 24.1 %collective-permute-start.9 = (f32[256,8,128]{2,1,0:T(8,128)S(1)}, f32[256,8,128]{2,1,0:T(8,128)S(1)}, u32[]{:S(2)}, u32[]{:S(2)}) collective-permute-start(f32[256,8,128]{2,1,0:T(8,128)S(1)} %get-tuple-element.69), channel_id=1, source_target_pairs={{0,1},{1,0},{2,3},{3,2},{4,5},{5,4},{6,7},{7,6},{8,9},{9,8},{10,11... | collective-permute-start | bytes 3145736 | tf_op jit(solution)/shard_map/ppermute | solution.py:537
  39.4 12.1 %collective-permute-start.3 = (f32[80,8,128]{2,1,0:T(8,128)S(1)}, f32[80,8,128]{2,1,0:T(8,128)S(1)}, u32[]{:S(2)}, u32[]{:S(2)}) collective-permute-start(f32[80,8,128]{2,1,0:T(8,128)S(1)} %slice_add_fusion.7), channel_id=1, source_target_pairs={{0,4},{2,6},{4,0},{6,2},{8,12},{10,14},{12,8},{14,10},{1,5},{3,7},... | collective-permute-start | bytes 983048 | tf_op jit(solution)/shard_map/ppermute | solution.py:540
  42.6 25.0 %collective-permute-start.13 = (f32[256,8,128]{2,1,0:T(8,128)S(1)}, f32[256,8,128]{2,1,0:T(8,128)S(1)}, u32[]{:S(2)}, u32[]{:S(2)}) collective-permute-start(f32[256,8,128]{2,1,0:T(8,128)S(1)} %get-tuple-element.74), channel_id=1, source_target_pairs={{0,1},{1,0},{2,3},{3,2},{4,5},{5,4},{6,7},{7,6},{8,9},{9,8},{10,11... | collective-permute-start | bytes 3145736 | tf_op jit(solution)/shard_map/ppermute | solution.py:537
  42.6 39.0 %collective-permute-start.17 = (f32[256,8,128]{2,1,0:T(8,128)S(1)}, f32[256,8,128]{2,1,0:T(8,128)S(1)}, u32[]{:S(2)}, u32[]{:S(2)}) collective-permute-start(f32[256,8,128]{2,1,0:T(8,128)S(1)} %get-tuple-element.79), channel_id=1, source_target_pairs={{0,1},{1,0},{2,3},{3,2},{4,5},{5,4},{6,7},{7,6},{8,9},{9,8},{10,11... | collective-permute-start | bytes 3145736 | tf_op jit(solution)/shard_map/ppermute | solution.py:537
  50.1 13.5 %collective-permute-start.10 = (f32[128,8,128]{2,1,0:T(8,128)S(1)}, f32[128,8,128]{2,1,0:T(8,128)S(1)}, u32[]{:S(2)}, u32[]{:S(2)}) collective-permute-start(f32[128,8,128]{2,1,0:T(8,128)S(1)} %slice_add_fusion.6), channel_id=1, source_target_pairs={{0,2},{2,0},{4,6},{6,4},{8,10},{10,8},{12,14},{14,12},{1,3},{3,1},... | collective-permute-start | bytes 1572872 | tf_op jit(solution)/shard_map/ppermute | solution.py:540
  51.5 14.2 %collective-permute-start.7 = (f32[40,8,128]{2,1,0:T(8,128)S(1)}, f32[40,8,128]{2,1,0:T(8,128)S(1)}, u32[]{:S(2)}, u32[]{:S(2)}) collective-permute-start(f32[40,8,128]{2,1,0:T(8,128)S(1)} %slice_add_fusion.21), channel_id=1, source_target_pairs={{0,8},{2,10},{4,12},{6,14},{8,0},{10,2},{12,4},{14,6},{1,9},{3,11}... | collective-permute-start | bytes 491528 | tf_op jit(solution)/shard_map/ppermute | solution.py:540
  55.8 9.9 %collective-permute-start.8 = (f32[64,8,128]{2,1,0:T(8,128)S(1)}, f32[64,8,128]{2,1,0:T(8,128)S(1)}, u32[]{:S(2)}, u32[]{:S(2)}) collective-permute-start(f32[64,8,128]{2,1,0:T(8,128)S(1)} %slice_add_fusion.19), channel_id=1, source_target_pairs={{0,4},{2,6},{4,0},{6,2},{8,12},{10,14},{12,8},{14,10},{1,5},{3,7},... | collective-permute-start | bytes 786440 | tf_op jit(solution)/shard_map/ppermute | solution.py:540
  63.6 14.9 %collective-permute-start.14 = (f32[128,8,128]{2,1,0:T(8,128)S(1)}, f32[128,8,128]{2,1,0:T(8,128)S(1)}, u32[]{:S(2)}, u32[]{:S(2)}) collective-permute-start(f32[128,8,128]{2,1,0:T(8,128)S(1)} %slice_add_fusion.5), channel_id=1, source_target_pairs={{0,2},{2,0},{4,6},{6,4},{8,10},{10,8},{12,14},{14,12},{1,3},{3,1},... | collective-permute-start | bytes 1572872 | tf_op jit(solution)/shard_map/ppermute | solution.py:540
  65.8 9.4 %collective-permute-start.12 = (f32[64,8,128]{2,1,0:T(8,128)S(1)}, f32[64,8,128]{2,1,0:T(8,128)S(1)}, u32[]{:S(2)}, u32[]{:S(2)}) collective-permute-start(f32[64,8,128]{2,1,0:T(8,128)S(1)} %slice_add_fusion.17), channel_id=1, source_target_pairs={{0,4},{2,6},{4,0},{6,2},{8,12},{10,14},{12,8},{14,10},{1,5},{3,7},... | collective-permute-start | bytes 786440 | tf_op jit(solution)/shard_map/ppermute | solution.py:540
  67.7 10.9 %collective-permute-start.11 = (f32[32,8,128]{2,1,0:T(8,128)S(1)}, f32[32,8,128]{2,1,0:T(8,128)S(1)}, u32[]{:S(2)}, u32[]{:S(2)}) collective-permute-start(f32[32,8,128]{2,1,0:T(8,128)S(1)} %slice_add_fusion.57), channel_id=1, source_target_pairs={{0,8},{2,10},{4,12},{6,14},{8,0},{10,2},{12,4},{14,6},{1,9},{3,11}... | collective-permute-start | bytes 393224 | tf_op jit(solution)/shard_map/ppermute | solution.py:540
  70.9 18.8 %collective-permute-start.18 = (f32[128,8,128]{2,1,0:T(8,128)S(1)}, f32[128,8,128]{2,1,0:T(8,128)S(1)}, u32[]{:S(2)}, u32[]{:S(2)}) collective-permute-start(f32[128,8,128]{2,1,0:T(8,128)S(1)} %slice_add_fusion.3), channel_id=1, source_target_pairs={{0,2},{2,0},{4,6},{6,4},{8,10},{10,8},{12,14},{14,12},{1,3},{3,1},... | collective-permute-start | bytes 1572872 | tf_op jit(solution)/shard_map/ppermute | solution.py:540
  78.5 11.2 %collective-permute-start.16 = (f32[64,8,128]{2,1,0:T(8,128)S(1)}, f32[64,8,128]{2,1,0:T(8,128)S(1)}, u32[]{:S(2)}, u32[]{:S(2)}) collective-permute-start(f32[64,8,128]{2,1,0:T(8,128)S(1)} %slice_add_fusion.15), channel_id=1, source_target_pairs={{0,4},{2,6},{4,0},{6,2},{8,12},{10,14},{12,8},{14,10},{1,5},{3,7},... | collective-permute-start | bytes 786440 | tf_op jit(solution)/shard_map/ppermute | solution.py:540
  81.7 8.1 %collective-permute-start.15 = (f32[32,8,128]{2,1,0:T(8,128)S(1)}, f32[32,8,128]{2,1,0:T(8,128)S(1)}, u32[]{:S(2)}, u32[]{:S(2)}) collective-permute-start(f32[32,8,128]{2,1,0:T(8,128)S(1)} %slice_add_fusion.51), channel_id=1, source_target_pairs={{0,8},{2,10},{4,12},{6,14},{8,0},{10,2},{12,4},{14,6},{1,9},{3,11}... | collective-permute-start | bytes 393224 | tf_op jit(solution)/shard_map/ppermute | solution.py:540
  83.9 17.0 %collective-permute-start.21 = (f32[128,8,128]{2,1,0:T(8,128)S(1)}, f32[128,8,128]{2,1,0:T(8,128)S(1)}, u32[]{:S(2)}, u32[]{:S(2)}) collective-permute-start(f32[128,8,128]{2,1,0:T(8,128)S(1)} %slice_add_fusion.2), channel_id=1, source_target_pairs={{0,2},{2,0},{4,6},{6,4},{8,10},{10,8},{12,14},{14,12},{1,3},{3,1},... | collective-permute-start | bytes 1572872 | tf_op jit(solution)/shard_map/ppermute | solution.py:540
  89.8 11.2 %collective-permute-start.20 = (f32[64,8,128]{2,1,0:T(8,128)S(1)}, f32[64,8,128]{2,1,0:T(8,128)S(1)}, u32[]{:S(2)}, u32[]{:S(2)}) collective-permute-start(f32[64,8,128]{2,1,0:T(8,128)S(1)} %slice_add_fusion.13), channel_id=1, source_target_pairs={{0,4},{2,6},{4,0},{6,2},{8,12},{10,14},{12,8},{14,10},{1,5},{3,7},... | collective-permute-start | bytes 786440 | tf_op jit(solution)/shard_map/ppermute | solution.py:540
  93.0 8.1 %collective-permute-start.19 = (f32[32,8,128]{2,1,0:T(8,128)S(1)}, f32[32,8,128]{2,1,0:T(8,128)S(1)}, u32[]{:S(2)}, u32[]{:S(2)}) collective-permute-start(f32[32,8,128]{2,1,0:T(8,128)S(1)} %slice_add_fusion.45), channel_id=1, source_target_pairs={{0,8},{2,10},{4,12},{6,14},{8,0},{10,2},{12,4},{14,6},{1,9},{3,11}... | collective-permute-start | bytes 393224 | tf_op jit(solution)/shard_map/ppermute | solution.py:540
  95.2 14.7 %collective-permute-start.24 = (f32[128,8,128]{2,1,0:T(8,128)S(1)}, f32[128,8,128]{2,1,0:T(8,128)S(1)}, u32[]{:S(2)}, u32[]{:S(2)}) collective-permute-start(f32[128,8,128]{2,1,0:T(8,128)S(1)} %slice_add_fusion.1), channel_id=1, source_target_pairs={{0,2},{2,0},{4,6},{6,4},{8,10},{10,8},{12,14},{14,12},{1,3},{3,1},... | collective-permute-start | bytes 1572872 | tf_op jit(solution)/shard_map/ppermute | solution.py:540
  101.1 8.9 %collective-permute-start.23 = (f32[64,8,128]{2,1,0:T(8,128)S(1)}, f32[64,8,128]{2,1,0:T(8,128)S(1)}, u32[]{:S(2)}, u32[]{:S(2)}) collective-permute-start(f32[64,8,128]{2,1,0:T(8,128)S(1)} %slice_add_fusion.11), channel_id=1, source_target_pairs={{0,4},{2,6},{4,0},{6,2},{8,12},{10,14},{12,8},{14,10},{1,5},{3,7},... | collective-permute-start | bytes 786440 | tf_op jit(solution)/shard_map/ppermute | solution.py:540
  104.2 5.9 %collective-permute-start.22 = (f32[32,8,128]{2,1,0:T(8,128)S(1)}, f32[32,8,128]{2,1,0:T(8,128)S(1)}, u32[]{:S(2)}, u32[]{:S(2)}) collective-permute-start(f32[32,8,128]{2,1,0:T(8,128)S(1)} %slice_add_fusion.39), channel_id=1, source_target_pairs={{0,8},{2,10},{4,12},{6,14},{8,0},{10,2},{12,4},{14,6},{1,9},{3,11}... | collective-permute-start | bytes 393224 | tf_op jit(solution)/shard_map/ppermute | solution.py:540
  110.1 10.1 %collective-permute-start.26 = (f32[64,8,128]{2,1,0:T(8,128)S(1)}, f32[64,8,128]{2,1,0:T(8,128)S(1)}, u32[]{:S(2)}, u32[]{:S(2)}) collective-permute-start(f32[64,8,128]{2,1,0:T(8,128)S(1)} %slice_add_fusion.9), channel_id=1, source_target_pairs={{0,4},{2,6},{4,0},{6,2},{8,12},{10,14},{12,8},{14,10},{1,5},{3,7},... | collective-permute-start | bytes 786440 | tf_op jit(solution)/shard_map/ppermute | solution.py:540
  113.2 7.1 %collective-permute-start.25 = (f32[32,8,128]{2,1,0:T(8,128)S(1)}, f32[32,8,128]{2,1,0:T(8,128)S(1)}, u32[]{:S(2)}, u32[]{:S(2)}) collective-permute-start(f32[32,8,128]{2,1,0:T(8,128)S(1)} %slice_add_fusion.33), channel_id=1, source_target_pairs={{0,8},{2,10},{4,12},{6,14},{8,0},{10,2},{12,4},{14,6},{1,9},{3,11}... | collective-permute-start | bytes 393224 | tf_op jit(solution)/shard_map/ppermute | solution.py:540
  120.3 5.9 %collective-permute-start.27 = (f32[32,8,128]{2,1,0:T(8,128)S(1)}, f32[32,8,128]{2,1,0:T(8,128)S(1)}, u32[]{:S(2)}, u32[]{:S(2)}) collective-permute-start(f32[32,8,128]{2,1,0:T(8,128)S(1)} %slice_add_fusion.27), channel_id=1, source_target_pairs={{0,8},{2,10},{4,12},{6,14},{8,0},{10,2},{12,4},{14,6},{1,9},{3,11}... | collective-permute-start | bytes 393224 | tf_op jit(solution)/shard_map/ppermute | solution.py:540
  123.1 4.0 %copy-start.3 = (s32[32,128]{1,0:T(8,128)S(1)}, s32[32,128]{1,0:T(8,128)}, u32[]{:S(2)}) copy-start(s32[32,128]{1,0:T(8,128)} %refs_2_.7) | copy-start | bytes 49156
  123.1 4.0 %copy-start.5 = (s32[32]{0:T(128)S(1)}, s32[32]{0:T(128)}, u32[]{:S(2)}) copy-start(s32[32]{0:T(128)} %refs_1_.4) | copy-start | bytes 388
  128.6 8.4 %collective-permute-start.28 = (f32[30,8,128]{2,1,0:T(8,128)S(1)}, f32[30,8,128]{2,1,0:T(8,128)S(1)}, u32[]{:S(2)}, u32[]{:S(2)}) collective-permute-start(f32[30,8,128]{2,1,0:T(8,128)S(1)} %get-tuple-element.92), channel_id=1, source_target_pairs={{0,2},{2,0},{4,6},{6,4},{8,10},{10,8},{12,14},{14,12},{1,3},{3,1},... | collective-permute-start | bytes 368648 | tf_op jit(solution)/shard_map/ppermute | solution.py:618
  130.3 10.5 %collective-permute-start.29 = (f32[30,8,128]{2,1,0:T(8,128)S(1)}, f32[30,8,128]{2,1,0:T(8,128)S(1)}, u32[]{:S(2)}, u32[]{:S(2)}) collective-permute-start(f32[30,8,128]{2,1,0:T(8,128)S(1)} %get-tuple-element.94), channel_id=1, source_target_pairs={{0,4},{2,6},{4,0},{6,2},{8,12},{10,14},{12,8},{14,10},{1,5},{3,7},... | collective-permute-start | bytes 368648 | tf_op jit(solution)/shard_map/ppermute | solution.py:618
  133.1 11.6 %collective-permute-start.30 = (f32[30,8,128]{2,1,0:T(8,128)S(1)}, f32[30,8,128]{2,1,0:T(8,128)S(1)}, u32[]{:S(2)}, u32[]{:S(2)}) collective-permute-start(f32[30,8,128]{2,1,0:T(8,128)S(1)} %get-tuple-element.96), channel_id=1, source_target_pairs={{0,6},{2,4},{4,2},{6,0},{8,14},{10,12},{12,10},{14,8},{1,7},{3,5},... | collective-permute-start | bytes 368648 | tf_op jit(solution)/shard_map/ppermute | solution.py:618
  133.2 14.8 %collective-permute-start.31 = (f32[30,8,128]{2,1,0:T(8,128)S(1)}, f32[30,8,128]{2,1,0:T(8,128)S(1)}, u32[]{:S(2)}, u32[]{:S(2)}) collective-permute-start(f32[30,8,128]{2,1,0:T(8,128)S(1)} %get-tuple-element.98), channel_id=1, source_target_pairs={{0,8},{2,10},{4,12},{6,14},{8,0},{10,2},{12,4},{14,6},{1,9},{3,11}... | collective-permute-start | bytes 368648 | tf_op jit(solution)/shard_map/ppermute | solution.py:618
  135.6 16.1 %collective-permute-start.32 = (f32[30,8,128]{2,1,0:T(8,128)S(1)}, f32[30,8,128]{2,1,0:T(8,128)S(1)}, u32[]{:S(2)}, u32[]{:S(2)}) collective-permute-start(f32[30,8,128]{2,1,0:T(8,128)S(1)} %get-tuple-element.100), channel_id=1, source_target_pairs={{0,10},{2,8},{4,14},{6,12},{8,2},{10,0},{12,6},{14,4},{1,11},{3,9}... | collective-permute-start | bytes 368648 | tf_op jit(solution)/shard_map/ppermute | solution.py:618
  137.0 14.7 %collective-permute-start.33 = (f32[30,8,128]{2,1,0:T(8,128)S(1)}, f32[30,8,128]{2,1,0:T(8,128)S(1)}, u32[]{:S(2)}, u32[]{:S(2)}) collective-permute-start(f32[30,8,128]{2,1,0:T(8,128)S(1)} %get-tuple-element.102), channel_id=1, source_target_pairs={{0,12},{2,14},{4,8},{6,10},{8,4},{10,6},{12,0},{14,2},{1,13},{3,15... | collective-permute-start | bytes 368648 | tf_op jit(solution)/shard_map/ppermute | solution.py:618
  140.8 10.9 %collective-permute-start.34 = (f32[30,8,128]{2,1,0:T(8,128)S(1)}, f32[30,8,128]{2,1,0:T(8,128)S(1)}, u32[]{:S(2)}, u32[]{:S(2)}) collective-permute-start(f32[30,8,128]{2,1,0:T(8,128)S(1)} %get-tuple-element.104), channel_id=1, source_target_pairs={{0,14},{2,12},{4,10},{6,8},{8,6},{10,4},{12,2},{14,0},{1,15},{3,13... | collective-permute-start | bytes 368648 | tf_op jit(solution)/shard_map/ppermute | solution.py:618
  153.2 1.6 %collective-permute-start.35 = (f32[58,8,128]{2,1,0:T(8,128)S(1)}, f32[58,8,128]{2,1,0:T(8,128)S(1)}, u32[]{:S(2)}, u32[]{:S(2)}) collective-permute-start(f32[58,8,128]{2,1,0:T(8,128)S(1)} %get-tuple-element.107), channel_id=1, source_target_pairs={{0,1},{1,0},{2,3},{3,2},{4,5},{5,4},{6,7},{7,6},{8,9},{9,8},{10,11... | collective-permute-start | bytes 712712 | tf_op jit(solution)/shard_map/ppermute | solution.py:537

commit v4 on v3

--- a/solution.py
+++ b/solution.py
@@ -156,14 +156,7 @@
 TILE = 8
 UNROLL = 8
 WIDTHS = (8, 8, 8, 8, 8, 8)
-FOLDS = ((0,), (1, 2, 3), (4, 5, 6))
-GROUPS = {8: (0, 1, 2, 3, 4, 5, 6)}
-WAIT_FETCH = False
-LOOSE = -9
-EARLY_ONE = True
-PHASE0 = False
-TIES = 1
-HEAD = 1
+LINE_FIRST = {0: 1, 3: 2}
 
 
 def tile_count(width, slots):
@@ -204,8 +197,9 @@
 
 def child_kernel(first, widths, regions, slots, *refs):
     geometry = first == 0
+    colour_total = max(first + sum(widths) - max(first, 10), 0)
     place_ref, live_ref = refs[:2]
-    count = 4 if geometry else 3
+    count = 2 + 2 * geometry + (colour_total > 0)
     sources = refs[2 : 2 + count]
     refs = refs[2 + count :]
     out_refs, refs = refs[: 2 * len(widths)], refs[2 * len(widths) :]
@@ -214,22 +208,26 @@
     moments, totals, load_sems, out_sems = refs[count:]
     block_count, row_count = rows_ref.shape
     width = sum(widths)
-    full, extra = width // TILE, width % TILE
     sizes = [tile_count(part, slots) for part in widths]
     starts = [2 * regions * sum(sizes[:at]) for at in range(len(sizes))]
     tiles = [(at, tile) for at, part in enumerate(widths) for tile in range(part // TILE)]
+    bases = [first + sum(widths[:at]) for at in range(len(widths))]
+    components = [bases[at] + tile * TILE + line for at, tile in tiles for line in range(TILE)]
+    full, extra = len(tiles), 0
+    for at, part in enumerate(widths):
+        if part % TILE:
+            extra, shared = part % TILE, at
+            components += [bases[at] + part - extra + line % extra for line in range(TILE)]
     group = 16
     first_colour = max(first, 10) - 10
-    colour_total = 0 if geometry else width
     loads = []
     for at, (source, target) in enumerate(zip(sources, targets, strict=True)):
-        if colour_total and at == 2:
+        if colour_total and at == count - 1:
             source = source.at[pl.ds(first_colour, colour_total)]
         loads.append(pltpu.make_async_copy(source, target, load_sems.at[at]))
     if geometry:
         mean_ref, factor_ref = targets[2:4]
-    else:
-        colours = targets[2]
+    colours = targets[-1]
     for load in loads:
         load.start()
 
@@ -264,8 +262,7 @@
                 values[4 + entry] = weight * (spread[entry] + centre[left] * centre[right])
         for entry in range(colour_total):
             values[10 + first_colour + entry] = weight * colours[entry, part, :].astype(jnp.float32)
-        for place in range(full * TILE + (TILE if extra else 0)):
-            component = first + (place if place < full * TILE else full * TILE + place % extra)
+        for place, component in enumerate(components):
             moments[pl.ds(place * block_count + start, group), :] = values[component]
         return carry
 
@@ -292,7 +289,7 @@
                 spot = starts[at] + region * sizes[at] + tile * slots + slot
                 totals[spot] += result[line * TILE : (line + 1) * TILE]
             if extra:
-                spot = starts[-1] + region * sizes[-1] + (widths[-1] // TILE) * slots
+                spot = starts[shared] + region * sizes[shared] + (widths[shared] // TILE) * slots
                 totals[spot + slot // (TILE // extra)] += result[full * TILE :]
         return carry
 
@@ -311,8 +308,10 @@
 
 def fold_children(place, live, arrays, first, widths, regions, slots, vmem):
     rows, weight, mean, factor, colour = arrays
-    geometry = first == 0
-    used = [rows, weight, mean, factor] if geometry else [rows, weight, colour]
+    colour_total = max(first + sum(widths) - max(first, 10), 0)
+    used = [rows, weight] + ([mean, factor] if first == 0 else [])
+    if colour_total:
+        used.append(colour)
     block_count, row_count = rows.shape
     width = sum(widths)
     sizes = [tile_count(part, slots) for part in widths]
@@ -324,10 +323,9 @@
     ]
     scalars = pl.BlockSpec(memory_space=pltpu.SMEM)
     outside = pl.BlockSpec(memory_space=pl.ANY)
-    targets = [
-        pltpu.VMEM(array.shape if geometry or at < 2 else (width,) + array.shape[1:], array.dtype)
-        for at, array in enumerate(used)
-    ]
+    targets = [pltpu.VMEM(array.shape, array.dtype) for array in used]
+    if colour_total:
+        targets[-1] = pltpu.VMEM((colour_total,) + colour.shape[1:], colour.dtype)
 
     def kernel(*refs):
         child_kernel(first, widths, regions, slots, *refs)
@@ -561,9 +559,8 @@
         if others:
             place = after(place, *others)
         widths = [chunks[at][1] for at in group]
-        vmem = 56 if group[0] < HEAD else 40
         halves = fold_children(
-            place, live_blocks, arrays, chunks[group[0]][0], widths, spans, PB_DEV, vmem
+            place, live_blocks, arrays, chunks[group[0]][0], widths, spans, PB_DEV, 56
         )
         for turn, at in enumerate(group):
             terms[at] = [halves[2 * turn], swap(halves[2 * turn + 1])]
@@ -619,44 +616,59 @@
             for away, part in enumerate(parts)
         ]
         fetched.append(parts[-1])
-        if EARLY_ONE and group[-1] == total - 1:
-            level_one.append(merged_parts(unpack_one()))
-            parts = [after(part, level_one[0]) for part in parts]
+        level_one.append(merged_parts(unpack_one()))
+        parts = [after(part, level_one[0]) for part in parts]
         placed = place_parents(sub_at, codes[0], parts, widths, spans, cap_two, GB_DEV)
         if codes[0] is None:
             codes[0] = placed[2]
         level_two.extend(unpack(placed[0] + swap(placed[1]), widths, GB_DEV))
 
-    fold(FOLDS[0])
-    fold(FOLDS[1], terms[FOLDS[0][0]][0])
-    ready_sends = [depart_alone(at, 0) for at in range(2)]
-    for turn in range(2, len(FOLDS)):
-        fold(FOLDS[turn], terms[FOLDS[turn - 1][0]][0], *ready_sends[: turn - 1 + TIES])
+    fold(list(range(total)))
+    depart_alone(0, 0)
+    depart_alone(1, 0)
     sums = [None] * total
-    for phase in range(total + levels - 2):
+    last, size = total - 1, sizes[total - 1]
+    lines = []
+
+    def here(*regions):
+        return jnp.concatenate([part(last, region, region + 1) for region in regions], 0)
+
+    def line_send(step):
+        if step == 0:
+            return here(2, 3, 6, 7)
+        if step == 1:
+            return here(1, 5) + jnp.concatenate([lines[0][size : 2 * size], lines[0][3 * size :]], 0)
+        return here(4) + lines[0][2 * size : 3 * size] + lines[1][size:]
+
+    def line_depart(step, send):
+        lines.append(cross(send, (1, 2, 0)[step]))
+        if step == 2:
+            sums[last] = here(0) + lines[0][:size] + lines[1][:size] + lines[2]
+
+    line_depart(0, line_send(0))
+    for phase in range(last + levels - 2):
         moves, done = [], []
-        if phase + 2 < total:
+        if phase + 2 < last:
             moves.append((phase + 2, 0))
         for turn in range(levels - 1):
-            if 0 <= phase - turn < total:
+            if 0 <= phase - turn < last:
                 moves.append((phase - turn, turn + 1))
         if phase >= levels - 1:
             done.append(terms[phase - levels + 1][-1])
-        if phase == 0 and PHASE0:
-            done.append(terms[total - 1][1])
-        if WAIT_FETCH:
-            done += fetched[-1:]
         ready = [send_of(at, level) for at, level in moves]
-        if phase < total - LOOSE:
-            ready = lax.optimization_barrier(tuple(ready + done))[: len(ready)]
+        if phase in LINE_FIRST:
+            moves.append((last, LINE_FIRST[phase]))
+            ready.append(line_send(LINE_FIRST[phase]))
+        ready = lax.optimization_barrier(tuple(ready + done))[: len(ready)]
         for (at, level), send in zip(moves, ready, strict=True):
+            if at == last:
+                line_depart(level, send)
+                continue
             depart(at, level, send)
             if level == levels - 1:
                 sums[at] = part(at, 0, 1)
-        if phase in GROUPS:
-            raise_level(GROUPS[phase], *ready)
-    raise_level(GROUPS[total + levels - 2])
-    return (level_one[0] if level_one else merged_parts(unpack_one()), merged_parts(level_two))
+    raise_level(list(range(total)))
+    return (level_one[0], merged_parts(level_two))
 
 
 def body(*arrays):

time: 159 us -> 151 us (0.950)
  Pallas kernels: 24.1 us -> 16.1 us
  waiting for transfers between devices: 55.8 us -> 62.4 us
  starting transfers between devices: 61.6 us -> 55.1 us
  local copies, waits for them, and re-layouts: 9.49 us -> 5.79 us
  other arithmetic: 3.85 us -> 6.77 us
    ppermute x21, waiting for transfers between devices: 48.8 us -> 57.5 us  [cross(): lax.ppermute(values, 'span', [(at, at ^ 1 << bit) for at in range(spans)])]
    pallas_call x3 -> x1, Pallas kernels: 21.1 us -> 13 us  [fold_children(): pl.pallas_call(kernel, out_shape=halves, in_specs=[scalars, scalars] + [o...]
    ppermute x21, starting transfers between devices: 46.8 us -> 39.5 us  [cross(): lax.ppermute(values, 'span', [(at, at ^ 1 << bit) for at in range(spans)])]
    unnamed x18 -> x22, local copies, waits for them, and re-layouts: 6.08 us -> 2.36 us
    ppermute x7, waiting for transfers between devices: 6.97 us -> 3.61 us  [raise_level(): lax.ppermute(part, 'span', [(at, at ^ away) for at in range(spans)])]
  transfers between devices with their start and end apart: 36 -> 36, of which waited for: 15 -> 15; matrix products, arithmetic and copies ran while one was open for 4% -> 6% of each run, Pallas kernels for 9% -> 0%
where the time goes in v4:
time: 151 us; the launch traced here: 148 us
  waiting for transfers between devices  62.4 us (41%)
  starting transfers between devices  55.1 us (36%)
  Pallas kernels  16.1 us (11%)
  other arithmetic  6.77 us (4%)
  local copies, waits for them, and re-layouts  5.79 us (4%)
  between operations  1.72 us (1%)
    ppermute x21, waiting for transfers between devices, cross(): lax.ppermute(values, 'span', [(at, at ^ 1 << bit) for at in range(spans)])  57.5 us
    ppermute x21, starting transfers between devices, cross(): lax.ppermute(values, 'span', [(at, at ^ 1 << bit) for at in range(spans)])  39.5 us
    ppermute x7, starting transfers between devices, raise_level(): lax.ppermute(part, 'span', [(at, at ^ away) for at in range(spans)])  13.5 us
    pallas_call x1, Pallas kernels, fold_children(): pl.pallas_call(kernel, out_shape=halves, in_specs=[scalars, scalars] + [o...  13 us
    ppermute x7, waiting for transfers between devices, raise_level(): lax.ppermute(part, 'span', [(at, at ^ away) for at in range(spans)])  3.61 us
    concatenate x2, local copies, waits for them, and re-layouts, merged_parts(): return jnp.concatenate([sums[:1], centre, spread] + rest, 0)  3.17 us
  transfers between devices with their start and end apart: 36, of which 15 were waited for; matrix products, arithmetic and copies ran while one was open for 6% of the time, Pallas kernels for 0%

profile of v4, /device:TPU:0, one launch (start us, length us, event | category | flops | bytes accessed | tf_op | source)
XLA Modules:
  0.0 147.8 jit_solution(10766826156871339148)
XLA Ops:
  1.3 1.2 fusion.20.refs_0_
  2.5 13.0 %fold_children.1 = (f32[320,8,128]{2,1,0:T(8,128)}, f32[320,8,128]{2,1,0:T(8,128)}, f32[256,8,128]{2,1,0:T(8,128)}, f32[256,8,128]{2,1,0:T(8,128)}, f32[256,8,12...) custom-call(s32[128]{0:T(128)} %fusion.20.refs_0_, ...), custom_call_target="tpu_custom_call" | custom-call | flops 1024 | bytes 1024 | tf_op jit(solution)/shard_map/fold_children/pallas_call | solution.py:333
  17.3 1.3 collective-permute-done.3
  18.9 1.4 slice_add_fusion.63
  20.4 3.6 %collective-permute-start.4 = (f32[128,8,128]{2,1,0:T(8,128)S(1)}, f32[128,8,128]{2,1,0:T(8,128)S(1)}, u32[]{:S(2)}, u32[]{:S(2)}) collective-permute-start(f32[128,8,128]{2,1,0:T(8,128)S(1)} %pad_maximum_fusion), channel_id=1, source_target_pairs={{0,4},{2,6},{4,0},{6,2},{8,12},{10,14},{12,8},{14,10},{1,5},{3,7},... | collective-permute-start | bytes 1572872 | tf_op jit(solution)/shard_map/ppermute | solution.py:538
  24.2 1.6 %collective-permute-start.1 = (f32[160,8,128]{2,1,0:T(8,128)S(1)}, f32[160,8,128]{2,1,0:T(8,128)S(1)}, u32[]{:S(2)}, u32[]{:S(2)}) collective-permute-start(f32[160,8,128]{2,1,0:T(8,128)S(1)} %slice_add_fusion), channel_id=1, source_target_pairs={{0,2},{2,0},{4,6},{6,4},{8,10},{10,8},{12,14},{14,12},{1,3},{3,1},... | collective-permute-start | bytes 1966088 | tf_op jit(solution)/shard_map/ppermute | solution.py:538
  26.0 10.4 %collective-permute-done.4 = f32[128,8,128]{2,1,0:T(8,128)S(1)} collective-permute-done((f32[128,8,128]{2,1,0:T(8,128)S(1)}, f32[128,8,128]{2,1,0:T(8,128)S(1)}, u32[]{:S(2)}, u32[]{:S(2)}) %collective-permute-start.4) | collective-permute-done | bytes 524320 | tf_op jit(solution)/shard_map/ppermute | solution.py:538
  36.3 1.5 %collective-permute-start.8 = (f32[128,8,128]{2,1,0:T(8,128)S(1)}, f32[128,8,128]{2,1,0:T(8,128)S(1)}, u32[]{:S(2)}, u32[]{:S(2)}) collective-permute-start(f32[128,8,128]{2,1,0:T(8,128)S(1)} %slice_add_fusion.3), channel_id=1, source_target_pairs={{0,2},{2,0},{4,6},{6,4},{8,10},{10,8},{12,14},{14,12},{1,3},{3,1},... | collective-permute-start | bytes 1572872 | tf_op jit(solution)/shard_map/ppermute | solution.py:538
  37.9 3.9 %collective-permute-done.1 = f32[160,8,128]{2,1,0:T(8,128)S(1)} collective-permute-done((f32[160,8,128]{2,1,0:T(8,128)S(1)}, f32[160,8,128]{2,1,0:T(8,128)S(1)}, u32[]{:S(2)}, u32[]{:S(2)}) %collective-permute-start.1) | collective-permute-done | bytes 655392 | tf_op jit(solution)/shard_map/ppermute | solution.py:538
  41.9 1.4 collective-permute-start.5
  43.3 1.6 %collective-permute-start.12 = (f32[128,8,128]{2,1,0:T(8,128)S(1)}, f32[128,8,128]{2,1,0:T(8,128)S(1)}, u32[]{:S(2)}, u32[]{:S(2)}) collective-permute-start(f32[128,8,128]{2,1,0:T(8,128)S(1)} %slice_add_fusion.5), channel_id=1, source_target_pairs={{0,2},{2,0},{4,6},{6,4},{8,10},{10,8},{12,14},{14,12},{1,3},{3,1},... | collective-permute-start | bytes 1572872 | tf_op jit(solution)/shard_map/ppermute | solution.py:538
  44.9 8.2 %collective-permute-done.8 = f32[128,8,128]{2,1,0:T(8,128)S(1)} collective-permute-done((f32[128,8,128]{2,1,0:T(8,128)S(1)}, f32[128,8,128]{2,1,0:T(8,128)S(1)}, u32[]{:S(2)}, u32[]{:S(2)}) %collective-permute-start.8) | collective-permute-done | bytes 524320 | tf_op jit(solution)/shard_map/ppermute | solution.py:538
  53.2 1.4 collective-permute-start.10
  54.6 2.1 %collective-permute-start.17 = (f32[64,8,128]{2,1,0:T(8,128)S(1)}, f32[64,8,128]{2,1,0:T(8,128)S(1)}, u32[]{:S(2)}, u32[]{:S(2)}) collective-permute-start(f32[64,8,128]{2,1,0:T(8,128)S(1)} %maximum_add_fusion), channel_id=1, source_target_pairs={{0,8},{2,10},{4,12},{6,14},{8,0},{10,2},{12,4},{14,6},{1,9},{3,11}... | collective-permute-start | bytes 786440 | tf_op jit(solution)/shard_map/ppermute | solution.py:538
  56.7 0.9 collective-permute-start.9
  57.6 5.6 %collective-permute-done.12 = f32[128,8,128]{2,1,0:T(8,128)S(1)} collective-permute-done((f32[128,8,128]{2,1,0:T(8,128)S(1)}, f32[128,8,128]{2,1,0:T(8,128)S(1)}, u32[]{:S(2)}, u32[]{:S(2)}) %collective-permute-start.12) | collective-permute-done | bytes 524320 | tf_op jit(solution)/shard_map/ppermute | solution.py:538
  63.2 1.5 %collective-permute-start.16 = (f32[128,8,128]{2,1,0:T(8,128)S(1)}, f32[128,8,128]{2,1,0:T(8,128)S(1)}, u32[]{:S(2)}, u32[]{:S(2)}) collective-permute-start(f32[128,8,128]{2,1,0:T(8,128)S(1)} %slice_add_fusion.4), channel_id=1, source_target_pairs={{0,2},{2,0},{4,6},{6,4},{8,10},{10,8},{12,14},{14,12},{1,3},{3,1},... | collective-permute-start | bytes 1572872 | tf_op jit(solution)/shard_map/ppermute | solution.py:538
  64.8 9.9 %collective-permute-done.9 = f32[40,8,128]{2,1,0:T(8,128)S(1)} collective-permute-done((f32[40,8,128]{2,1,0:T(8,128)S(1)}, f32[40,8,128]{2,1,0:T(8,128)S(1)}, u32[]{:S(2)}, u32[]{:S(2)}) %collective-permute-start.9) | collective-permute-done | bytes 163872 | tf_op jit(solution)/shard_map/ppermute | solution.py:538
  74.8 0.9 slice_add_fusion.45
  75.8 2.9 %collective-permute-start.13 = (f32[32,8,128]{2,1,0:T(8,128)S(1)}, f32[32,8,128]{2,1,0:T(8,128)S(1)}, u32[]{:S(2)}, u32[]{:S(2)}) collective-permute-start(f32[32,8,128]{2,1,0:T(8,128)S(1)} %slice_add_fusion.54), channel_id=1, source_target_pairs={{0,8},{2,10},{4,12},{6,14},{8,0},{10,2},{12,4},{14,6},{1,9},{3,11}... | collective-permute-start | bytes 393224 | tf_op jit(solution)/shard_map/ppermute | solution.py:538
  78.7 1.3 collective-permute-start.20
  80.0 3.8 %collective-permute-done.14 = f32[64,8,128]{2,1,0:T(8,128)S(1)} collective-permute-done((f32[64,8,128]{2,1,0:T(8,128)S(1)}, f32[64,8,128]{2,1,0:T(8,128)S(1)}, u32[]{:S(2)}, u32[]{:S(2)}) %collective-permute-start.14) | collective-permute-done | bytes 262176 | tf_op jit(solution)/shard_map/ppermute | solution.py:538
  84.8 1.3 collective-permute-start.23
  86.0 2.5 %collective-permute-start.18 = (f32[32,8,128]{2,1,0:T(8,128)S(1)}, f32[32,8,128]{2,1,0:T(8,128)S(1)}, u32[]{:S(2)}, u32[]{:S(2)}) collective-permute-start(f32[32,8,128]{2,1,0:T(8,128)S(1)} %slice_add_fusion.48), channel_id=1, source_target_pairs={{0,8},{2,10},{4,12},{6,14},{8,0},{10,2},{12,4},{14,6},{1,9},{3,11}... | collective-permute-start | bytes 393224 | tf_op jit(solution)/shard_map/ppermute | solution.py:538
  88.6 4.9 %collective-permute-done.20 = f32[128,8,128]{2,1,0:T(8,128)S(1)} collective-permute-done((f32[128,8,128]{2,1,0:T(8,128)S(1)}, f32[128,8,128]{2,1,0:T(8,128)S(1)}, u32[]{:S(2)}, u32[]{:S(2)}) %collective-permute-start.20) | collective-permute-done | bytes 524320 | tf_op jit(solution)/shard_map/ppermute | solution.py:538
  93.6 1.3 collective-permute-start.22
  94.9 3.3 %collective-permute-start.21 = (f32[32,8,128]{2,1,0:T(8,128)S(1)}, f32[32,8,128]{2,1,0:T(8,128)S(1)}, u32[]{:S(2)}, u32[]{:S(2)}) collective-permute-start(f32[32,8,128]{2,1,0:T(8,128)S(1)} %slice_add_fusion.39), channel_id=1, source_target_pairs={{0,8},{2,10},{4,12},{6,14},{8,0},{10,2},{12,4},{14,6},{1,9},{3,11}... | collective-permute-start | bytes 393224 | tf_op jit(solution)/shard_map/ppermute | solution.py:538
  98.2 3.2 %collective-permute-done.23 = f32[128,8,128]{2,1,0:T(8,128)S(1)} collective-permute-done((f32[128,8,128]{2,1,0:T(8,128)S(1)}, f32[128,8,128]{2,1,0:T(8,128)S(1)}, u32[]{:S(2)}, u32[]{:S(2)}) %collective-permute-start.23) | collective-permute-done | bytes 524320 | tf_op jit(solution)/shard_map/ppermute | solution.py:538
  102.1 4.7 %collective-permute-start.25 = (f32[64,8,128]{2,1,0:T(8,128)S(1)}, f32[64,8,128]{2,1,0:T(8,128)S(1)}, u32[]{:S(2)}, u32[]{:S(2)}) collective-permute-start(f32[64,8,128]{2,1,0:T(8,128)S(1)} %slice_add_fusion.8), channel_id=1, source_target_pairs={{0,4},{2,6},{4,0},{6,2},{8,12},{10,14},{12,8},{14,10},{1,5},{3,7},... | collective-permute-start | bytes 786440 | tf_op jit(solution)/shard_map/ppermute | solution.py:538
  107.4 2.7 %collective-permute-start.24 = (f32[32,8,128]{2,1,0:T(8,128)S(1)}, f32[32,8,128]{2,1,0:T(8,128)S(1)}, u32[]{:S(2)}, u32[]{:S(2)}) collective-permute-start(f32[32,8,128]{2,1,0:T(8,128)S(1)} %slice_add_fusion.33), channel_id=1, source_target_pairs={{0,8},{2,10},{4,12},{6,14},{8,0},{10,2},{12,4},{14,6},{1,9},{3,11}... | collective-permute-start | bytes 393224 | tf_op jit(solution)/shard_map/ppermute | solution.py:538
  110.1 3.0 %collective-permute-done.25 = f32[64,8,128]{2,1,0:T(8,128)S(1)} collective-permute-done((f32[64,8,128]{2,1,0:T(8,128)S(1)}, f32[64,8,128]{2,1,0:T(8,128)S(1)}, u32[]{:S(2)}, u32[]{:S(2)}) %collective-permute-start.25) | collective-permute-done | bytes 262176 | tf_op jit(solution)/shard_map/ppermute | solution.py:538
  113.2 1.0 collective-permute-done.24
  114.1 2.8 %collective-permute-start.26 = (f32[32,8,128]{2,1,0:T(8,128)S(1)}, f32[32,8,128]{2,1,0:T(8,128)S(1)}, u32[]{:S(2)}, u32[]{:S(2)}) collective-permute-start(f32[32,8,128]{2,1,0:T(8,128)S(1)} %slice_add_fusion.27), channel_id=1, source_target_pairs={{0,8},{2,10},{4,12},{6,14},{8,0},{10,2},{12,4},{14,6},{1,9},{3,11}... | collective-permute-start | bytes 393224 | tf_op jit(solution)/shard_map/ppermute | solution.py:538
  116.9 1.0 bitcast_divide_fusion
  118.0 2.8 %collective-permute-done.26 = f32[32,8,128]{2,1,0:T(8,128)S(1)} collective-permute-done((f32[32,8,128]{2,1,0:T(8,128)S(1)}, f32[32,8,128]{2,1,0:T(8,128)S(1)}, u32[]{:S(2)}, u32[]{:S(2)}) %collective-permute-start.26) | collective-permute-done | bytes 131104 | tf_op jit(solution)/shard_map/ppermute | solution.py:538
  121.6 1.6 %fold_parents.1 = (f32[30,8,128]{2,1,0:T(8,128)S(1)}, f32[30,8,128]{2,1,0:T(8,128)S(1)}, f32[30,8,128]{2,1,0:T(8,128)S(1)}, f32[30,8,128]{2,1,0:T(8,128)S(1)}, f...) custom-call(s32[32]{0:T(128)S(1)} %multiply_add_fusion.refs_0_, ...), custom_call_target="tpu_custom_call" | custom-call | flops 1024 | bytes 1024 | tf_op jit(solution)/shard_map/fold_parents/pallas_call | solution.py:403
  123.2 4.2 %collective-permute-start.28 = (f32[30,8,128]{2,1,0:T(8,128)S(1)}, f32[30,8,128]{2,1,0:T(8,128)S(1)}, u32[]{:S(2)}, u32[]{:S(2)}) collective-permute-start(f32[30,8,128]{2,1,0:T(8,128)S(1)} %get-tuple-element.86), channel_id=1, source_target_pairs={{0,2},{2,0},{4,6},{6,4},{8,10},{10,8},{12,14},{14,12},{1,3},{3,1},... | collective-permute-start | bytes 368648 | tf_op jit(solution)/shard_map/ppermute | solution.py:615
  127.6 1.6 %collective-permute-start.30 = (f32[30,8,128]{2,1,0:T(8,128)S(1)}, f32[30,8,128]{2,1,0:T(8,128)S(1)}, u32[]{:S(2)}, u32[]{:S(2)}) collective-permute-start(f32[30,8,128]{2,1,0:T(8,128)S(1)} %get-tuple-element.90), channel_id=1, source_target_pairs={{0,6},{2,4},{4,2},{6,0},{8,14},{10,12},{12,10},{14,8},{1,7},{3,5},... | collective-permute-start | bytes 368648 | tf_op jit(solution)/shard_map/ppermute | solution.py:615
  129.2 1.2 collective-permute-start.31
  130.4 3.2 %collective-permute-start.32 = (f32[30,8,128]{2,1,0:T(8,128)S(1)}, f32[30,8,128]{2,1,0:T(8,128)S(1)}, u32[]{:S(2)}, u32[]{:S(2)}) collective-permute-start(f32[30,8,128]{2,1,0:T(8,128)S(1)} %get-tuple-element.94), channel_id=1, source_target_pairs={{0,10},{2,8},{4,14},{6,12},{8,2},{10,0},{12,6},{14,4},{1,11},{3,9}... | collective-permute-start | bytes 368648 | tf_op jit(solution)/shard_map/ppermute | solution.py:615
  133.5 1.3 collective-permute-start.33
  134.8 2.1 %collective-permute-start.34 = (f32[30,8,128]{2,1,0:T(8,128)S(1)}, f32[30,8,128]{2,1,0:T(8,128)S(1)}, u32[]{:S(2)}, u32[]{:S(2)}) collective-permute-start(f32[30,8,128]{2,1,0:T(8,128)S(1)} %get-tuple-element.98), channel_id=1, source_target_pairs={{0,14},{2,12},{4,10},{6,8},{8,6},{10,4},{12,2},{14,0},{1,15},{3,13... | collective-permute-start | bytes 368648 | tf_op jit(solution)/shard_map/ppermute | solution.py:615
  136.9 2.4 %concatenate.25 = f32[58,32,128]{2,0,1:T(8,128)S(1)} concatenate(f32[1,32,128]{2,0,1:T(1,128)S(1)} %get-tuple-element.137, f32[3,32,128]{2,0,1:T(4,128)S(1)} %fusion.9, f32[6,32,128]{2,0,1:T(8,128)S(1)} %fusion.8, f32[8,32,128]{2,0,1:T(8,128)} %get-tuple-element.158, f32[8,32,128]{2,0,1:T(8,128)S(1)} %get-tuple-element.152, f32[8,32,128]{2,0,1:T(8,128)S(1)} %get-tuple-element.154, ...), dimensions={0} | concatenate | bytes 1900544 | tf_op jit(solution)/shard_map/concatenate | solution.py:496
  139.4 3.6 %collective-permute-done.32.refs_6_ = f32[30,8,128]{2,1,0:T(8,128)S(1)} collective-permute-done((f32[30,8,128]{2,1,0:T(8,128)S(1)}, f32[30,8,128]{2,1,0:T(8,128)S(1)}, u32[]{:S(2)}, u32[]{:S(2)}) %collective-permute-start.32) | collective-permute-done | bytes 122912 | tf_op jit(solution)/shard_map/ppermute | solution.py:615
  143.0 1.4 place_parents.1
  144.5 1.5 %copy.19 = f32[58,32,128]{2,1,0:T(8,128)} copy(f32[58,32,128]{2,0,1:T(8,128)S(1)} %concatenate.25) | data formatting | bytes 1900544
  146.2 0.8 concatenate.27
  147.0 0.8 copy.20
  (96 shorter events, 6.6 us)
Async XLA Ops:
  0.6 16.5 %copy-start.8 = (s32[32]{0:T(128)S(1)}, s32[32]{0:T(128)}, u32[]{:S(2)}) copy-start(s32[32]{0:T(128)} %param.19) | copy-start | bytes 388
  15.6 3.0 %collective-permute-start.3 = (f32[256,8,128]{2,1,0:T(8,128)}, f32[256,8,128]{2,1,0:T(8,128)S(1)}, u32[]{:S(2)}, u32[]{:S(2)}) collective-permute-start(f32[256,8,128]{2,1,0:T(8,128)} %get-tuple-element.57), channel_id=1, source_target_pairs={{0,1},{1,0},{2,3},{3,2},{4,5},{5,4},{6,7},{7,6},{8,9},{9,8},{10,11... | collective-permute-start | bytes 3145736 | tf_op jit(solution)/shard_map/ppermute | solution.py:535
  16.1 4.4 %collective-permute-start = (f32[320,8,128]{2,1,0:T(8,128)}, f32[320,8,128]{2,1,0:T(8,128)S(1)}, u32[]{:S(2)}, u32[]{:S(2)}) collective-permute-start(f32[320,8,128]{2,1,0:T(8,128)} %get-tuple-element.53), channel_id=1, source_target_pairs={{0,1},{1,0},{2,3},{3,2},{4,5},{5,4},{6,7},{7,6},{8,9},{9,8},{10,11... | collective-permute-start | bytes 3932168 | tf_op jit(solution)/shard_map/ppermute | solution.py:535
  16.2 8.0 %collective-permute-start.7 = (f32[256,8,128]{2,1,0:T(8,128)}, f32[256,8,128]{2,1,0:T(8,128)S(1)}, u32[]{:S(2)}, u32[]{:S(2)}) collective-permute-start(f32[256,8,128]{2,1,0:T(8,128)} %get-tuple-element.62), channel_id=1, source_target_pairs={{0,1},{1,0},{2,3},{3,2},{4,5},{5,4},{6,7},{7,6},{8,9},{9,8},{10,11... | collective-permute-start | bytes 3145736 | tf_op jit(solution)/shard_map/ppermute | solution.py:535
  16.6 26.7 %collective-permute-start.6 = (f32[256,8,128]{2,1,0:T(8,128)}, f32[256,8,128]{2,1,0:T(8,128)S(1)}, u32[]{:S(2)}, u32[]{:S(2)}) collective-permute-start(f32[256,8,128]{2,1,0:T(8,128)} %get-tuple-element.60), channel_id=1, source_target_pairs={{0,1},{1,0},{2,3},{3,2},{4,5},{5,4},{6,7},{7,6},{8,9},{9,8},{10,11... | collective-permute-start | bytes 3145736 | tf_op jit(solution)/shard_map/ppermute | solution.py:535
  16.7 9.1 %collective-permute-start.2 = (f32[256,8,128]{2,1,0:T(8,128)}, f32[256,8,128]{2,1,0:T(8,128)S(1)}, u32[]{:S(2)}, u32[]{:S(2)}) collective-permute-start(f32[256,8,128]{2,1,0:T(8,128)} %get-tuple-element.55), channel_id=1, source_target_pairs={{0,1},{1,0},{2,3},{3,2},{4,5},{5,4},{6,7},{7,6},{8,9},{9,8},{10,11... | collective-permute-start | bytes 3145736 | tf_op jit(solution)/shard_map/ppermute | solution.py:535
  18.6 56.2 %collective-permute-start.15 = (f32[256,8,128]{2,1,0:T(8,128)}, f32[256,8,128]{2,1,0:T(8,128)S(1)}, u32[]{:S(2)}, u32[]{:S(2)}) collective-permute-start(f32[256,8,128]{2,1,0:T(8,128)} %get-tuple-element.71), channel_id=1, source_target_pairs={{0,1},{1,0},{2,3},{3,2},{4,5},{5,4},{6,7},{7,6},{8,9},{9,8},{10,11... | collective-permute-start | bytes 3145736 | tf_op jit(solution)/shard_map/ppermute | solution.py:535
  18.9 5.1 %copy-start.2 = (f32[320,8,128]{2,1,0:T(8,128)S(1)}, f32[320,8,128]{2,1,0:T(8,128)}, u32[]{:S(2)}) copy-start(f32[320,8,128]{2,1,0:T(8,128)} %get-tuple-element.52) | copy-start | bytes 3932164
  20.4 5.4 %copy-start.3 = (f32[256,8,128]{2,1,0:T(8,128)S(1)}, f32[256,8,128]{2,1,0:T(8,128)}, u32[]{:S(2)}) copy-start(f32[256,8,128]{2,1,0:T(8,128)} %get-tuple-element.61) | copy-start | bytes 3145732
  20.4 15.9 %collective-permute-start.4 = (f32[128,8,128]{2,1,0:T(8,128)S(1)}, f32[128,8,128]{2,1,0:T(8,128)S(1)}, u32[]{:S(2)}, u32[]{:S(2)}) collective-permute-start(f32[128,8,128]{2,1,0:T(8,128)S(1)} %pad_maximum_fusion), channel_id=1, source_target_pairs={{0,4},{2,6},{4,0},{6,2},{8,12},{10,14},{12,8},{14,10},{1,5},{3,7},... | collective-permute-start | bytes 1572872 | tf_op jit(solution)/shard_map/ppermute | solution.py:538
  24.1 1.7 %copy-start.9 = (f32[256,8,128]{2,1,0:T(8,128)S(1)}, f32[256,8,128]{2,1,0:T(8,128)}, u32[]{:S(2)}) copy-start(f32[256,8,128]{2,1,0:T(8,128)} %get-tuple-element.66) | copy-start | bytes 3145732
  24.1 1.8 %copy-start.6 = (f32[256,8,128]{2,1,0:T(8,128)S(1)}, f32[256,8,128]{2,1,0:T(8,128)}, u32[]{:S(2)}) copy-start(f32[256,8,128]{2,1,0:T(8,128)} %get-tuple-element.54) | copy-start | bytes 3145732
  24.2 17.7 %collective-permute-start.1 = (f32[160,8,128]{2,1,0:T(8,128)S(1)}, f32[160,8,128]{2,1,0:T(8,128)S(1)}, u32[]{:S(2)}, u32[]{:S(2)}) collective-permute-start(f32[160,8,128]{2,1,0:T(8,128)S(1)} %slice_add_fusion), channel_id=1, source_target_pairs={{0,2},{2,0},{4,6},{6,4},{8,10},{10,8},{12,14},{14,12},{1,3},{3,1},... | collective-permute-start | bytes 1966088 | tf_op jit(solution)/shard_map/ppermute | solution.py:538
  25.8 28.8 %collective-permute-start.11 = (f32[256,8,128]{2,1,0:T(8,128)S(1)}, f32[256,8,128]{2,1,0:T(8,128)S(1)}, u32[]{:S(2)}, u32[]{:S(2)}) collective-permute-start(f32[256,8,128]{2,1,0:T(8,128)S(1)} %copy-done.9), channel_id=1, source_target_pairs={{0,1},{1,0},{2,3},{3,2},{4,5},{5,4},{6,7},{7,6},{8,9},{9,8},{10,11... | collective-permute-start | bytes 3145736 | tf_op jit(solution)/shard_map/ppermute | solution.py:535
  26.0 17.3 %copy-start.7 = (f32[256,8,128]{2,1,0:T(8,128)S(1)}, f32[256,8,128]{2,1,0:T(8,128)}, u32[]{:S(2)}) copy-start(f32[256,8,128]{2,1,0:T(8,128)} %get-tuple-element.59) | copy-start | bytes 3145732
  36.3 16.7 %collective-permute-start.8 = (f32[128,8,128]{2,1,0:T(8,128)S(1)}, f32[128,8,128]{2,1,0:T(8,128)S(1)}, u32[]{:S(2)}, u32[]{:S(2)}) collective-permute-start(f32[128,8,128]{2,1,0:T(8,128)S(1)} %slice_add_fusion.3), channel_id=1, source_target_pairs={{0,2},{2,0},{4,6},{6,4},{8,10},{10,8},{12,14},{14,12},{1,3},{3,1},... | collective-permute-start | bytes 1572872 | tf_op jit(solution)/shard_map/ppermute | solution.py:538
  41.9 11.2 %collective-permute-start.5 = (f32[80,8,128]{2,1,0:T(8,128)S(1)}, f32[80,8,128]{2,1,0:T(8,128)S(1)}, u32[]{:S(2)}, u32[]{:S(2)}) collective-permute-start(f32[80,8,128]{2,1,0:T(8,128)S(1)} %slice_add_fusion.6), channel_id=1, source_target_pairs={{0,4},{2,6},{4,0},{6,2},{8,12},{10,14},{12,8},{14,10},{1,5},{3,7},... | collective-permute-start | bytes 983048 | tf_op jit(solution)/shard_map/ppermute | solution.py:538
  43.3 11.2 %copy-start.4 = (f32[256,8,128]{2,1,0:T(8,128)S(1)}, f32[256,8,128]{2,1,0:T(8,128)}, u32[]{:S(2)}) copy-start(f32[256,8,128]{2,1,0:T(8,128)} %get-tuple-element.65) | copy-start | bytes 3145732
  43.3 19.9 %collective-permute-start.12 = (f32[128,8,128]{2,1,0:T(8,128)S(1)}, f32[128,8,128]{2,1,0:T(8,128)S(1)}, u32[]{:S(2)}, u32[]{:S(2)}) collective-permute-start(f32[128,8,128]{2,1,0:T(8,128)S(1)} %slice_add_fusion.5), channel_id=1, source_target_pairs={{0,2},{2,0},{4,6},{6,4},{8,10},{10,8},{12,14},{14,12},{1,3},{3,1},... | collective-permute-start | bytes 1572872 | tf_op jit(solution)/shard_map/ppermute | solution.py:538
  53.2 11.6 %collective-permute-start.10 = (f32[64,8,128]{2,1,0:T(8,128)S(1)}, f32[64,8,128]{2,1,0:T(8,128)S(1)}, u32[]{:S(2)}, u32[]{:S(2)}) collective-permute-start(f32[64,8,128]{2,1,0:T(8,128)S(1)} %slice_add_fusion.16), channel_id=1, source_target_pairs={{0,4},{2,6},{4,0},{6,2},{8,12},{10,14},{12,8},{14,10},{1,5},{3,7},... | collective-permute-start | bytes 786440 | tf_op jit(solution)/shard_map/ppermute | solution.py:538
  54.6 20.2 %copy-start.5 = (f32[256,8,128]{2,1,0:T(8,128)S(1)}, f32[256,8,128]{2,1,0:T(8,128)}, u32[]{:S(2)}) copy-start(f32[256,8,128]{2,1,0:T(8,128)} %get-tuple-element.70) | copy-start | bytes 3145732
  54.6 20.2 %collective-permute-start.17 = (f32[64,8,128]{2,1,0:T(8,128)S(1)}, f32[64,8,128]{2,1,0:T(8,128)S(1)}, u32[]{:S(2)}, u32[]{:S(2)}) collective-permute-start(f32[64,8,128]{2,1,0:T(8,128)S(1)} %maximum_add_fusion), channel_id=1, source_target_pairs={{0,8},{2,10},{4,12},{6,14},{8,0},{10,2},{12,4},{14,6},{1,9},{3,11}... | collective-permute-start | bytes 786440 | tf_op jit(solution)/shard_map/ppermute | solution.py:538
  56.7 18.0 %collective-permute-start.9 = (f32[40,8,128]{2,1,0:T(8,128)S(1)}, f32[40,8,128]{2,1,0:T(8,128)S(1)}, u32[]{:S(2)}, u32[]{:S(2)}) collective-permute-start(f32[40,8,128]{2,1,0:T(8,128)S(1)} %slice_add_fusion.18), channel_id=1, source_target_pairs={{0,8},{2,10},{4,12},{6,14},{8,0},{10,2},{12,4},{14,6},{1,9},{3,11}... | collective-permute-start | bytes 491528 | tf_op jit(solution)/shard_map/ppermute | solution.py:538
  63.2 20.6 %collective-permute-start.16 = (f32[128,8,128]{2,1,0:T(8,128)S(1)}, f32[128,8,128]{2,1,0:T(8,128)S(1)}, u32[]{:S(2)}, u32[]{:S(2)}) collective-permute-start(f32[128,8,128]{2,1,0:T(8,128)S(1)} %slice_add_fusion.4), channel_id=1, source_target_pairs={{0,2},{2,0},{4,6},{6,4},{8,10},{10,8},{12,14},{14,12},{1,3},{3,1},... | collective-permute-start | bytes 1572872 | tf_op jit(solution)/shard_map/ppermute | solution.py:538
  74.7 9.1 %collective-permute-start.14 = (f32[64,8,128]{2,1,0:T(8,128)S(1)}, f32[64,8,128]{2,1,0:T(8,128)S(1)}, u32[]{:S(2)}, u32[]{:S(2)}) collective-permute-start(f32[64,8,128]{2,1,0:T(8,128)S(1)} %slice_add_fusion.14), channel_id=1, source_target_pairs={{0,4},{2,6},{4,0},{6,2},{8,12},{10,14},{12,8},{14,10},{1,5},{3,7},... | collective-permute-start | bytes 786440 | tf_op jit(solution)/shard_map/ppermute | solution.py:538
  75.8 8.2 %collective-permute-start.13 = (f32[32,8,128]{2,1,0:T(8,128)S(1)}, f32[32,8,128]{2,1,0:T(8,128)S(1)}, u32[]{:S(2)}, u32[]{:S(2)}) collective-permute-start(f32[32,8,128]{2,1,0:T(8,128)S(1)} %slice_add_fusion.54), channel_id=1, source_target_pairs={{0,8},{2,10},{4,12},{6,14},{8,0},{10,2},{12,4},{14,6},{1,9},{3,11}... | collective-permute-start | bytes 393224 | tf_op jit(solution)/shard_map/ppermute | solution.py:538
  78.7 14.9 %collective-permute-start.20 = (f32[128,8,128]{2,1,0:T(8,128)S(1)}, f32[128,8,128]{2,1,0:T(8,128)S(1)}, u32[]{:S(2)}, u32[]{:S(2)}) collective-permute-start(f32[128,8,128]{2,1,0:T(8,128)S(1)} %slice_add_fusion.2), channel_id=1, source_target_pairs={{0,2},{2,0},{4,6},{6,4},{8,10},{10,8},{12,14},{14,12},{1,3},{3,1},... | collective-permute-start | bytes 1572872 | tf_op jit(solution)/shard_map/ppermute | solution.py:538
  83.9 9.6 %collective-permute-start.19 = (f32[64,8,128]{2,1,0:T(8,128)S(1)}, f32[64,8,128]{2,1,0:T(8,128)S(1)}, u32[]{:S(2)}, u32[]{:S(2)}) collective-permute-start(f32[64,8,128]{2,1,0:T(8,128)S(1)} %slice_add_fusion.12), channel_id=1, source_target_pairs={{0,4},{2,6},{4,0},{6,2},{8,12},{10,14},{12,8},{14,10},{1,5},{3,7},... | collective-permute-start | bytes 786440 | tf_op jit(solution)/shard_map/ppermute | solution.py:538
  84.8 16.6 %collective-permute-start.23 = (f32[128,8,128]{2,1,0:T(8,128)S(1)}, f32[128,8,128]{2,1,0:T(8,128)S(1)}, u32[]{:S(2)}, u32[]{:S(2)}) collective-permute-start(f32[128,8,128]{2,1,0:T(8,128)S(1)} %slice_add_fusion.1), channel_id=1, source_target_pairs={{0,2},{2,0},{4,6},{6,4},{8,10},{10,8},{12,14},{14,12},{1,3},{3,1},... | collective-permute-start | bytes 1572872 | tf_op jit(solution)/shard_map/ppermute | solution.py:538
  86.0 7.6 %collective-permute-start.18 = (f32[32,8,128]{2,1,0:T(8,128)S(1)}, f32[32,8,128]{2,1,0:T(8,128)S(1)}, u32[]{:S(2)}, u32[]{:S(2)}) collective-permute-start(f32[32,8,128]{2,1,0:T(8,128)S(1)} %slice_add_fusion.48), channel_id=1, source_target_pairs={{0,8},{2,10},{4,12},{6,14},{8,0},{10,2},{12,4},{14,6},{1,9},{3,11}... | collective-permute-start | bytes 393224 | tf_op jit(solution)/shard_map/ppermute | solution.py:538
  93.6 8.0 %collective-permute-start.22 = (f32[64,8,128]{2,1,0:T(8,128)S(1)}, f32[64,8,128]{2,1,0:T(8,128)S(1)}, u32[]{:S(2)}, u32[]{:S(2)}) collective-permute-start(f32[64,8,128]{2,1,0:T(8,128)S(1)} %slice_add_fusion.10), channel_id=1, source_target_pairs={{0,4},{2,6},{4,0},{6,2},{8,12},{10,14},{12,8},{14,10},{1,5},{3,7},... | collective-permute-start | bytes 786440 | tf_op jit(solution)/shard_map/ppermute | solution.py:538
  94.9 7.2 %collective-permute-start.21 = (f32[32,8,128]{2,1,0:T(8,128)S(1)}, f32[32,8,128]{2,1,0:T(8,128)S(1)}, u32[]{:S(2)}, u32[]{:S(2)}) collective-permute-start(f32[32,8,128]{2,1,0:T(8,128)S(1)} %slice_add_fusion.39), channel_id=1, source_target_pairs={{0,8},{2,10},{4,12},{6,14},{8,0},{10,2},{12,4},{14,6},{1,9},{3,11}... | collective-permute-start | bytes 393224 | tf_op jit(solution)/shard_map/ppermute | solution.py:538
  102.1 11.0 %collective-permute-start.25 = (f32[64,8,128]{2,1,0:T(8,128)S(1)}, f32[64,8,128]{2,1,0:T(8,128)S(1)}, u32[]{:S(2)}, u32[]{:S(2)}) collective-permute-start(f32[64,8,128]{2,1,0:T(8,128)S(1)} %slice_add_fusion.8), channel_id=1, source_target_pairs={{0,4},{2,6},{4,0},{6,2},{8,12},{10,14},{12,8},{14,10},{1,5},{3,7},... | collective-permute-start | bytes 786440 | tf_op jit(solution)/shard_map/ppermute | solution.py:538
  106.8 10.1 %collective-permute-start.27 = (f32[32,8,128]{2,1,0:T(8,128)S(1)}, f32[32,8,128]{2,1,0:T(8,128)S(1)}, u32[]{:S(2)}, u32[]{:S(2)}) collective-permute-start(f32[32,8,128]{2,1,0:T(8,128)S(1)} %slice_add_fusion.45), channel_id=1, source_target_pairs={{0,2},{2,0},{4,6},{6,4},{8,10},{10,8},{12,14},{14,12},{1,3},{3,1},... | collective-permute-start | bytes 393224 | tf_op jit(solution)/shard_map/ppermute | solution.py:538
  107.4 6.7 %collective-permute-start.24 = (f32[32,8,128]{2,1,0:T(8,128)S(1)}, f32[32,8,128]{2,1,0:T(8,128)S(1)}, u32[]{:S(2)}, u32[]{:S(2)}) collective-permute-start(f32[32,8,128]{2,1,0:T(8,128)S(1)} %slice_add_fusion.33), channel_id=1, source_target_pairs={{0,8},{2,10},{4,12},{6,14},{8,0},{10,2},{12,4},{14,6},{1,9},{3,11}... | collective-permute-start | bytes 393224 | tf_op jit(solution)/shard_map/ppermute | solution.py:538
  114.1 6.7 %collective-permute-start.26 = (f32[32,8,128]{2,1,0:T(8,128)S(1)}, f32[32,8,128]{2,1,0:T(8,128)S(1)}, u32[]{:S(2)}, u32[]{:S(2)}) collective-permute-start(f32[32,8,128]{2,1,0:T(8,128)S(1)} %slice_add_fusion.27), channel_id=1, source_target_pairs={{0,8},{2,10},{4,12},{6,14},{8,0},{10,2},{12,4},{14,6},{1,9},{3,11}... | collective-permute-start | bytes 393224 | tf_op jit(solution)/shard_map/ppermute | solution.py:538
  118.0 3.6 %copy-start = (s32[32,128]{1,0:T(8,128)S(1)}, s32[32,128]{1,0:T(8,128)}, u32[]{:S(2)}) copy-start(s32[32,128]{1,0:T(8,128)} %refs_2_.3) | copy-start | bytes 49156
  118.0 3.6 %copy-start.1 = (s32[32]{0:T(128)S(1)}, s32[32]{0:T(128)}, u32[]{:S(2)}) copy-start(s32[32]{0:T(128)} %refs_1_.2) | copy-start | bytes 388
  123.2 10.4 %collective-permute-start.28 = (f32[30,8,128]{2,1,0:T(8,128)S(1)}, f32[30,8,128]{2,1,0:T(8,128)S(1)}, u32[]{:S(2)}, u32[]{:S(2)}) collective-permute-start(f32[30,8,128]{2,1,0:T(8,128)S(1)} %get-tuple-element.86), channel_id=1, source_target_pairs={{0,2},{2,0},{4,6},{6,4},{8,10},{10,8},{12,14},{14,12},{1,3},{3,1},... | collective-permute-start | bytes 368648 | tf_op jit(solution)/shard_map/ppermute | solution.py:615
  127.4 7.4 %collective-permute-start.29 = (f32[30,8,128]{2,1,0:T(8,128)S(1)}, f32[30,8,128]{2,1,0:T(8,128)S(1)}, u32[]{:S(2)}, u32[]{:S(2)}) collective-permute-start(f32[30,8,128]{2,1,0:T(8,128)S(1)} %get-tuple-element.88), channel_id=1, source_target_pairs={{0,4},{2,6},{4,0},{6,2},{8,12},{10,14},{12,8},{14,10},{1,5},{3,7},... | collective-permute-start | bytes 368648 | tf_op jit(solution)/shard_map/ppermute | solution.py:615
  127.6 11.7 %collective-permute-start.30 = (f32[30,8,128]{2,1,0:T(8,128)S(1)}, f32[30,8,128]{2,1,0:T(8,128)S(1)}, u32[]{:S(2)}, u32[]{:S(2)}) collective-permute-start(f32[30,8,128]{2,1,0:T(8,128)S(1)} %get-tuple-element.90), channel_id=1, source_target_pairs={{0,6},{2,4},{4,2},{6,0},{8,14},{10,12},{12,10},{14,8},{1,7},{3,5},... | collective-permute-start | bytes 368648 | tf_op jit(solution)/shard_map/ppermute | solution.py:615
  129.2 10.1 %collective-permute-start.31 = (f32[30,8,128]{2,1,0:T(8,128)S(1)}, f32[30,8,128]{2,1,0:T(8,128)S(1)}, u32[]{:S(2)}, u32[]{:S(2)}) collective-permute-start(f32[30,8,128]{2,1,0:T(8,128)S(1)} %get-tuple-element.92), channel_id=1, source_target_pairs={{0,8},{2,10},{4,12},{6,14},{8,0},{10,2},{12,4},{14,6},{1,9},{3,11}... | collective-permute-start | bytes 368648 | tf_op jit(solution)/shard_map/ppermute | solution.py:615
  130.4 12.6 %collective-permute-start.32 = (f32[30,8,128]{2,1,0:T(8,128)S(1)}, f32[30,8,128]{2,1,0:T(8,128)S(1)}, u32[]{:S(2)}, u32[]{:S(2)}) collective-permute-start(f32[30,8,128]{2,1,0:T(8,128)S(1)} %get-tuple-element.94), channel_id=1, source_target_pairs={{0,10},{2,8},{4,14},{6,12},{8,2},{10,0},{12,6},{14,4},{1,11},{3,9}... | collective-permute-start | bytes 368648 | tf_op jit(solution)/shard_map/ppermute | solution.py:615
  133.5 9.4 %collective-permute-start.33 = (f32[30,8,128]{2,1,0:T(8,128)S(1)}, f32[30,8,128]{2,1,0:T(8,128)S(1)}, u32[]{:S(2)}, u32[]{:S(2)}) collective-permute-start(f32[30,8,128]{2,1,0:T(8,128)S(1)} %get-tuple-element.96), channel_id=1, source_target_pairs={{0,12},{2,14},{4,8},{6,10},{8,4},{10,6},{12,0},{14,2},{1,13},{3,15... | collective-permute-start | bytes 368648 | tf_op jit(solution)/shard_map/ppermute | solution.py:615
  134.8 8.1 %collective-permute-start.34 = (f32[30,8,128]{2,1,0:T(8,128)S(1)}, f32[30,8,128]{2,1,0:T(8,128)S(1)}, u32[]{:S(2)}, u32[]{:S(2)}) collective-permute-start(f32[30,8,128]{2,1,0:T(8,128)S(1)} %get-tuple-element.98), channel_id=1, source_target_pairs={{0,14},{2,12},{4,10},{6,8},{8,6},{10,4},{12,2},{14,0},{1,15},{3,13... | collective-permute-start | bytes 368648 | tf_op jit(solution)/shard_map/ppermute | solution.py:615
  144.4 1.6 %collective-permute-start.35 = (f32[58,8,128]{2,1,0:T(8,128)S(1)}, f32[58,8,128]{2,1,0:T(8,128)S(1)}, u32[]{:S(2)}, u32[]{:S(2)}) collective-permute-start(f32[58,8,128]{2,1,0:T(8,128)S(1)} %get-tuple-element.101), channel_id=1, source_target_pairs={{0,1},{1,0},{2,3},{3,2},{4,5},{5,4},{6,7},{7,6},{8,9},{9,8},{10,11... | collective-permute-start | bytes 712712 | tf_op jit(solution)/shard_map/ppermute | solution.py:535

commit v5 on v4

--- a/solution.py
+++ b/solution.py
@@ -155,7 +155,6 @@
 
 TILE = 8
 UNROLL = 8
-WIDTHS = (8, 8, 8, 8, 8, 8)
 LINE_FIRST = {0: 1, 3: 2}
 
 
@@ -337,7 +336,7 @@
         out_specs=[outside] * len(halves),
         scratch_shapes=targets
         + [
-            pltpu.VMEM((padded * block_count, row_count), jnp.float32),
+            pltpu.VMEM(((padded + 1) * block_count, row_count), jnp.float32),
             pltpu.VMEM((2 * regions * sum(sizes), TILE, row_count), jnp.float32),
             pltpu.SemaphoreType.DMA((len(used),)),
             pltpu.SemaphoreType.DMA((len(halves),)),
@@ -471,19 +470,15 @@
     )(sub_at.reshape(1) if coded else codes, *received)
 
 
-def unpack(tiles, widths, slots):
+def unpack(tiles, width, slots):
+    full, extra = width // TILE, width % TILE
     row_count = tiles.shape[2]
-    parts, start = [], 0
-    for width in widths:
-        full = width // TILE
-        whole = tiles[start : start + full * slots].reshape(full, slots, TILE, row_count)
-        parts.append([whole.transpose(0, 2, 1, 3).reshape(full * TILE, slots, row_count)])
-        start += full * slots
-    for part, width in zip(parts, widths, strict=True):
-        if width % TILE:
-            rest = tiles[start:].reshape(slots, width % TILE, row_count)
-            part.append(rest.transpose(1, 0, 2))
-    return [jnp.concatenate(part, 0) for part in parts]
+    whole = tiles[: full * slots].reshape(full, slots, TILE, row_count)
+    whole = whole.transpose(0, 2, 1, 3).reshape(full * TILE, slots, row_count)
+    if not extra:
+        return whole
+    rest = tiles[full * slots :].reshape(slots, extra, row_count).transpose(1, 0, 2)
+    return jnp.concatenate([whole, rest], 0)
 
 
 def merged_parts(parts):
@@ -492,20 +487,65 @@
     centre = sums[1:4] / divisor
     centre_outer = jnp.stack([centre[first] * centre[second] for first, second in PAIRS])
     spread = sums[4:10] / divisor - centre_outer
-    rest = [part / divisor for part in [sums[10:]] + parts[1:] if part.shape[0]]
+    rest = [part / divisor for part in parts[1:]]
     return jnp.concatenate([sums[:1], centre, spread] + rest, 0)
 
 
+def merge_kernel(colours, slots, tile, extra, out_ref):
+    rows = tile_rows()
+    for slot in range(slots):
+        sums = tile(0, slot)
+        scale = 1.0 / jnp.maximum(sums[:1], WEIGHT_FLOOR)
+        means = sums * scale
+        east, north, up = means[1:2], means[2:3], means[3:4]
+        left = jnp.where(rows == 7, north, east)
+        right = jnp.where(rows == 4, east, jnp.where(rows == 6, up, north))
+        means = jnp.where(rows >= 4, means - left * right, means)
+        out_ref[pl.ds(slot, TILE, stride=slots), :] = jnp.where(rows == 0, sums, means)
+        share = 2 * (slot % (TILE // 2))
+        rest = extra(slot // (TILE // 2))[share : share + 2] * scale
+        out_ref[pl.ds(TILE * slots + slot, 1), :] = rest[:1] - north * up
+        out_ref[pl.ds((TILE + 1) * slots + slot, 1), :] = rest[1:] - up * up
+        for line in range(colours):
+            start = (10 + line * TILE) * slots + slot
+            out_ref[pl.ds(start, TILE, stride=slots), :] = tile(1 + line, slot) * scale
+
+
+def merge_sums(sums, colours, slots, together):
+    row_count = sums[0].shape[2]
+    components = 10 + colours * TILE
+
+    def kernel(*refs):
+        ins, out_ref = refs[:-1], refs[-1]
+
+        def tile(line, slot):
+            if together:
+                return ins[0][line * slots + slot] + ins[1][line * slots + slot]
+            return ins[line][slot]
+
+        def extra(at):
+            if together:
+                place = (1 + colours) * slots + at
+                return ins[0][place] + ins[1][place]
+            return ins[0][slots + at]
+
+        merge_kernel(colours, slots, tile, extra, out_ref)
+
+    whole = pl.BlockSpec(memory_space=pltpu.VMEM)
+    merged = pl.pallas_call(
+        kernel,
+        out_shape=jax.ShapeDtypeStruct((components * slots, row_count), jnp.float32),
+        in_specs=[whole] * len(sums),
+        out_specs=whole,
+        compiler_params=pltpu.CompilerParams(vmem_limit_bytes=16 * 1024 * 1024),
+        cost_estimate=pl.CostEstimate(flops=1024, bytes_accessed=1024, transcendentals=0),
+        name="merge_sums",
+    )(*sums)
+    return merged.reshape(components, slots, row_count)
+
+
 def cut_components(components):
-    chunks, start = [(0, 10)], 10
-    for width in WIDTHS:
-        width = min(width, components - start)
-        if width > 0:
-            chunks.append((start, width))
-            start += width
-    if start < components:
-        chunks.append((start, components - start))
-    return chunks
+    return [(0, 10)] + [(start, TILE) for start in range(10, components, TILE)]
 
 
 def after(values, *others):
@@ -552,7 +592,6 @@
     sizes = [tile_count(width, PB_DEV) for _, width in chunks]
     orders = [list(range(levels)) for _ in chunks]
     terms = [[] for _ in chunks]
-    sends = [[] for _ in chunks]
 
     def fold(group, *others):
         place = place_in(orders[group[0]])
@@ -591,13 +630,8 @@
         depart(at, level, send)
         return send
 
-    level_one, level_two, codes, fetched = [], [], [None], []
-
-    def unpack_one():
-        return [
-            unpack(sums[at], [width], PB_DEV)[0] for at, (_, width) in enumerate(chunks)
-        ]
-
+    level_one, level_two, codes = [], [], [None]
+    colours = total - 1
 
     def raise_level(group, *others):
         widths = [chunks[at][1] for at in group]
@@ -615,13 +649,13 @@
             lax.ppermute(part, "span", [(at, at ^ away) for at in range(spans)]) if away else part
             for away, part in enumerate(parts)
         ]
-        fetched.append(parts[-1])
-        level_one.append(merged_parts(unpack_one()))
+        parted = zip(sums, chunks, strict=True)
+        level_one.append(merged_parts([unpack(part, width, PB_DEV) for part, (_, width) in parted]))
         parts = [after(part, level_one[0]) for part in parts]
         placed = place_parents(sub_at, codes[0], parts, widths, spans, cap_two, GB_DEV)
         if codes[0] is None:
             codes[0] = placed[2]
-        level_two.extend(unpack(placed[0] + swap(placed[1]), widths, GB_DEV))
+        level_two.append(merge_sums([placed[0], swap(placed[1])], colours, GB_DEV, True))
 
     fold(list(range(total)))
     depart_alone(0, 0)
@@ -668,7 +702,7 @@
             if level == levels - 1:
                 sums[at] = part(at, 0, 1)
     raise_level(list(range(total)))
-    return (level_one[0], merged_parts(level_two))
+    return (level_one[0], level_two[0])
 
 
 def body(*arrays):
@@ -676,7 +710,8 @@
     blocks = arrays[0].shape[0]
     dense = spans * subs * PB_DEV
     fits = subs == 2 and spans & (spans - 1) == 0 and dense <= 4 * blocks
-    if fits and PB_DEV == 4 * spans and blocks % 16 == 0:
+    colours = arrays[3].shape[0]
+    if fits and PB_DEV == 4 * spans and blocks % 16 == 0 and colours % TILE == 0:
         return span_body(*arrays)
     return plain_body(*arrays)
 

time: 151 us -> 149 us (0.987); the launches traced: 148 us -> 149 us
  waiting for transfers between devices: 62.4 us -> 64.1 us
  local copies, waits for them, and re-layouts: 5.79 us -> 4.12 us
    concatenate x2 -> x1, local copies, waits for them, and re-layouts: 3.17 us -> 2.4 us  [merged_parts(): return jnp.concatenate([sums[:1], centre, spread] + rest, 0)]
  transfers between devices with their start and end apart: 36 -> 36, of which waited for: 15 -> 18; matrix products, arithmetic and copies ran while one was open for 6% -> 6% of each run, Pallas kernels for 0% -> 0%
where the time goes in v5:
time: 149 us
  waiting for transfers between devices  64.1 us (43%)
  starting transfers between devices  55 us (37%)
  Pallas kernels  17.2 us (12%)
  other arithmetic  6.66 us (4%)
  local copies, waits for them, and re-layouts  4.12 us (3%)
  between operations  1.66 us (1%)
    ppermute x21, waiting for transfers between devices, cross(): lax.ppermute(values, 'span', [(at, at ^ 1 << bit) for at in range(spans)])  58.5 us
    ppermute x21, starting transfers between devices, cross(): lax.ppermute(values, 'span', [(at, at ^ 1 << bit) for at in range(spans)])  38.8 us
    ppermute x7, starting transfers between devices, raise_level(): lax.ppermute(part, 'span', [(at, at ^ away) for at in range(spans)])  14.7 us
    pallas_call x1, Pallas kernels, fold_children(): pl.pallas_call(kernel, out_shape=halves, in_specs=[scalars, scalars] + [o...  13.4 us
    ppermute x7, waiting for transfers between devices, raise_level(): lax.ppermute(part, 'span', [(at, at ^ away) for at in range(spans)])  3.76 us
  transfers between devices with their start and end apart: 36, of which 18 were waited for; matrix products, arithmetic and copies ran while one was open for 6% of the time, Pallas kernels for 0%

profile of v5, /device:TPU:0, one launch (start us, length us, event | category | flops | bytes accessed | tf_op | source)
XLA Modules:
  0.0 148.7 jit_solution(10226254550774104692)
XLA Ops:
  1.3 1.2 fusion.11.refs_0_
  2.5 13.4 %fold_children.1 = (f32[320,8,128]{2,1,0:T(8,128)}, f32[320,8,128]{2,1,0:T(8,128)}, f32[256,8,128]{2,1,0:T(8,128)}, f32[256,8,128]{2,1,0:T(8,128)}, f32[256,8,12...) custom-call(s32[128]{0:T(128)} %fusion.11.refs_0_, ...), custom_call_target="tpu_custom_call" | custom-call | flops 1024 | bytes 1024 | tf_op jit(solution)/shard_map/fold_children/pallas_call | solution.py:332
  17.3 1.6 %collective-permute-done.3 = f32[256,8,128]{2,1,0:T(8,128)S(1)} collective-permute-done((f32[256,8,128]{2,1,0:T(8,128)}, f32[256,8,128]{2,1,0:T(8,128)S(1)}, u32[]{:S(2)}, u32[]{:S(2)}) %collective-permute-start.3) | collective-permute-done | bytes 1048608 | tf_op jit(solution)/shard_map/ppermute | solution.py:575
  19.0 1.4 slice_add_fusion.63
  20.7 2.3 %collective-permute-start.4 = (f32[128,8,128]{2,1,0:T(8,128)S(1)}, f32[128,8,128]{2,1,0:T(8,128)S(1)}, u32[]{:S(2)}, u32[]{:S(2)}) collective-permute-start(f32[128,8,128]{2,1,0:T(8,128)S(1)} %pad_maximum_fusion), channel_id=1, source_target_pairs={{0,4},{2,6},{4,0},{6,2},{8,12},{10,14},{12,8},{14,10},{1,5},{3,7},... | collective-permute-start | bytes 1572872 | tf_op jit(solution)/shard_map/ppermute | solution.py:578
  23.1 2.6 %collective-permute-start.1 = (f32[160,8,128]{2,1,0:T(8,128)S(1)}, f32[160,8,128]{2,1,0:T(8,128)S(1)}, u32[]{:S(2)}, u32[]{:S(2)}) collective-permute-start(f32[160,8,128]{2,1,0:T(8,128)S(1)} %slice_add_fusion), channel_id=1, source_target_pairs={{0,2},{2,0},{4,6},{6,4},{8,10},{10,8},{12,14},{14,12},{1,3},{3,1},... | collective-permute-start | bytes 1966088 | tf_op jit(solution)/shard_map/ppermute | solution.py:578
  26.0 9.3 %collective-permute-done.4 = f32[128,8,128]{2,1,0:T(8,128)S(1)} collective-permute-done((f32[128,8,128]{2,1,0:T(8,128)S(1)}, f32[128,8,128]{2,1,0:T(8,128)S(1)}, u32[]{:S(2)}, u32[]{:S(2)}) %collective-permute-start.4) | collective-permute-done | bytes 524320 | tf_op jit(solution)/shard_map/ppermute | solution.py:578
  35.3 2.7 %collective-permute-start.8 = (f32[128,8,128]{2,1,0:T(8,128)S(1)}, f32[128,8,128]{2,1,0:T(8,128)S(1)}, u32[]{:S(2)}, u32[]{:S(2)}) collective-permute-start(f32[128,8,128]{2,1,0:T(8,128)S(1)} %slice_add_fusion.3), channel_id=1, source_target_pairs={{0,2},{2,0},{4,6},{6,4},{8,10},{10,8},{12,14},{14,12},{1,3},{3,1},... | collective-permute-start | bytes 1572872 | tf_op jit(solution)/shard_map/ppermute | solution.py:578
  38.1 3.2 %collective-permute-done.1 = f32[160,8,128]{2,1,0:T(8,128)S(1)} collective-permute-done((f32[160,8,128]{2,1,0:T(8,128)S(1)}, f32[160,8,128]{2,1,0:T(8,128)S(1)}, u32[]{:S(2)}, u32[]{:S(2)}) %collective-permute-start.1) | collective-permute-done | bytes 655392 | tf_op jit(solution)/shard_map/ppermute | solution.py:578
  41.3 1.4 collective-permute-start.5
  42.8 2.1 %collective-permute-start.12 = (f32[128,8,128]{2,1,0:T(8,128)S(1)}, f32[128,8,128]{2,1,0:T(8,128)S(1)}, u32[]{:S(2)}, u32[]{:S(2)}) collective-permute-start(f32[128,8,128]{2,1,0:T(8,128)S(1)} %slice_add_fusion.5), channel_id=1, source_target_pairs={{0,2},{2,0},{4,6},{6,4},{8,10},{10,8},{12,14},{14,12},{1,3},{3,1},... | collective-permute-start | bytes 1572872 | tf_op jit(solution)/shard_map/ppermute | solution.py:578
  44.9 7.6 %collective-permute-done.8 = f32[128,8,128]{2,1,0:T(8,128)S(1)} collective-permute-done((f32[128,8,128]{2,1,0:T(8,128)S(1)}, f32[128,8,128]{2,1,0:T(8,128)S(1)}, u32[]{:S(2)}, u32[]{:S(2)}) %collective-permute-start.8) | collective-permute-done | bytes 524320 | tf_op jit(solution)/shard_map/ppermute | solution.py:578
  52.6 1.4 collective-permute-start.10
  54.1 2.3 %collective-permute-start.17 = (f32[64,8,128]{2,1,0:T(8,128)S(1)}, f32[64,8,128]{2,1,0:T(8,128)S(1)}, u32[]{:S(2)}, u32[]{:S(2)}) collective-permute-start(f32[64,8,128]{2,1,0:T(8,128)S(1)} %maximum_add_fusion), channel_id=1, source_target_pairs={{0,8},{2,10},{4,12},{6,14},{8,0},{10,2},{12,4},{14,6},{1,9},{3,11}... | collective-permute-start | bytes 786440 | tf_op jit(solution)/shard_map/ppermute | solution.py:578
  56.4 0.7 collective-permute-start.9
  57.1 5.9 %collective-permute-done.12 = f32[128,8,128]{2,1,0:T(8,128)S(1)} collective-permute-done((f32[128,8,128]{2,1,0:T(8,128)S(1)}, f32[128,8,128]{2,1,0:T(8,128)S(1)}, u32[]{:S(2)}, u32[]{:S(2)}) %collective-permute-start.12) | collective-permute-done | bytes 524320 | tf_op jit(solution)/shard_map/ppermute | solution.py:578
  63.0 1.7 %collective-permute-start.16 = (f32[128,8,128]{2,1,0:T(8,128)S(1)}, f32[128,8,128]{2,1,0:T(8,128)S(1)}, u32[]{:S(2)}, u32[]{:S(2)}) collective-permute-start(f32[128,8,128]{2,1,0:T(8,128)S(1)} %slice_add_fusion.4), channel_id=1, source_target_pairs={{0,2},{2,0},{4,6},{6,4},{8,10},{10,8},{12,14},{14,12},{1,3},{3,1},... | collective-permute-start | bytes 1572872 | tf_op jit(solution)/shard_map/ppermute | solution.py:578
  64.9 9.8 %collective-permute-done.9 = f32[40,8,128]{2,1,0:T(8,128)S(1)} collective-permute-done((f32[40,8,128]{2,1,0:T(8,128)S(1)}, f32[40,8,128]{2,1,0:T(8,128)S(1)}, u32[]{:S(2)}, u32[]{:S(2)}) %collective-permute-start.9) | collective-permute-done | bytes 163872 | tf_op jit(solution)/shard_map/ppermute | solution.py:578
  74.9 0.9 slice_add_fusion.45
  75.8 3.0 %collective-permute-start.13 = (f32[32,8,128]{2,1,0:T(8,128)S(1)}, f32[32,8,128]{2,1,0:T(8,128)S(1)}, u32[]{:S(2)}, u32[]{:S(2)}) collective-permute-start(f32[32,8,128]{2,1,0:T(8,128)S(1)} %slice_add_fusion.54), channel_id=1, source_target_pairs={{0,8},{2,10},{4,12},{6,14},{8,0},{10,2},{12,4},{14,6},{1,9},{3,11}... | collective-permute-start | bytes 393224 | tf_op jit(solution)/shard_map/ppermute | solution.py:578
  78.8 1.5 %collective-permute-start.20 = (f32[128,8,128]{2,1,0:T(8,128)S(1)}, f32[128,8,128]{2,1,0:T(8,128)S(1)}, u32[]{:S(2)}, u32[]{:S(2)}) collective-permute-start(f32[128,8,128]{2,1,0:T(8,128)S(1)} %slice_add_fusion.2), channel_id=1, source_target_pairs={{0,2},{2,0},{4,6},{6,4},{8,10},{10,8},{12,14},{14,12},{1,3},{3,1},... | collective-permute-start | bytes 1572872 | tf_op jit(solution)/shard_map/ppermute | solution.py:578
  80.3 4.1 %collective-permute-done.14 = f32[64,8,128]{2,1,0:T(8,128)S(1)} collective-permute-done((f32[64,8,128]{2,1,0:T(8,128)S(1)}, f32[64,8,128]{2,1,0:T(8,128)S(1)}, u32[]{:S(2)}, u32[]{:S(2)}) %collective-permute-start.14) | collective-permute-done | bytes 262176 | tf_op jit(solution)/shard_map/ppermute | solution.py:578
  84.8 1.8 %collective-permute-start.23 = (f32[128,8,128]{2,1,0:T(8,128)S(1)}, f32[128,8,128]{2,1,0:T(8,128)S(1)}, u32[]{:S(2)}, u32[]{:S(2)}) collective-permute-start(f32[128,8,128]{2,1,0:T(8,128)S(1)} %slice_add_fusion.1), channel_id=1, source_target_pairs={{0,2},{2,0},{4,6},{6,4},{8,10},{10,8},{12,14},{14,12},{1,3},{3,1},... | collective-permute-start | bytes 1572872 | tf_op jit(solution)/shard_map/ppermute | solution.py:578
  86.5 2.3 %collective-permute-start.18 = (f32[32,8,128]{2,1,0:T(8,128)S(1)}, f32[32,8,128]{2,1,0:T(8,128)S(1)}, u32[]{:S(2)}, u32[]{:S(2)}) collective-permute-start(f32[32,8,128]{2,1,0:T(8,128)S(1)} %slice_add_fusion.48), channel_id=1, source_target_pairs={{0,8},{2,10},{4,12},{6,14},{8,0},{10,2},{12,4},{14,6},{1,9},{3,11}... | collective-permute-start | bytes 393224 | tf_op jit(solution)/shard_map/ppermute | solution.py:578
  88.9 4.8 %collective-permute-done.20 = f32[128,8,128]{2,1,0:T(8,128)S(1)} collective-permute-done((f32[128,8,128]{2,1,0:T(8,128)S(1)}, f32[128,8,128]{2,1,0:T(8,128)S(1)}, u32[]{:S(2)}, u32[]{:S(2)}) %collective-permute-start.20) | collective-permute-done | bytes 524320 | tf_op jit(solution)/shard_map/ppermute | solution.py:578
  93.8 0.9 collective-permute-done.18
  94.7 3.9 %collective-permute-start.21 = (f32[32,8,128]{2,1,0:T(8,128)S(1)}, f32[32,8,128]{2,1,0:T(8,128)S(1)}, u32[]{:S(2)}, u32[]{:S(2)}) collective-permute-start(f32[32,8,128]{2,1,0:T(8,128)S(1)} %slice_add_fusion.39), channel_id=1, source_target_pairs={{0,8},{2,10},{4,12},{6,14},{8,0},{10,2},{12,4},{14,6},{1,9},{3,11}... | collective-permute-start | bytes 393224 | tf_op jit(solution)/shard_map/ppermute | solution.py:578
  98.6 2.7 %collective-permute-done.23 = f32[128,8,128]{2,1,0:T(8,128)S(1)} collective-permute-done((f32[128,8,128]{2,1,0:T(8,128)S(1)}, f32[128,8,128]{2,1,0:T(8,128)S(1)}, u32[]{:S(2)}, u32[]{:S(2)}) %collective-permute-start.23) | collective-permute-done | bytes 524320 | tf_op jit(solution)/shard_map/ppermute | solution.py:578
  101.4 3.3 %collective-permute-done.22 = f32[64,8,128]{2,1,0:T(8,128)S(1)} collective-permute-done((f32[64,8,128]{2,1,0:T(8,128)S(1)}, f32[64,8,128]{2,1,0:T(8,128)S(1)}, u32[]{:S(2)}, u32[]{:S(2)}) %collective-permute-start.22) | collective-permute-done | bytes 262176 | tf_op jit(solution)/shard_map/ppermute | solution.py:578
  104.7 2.5 %collective-permute-start.25 = (f32[64,8,128]{2,1,0:T(8,128)S(1)}, f32[64,8,128]{2,1,0:T(8,128)S(1)}, u32[]{:S(2)}, u32[]{:S(2)}) collective-permute-start(f32[64,8,128]{2,1,0:T(8,128)S(1)} %slice_add_fusion.8), channel_id=1, source_target_pairs={{0,4},{2,6},{4,0},{6,2},{8,12},{10,14},{12,8},{14,10},{1,5},{3,7},... | collective-permute-start | bytes 786440 | tf_op jit(solution)/shard_map/ppermute | solution.py:578
  107.6 3.2 %collective-permute-start.24 = (f32[32,8,128]{2,1,0:T(8,128)S(1)}, f32[32,8,128]{2,1,0:T(8,128)S(1)}, u32[]{:S(2)}, u32[]{:S(2)}) collective-permute-start(f32[32,8,128]{2,1,0:T(8,128)S(1)} %slice_add_fusion.33), channel_id=1, source_target_pairs={{0,8},{2,10},{4,12},{6,14},{8,0},{10,2},{12,4},{14,6},{1,9},{3,11}... | collective-permute-start | bytes 393224 | tf_op jit(solution)/shard_map/ppermute | solution.py:578
  110.8 2.9 %collective-permute-done.25 = f32[64,8,128]{2,1,0:T(8,128)S(1)} collective-permute-done((f32[64,8,128]{2,1,0:T(8,128)S(1)}, f32[64,8,128]{2,1,0:T(8,128)S(1)}, u32[]{:S(2)}, u32[]{:S(2)}) %collective-permute-start.25) | collective-permute-done | bytes 262176 | tf_op jit(solution)/shard_map/ppermute | solution.py:578
  113.8 0.8 collective-permute-done.24
  114.6 2.9 %collective-permute-start.26 = (f32[32,8,128]{2,1,0:T(8,128)S(1)}, f32[32,8,128]{2,1,0:T(8,128)S(1)}, u32[]{:S(2)}, u32[]{:S(2)}) collective-permute-start(f32[32,8,128]{2,1,0:T(8,128)S(1)} %slice_add_fusion.27), channel_id=1, source_target_pairs={{0,8},{2,10},{4,12},{6,14},{8,0},{10,2},{12,4},{14,6},{1,9},{3,11}... | collective-permute-start | bytes 393224 | tf_op jit(solution)/shard_map/ppermute | solution.py:578
  117.5 1.0 bitcast_divide_fusion
  118.5 2.8 %collective-permute-done.26 = f32[32,8,128]{2,1,0:T(8,128)S(1)} collective-permute-done((f32[32,8,128]{2,1,0:T(8,128)S(1)}, f32[32,8,128]{2,1,0:T(8,128)S(1)}, u32[]{:S(2)}, u32[]{:S(2)}) %collective-permute-start.26) | collective-permute-done | bytes 131104 | tf_op jit(solution)/shard_map/ppermute | solution.py:578
  121.4 0.8 bitcast_divide_fusion.1
  122.2 1.6 %fold_parents.1 = (f32[30,8,128]{2,1,0:T(8,128)S(1)}, f32[30,8,128]{2,1,0:T(8,128)S(1)}, f32[30,8,128]{2,1,0:T(8,128)S(1)}, f32[30,8,128]{2,1,0:T(8,128)S(1)}, f...) custom-call(s32[32]{0:T(128)S(1)} %multiply_add_fusion.refs_0_, ...), custom_call_target="tpu_custom_call" | custom-call | flops 1024 | bytes 1024 | tf_op jit(solution)/shard_map/fold_parents/pallas_call | solution.py:402
  124.2 3.4 %collective-permute-start.29 = (f32[30,8,128]{2,1,0:T(8,128)S(1)}, f32[30,8,128]{2,1,0:T(8,128)S(1)}, u32[]{:S(2)}, u32[]{:S(2)}) collective-permute-start(f32[30,8,128]{2,1,0:T(8,128)S(1)} %get-tuple-element.88), channel_id=1, source_target_pairs={{0,4},{2,6},{4,0},{6,2},{8,12},{10,14},{12,8},{14,10},{1,5},{3,7},... | collective-permute-start | bytes 368648 | tf_op jit(solution)/shard_map/ppermute | solution.py:649
  127.8 5.5 %collective-permute-start.31 = (f32[30,8,128]{2,1,0:T(8,128)S(1)}, f32[30,8,128]{2,1,0:T(8,128)S(1)}, u32[]{:S(2)}, u32[]{:S(2)}) collective-permute-start(f32[30,8,128]{2,1,0:T(8,128)S(1)} %get-tuple-element.92), channel_id=1, source_target_pairs={{0,8},{2,10},{4,12},{6,14},{8,0},{10,2},{12,4},{14,6},{1,9},{3,11}... | collective-permute-start | bytes 368648 | tf_op jit(solution)/shard_map/ppermute | solution.py:649
  133.5 3.7 %collective-permute-start.33 = (f32[30,8,128]{2,1,0:T(8,128)S(1)}, f32[30,8,128]{2,1,0:T(8,128)S(1)}, u32[]{:S(2)}, u32[]{:S(2)}) collective-permute-start(f32[30,8,128]{2,1,0:T(8,128)S(1)} %get-tuple-element.96), channel_id=1, source_target_pairs={{0,12},{2,14},{4,8},{6,10},{8,4},{10,6},{12,0},{14,2},{1,13},{3,15... | collective-permute-start | bytes 368648 | tf_op jit(solution)/shard_map/ppermute | solution.py:649
  137.2 1.5 collective-permute-start.34
  138.7 2.4 %concatenate.19 = f32[58,32,128]{2,0,1:T(8,128)S(1)} concatenate(f32[1,32,128]{2,0,1:T(1,128)S(1)} %get-tuple-element.129, f32[3,32,128]{2,0,1:T(4,128)S(1)} %fusion.9, f32[6,32,128]{2,0,1:T(8,128)S(1)} %fusion.8, f32[8,32,128]{2,0,1:T(8,128)} %get-tuple-element.142, f32[8,32,128]{2,0,1:T(8,128)S(1)} %get-tuple-element.136, f32[8,32,128]{2,0,1:T(8,128)S(1)} %get-tuple-element.138, ...), dimensions={0} | concatenate | bytes 1900544 | tf_op jit(solution)/shard_map/concatenate | solution.py:491
  141.2 0.5 collective-permute-done.33.refs_7_
  141.7 3.2 %collective-permute-done.34.refs_8_ = f32[30,8,128]{2,1,0:T(8,128)S(1)} collective-permute-done((f32[30,8,128]{2,1,0:T(8,128)S(1)}, f32[30,8,128]{2,1,0:T(8,128)S(1)}, u32[]{:S(2)}, u32[]{:S(2)}) %collective-permute-start.34) | collective-permute-done | bytes 122912 | tf_op jit(solution)/shard_map/ppermute | solution.py:649
  144.9 1.4 place_parents.1
  146.4 1.5 %copy.16 = f32[58,32,128]{2,1,0:T(8,128)} copy(f32[58,32,128]{2,0,1:T(8,128)S(1)} %concatenate.19) | data formatting | bytes 1900544
  147.9 0.8 merge_sums.1
  (86 shorter events, 4.6 us)
Async XLA Ops:
  0.6 16.4 %copy-start.8 = (s32[32]{0:T(128)S(1)}, s32[32]{0:T(128)}, u32[]{:S(2)}) copy-start(s32[32]{0:T(128)} %param.19) | copy-start | bytes 388
  15.9 2.9 %collective-permute-start.3 = (f32[256,8,128]{2,1,0:T(8,128)}, f32[256,8,128]{2,1,0:T(8,128)S(1)}, u32[]{:S(2)}, u32[]{:S(2)}) collective-permute-start(f32[256,8,128]{2,1,0:T(8,128)} %get-tuple-element.57), channel_id=1, source_target_pairs={{0,1},{1,0},{2,3},{3,2},{4,5},{5,4},{6,7},{7,6},{8,9},{9,8},{10,11... | collective-permute-start | bytes 3145736 | tf_op jit(solution)/shard_map/ppermute | solution.py:575
  16.0 4.7 %collective-permute-start = (f32[320,8,128]{2,1,0:T(8,128)}, f32[320,8,128]{2,1,0:T(8,128)S(1)}, u32[]{:S(2)}, u32[]{:S(2)}) collective-permute-start(f32[320,8,128]{2,1,0:T(8,128)} %get-tuple-element.53), channel_id=1, source_target_pairs={{0,1},{1,0},{2,3},{3,2},{4,5},{5,4},{6,7},{7,6},{8,9},{9,8},{10,11... | collective-permute-start | bytes 3932168 | tf_op jit(solution)/shard_map/ppermute | solution.py:575
  16.5 6.7 %collective-permute-start.7 = (f32[256,8,128]{2,1,0:T(8,128)}, f32[256,8,128]{2,1,0:T(8,128)S(1)}, u32[]{:S(2)}, u32[]{:S(2)}) collective-permute-start(f32[256,8,128]{2,1,0:T(8,128)} %get-tuple-element.62), channel_id=1, source_target_pairs={{0,1},{1,0},{2,3},{3,2},{4,5},{5,4},{6,7},{7,6},{8,9},{9,8},{10,11... | collective-permute-start | bytes 3145736 | tf_op jit(solution)/shard_map/ppermute | solution.py:575
  16.6 26.2 %collective-permute-start.6 = (f32[256,8,128]{2,1,0:T(8,128)}, f32[256,8,128]{2,1,0:T(8,128)S(1)}, u32[]{:S(2)}, u32[]{:S(2)}) collective-permute-start(f32[256,8,128]{2,1,0:T(8,128)} %get-tuple-element.60), channel_id=1, source_target_pairs={{0,1},{1,0},{2,3},{3,2},{4,5},{5,4},{6,7},{7,6},{8,9},{9,8},{10,11... | collective-permute-start | bytes 3145736 | tf_op jit(solution)/shard_map/ppermute | solution.py:575
  17.0 8.8 %collective-permute-start.2 = (f32[256,8,128]{2,1,0:T(8,128)}, f32[256,8,128]{2,1,0:T(8,128)S(1)}, u32[]{:S(2)}, u32[]{:S(2)}) collective-permute-start(f32[256,8,128]{2,1,0:T(8,128)} %get-tuple-element.55), channel_id=1, source_target_pairs={{0,1},{1,0},{2,3},{3,2},{4,5},{5,4},{6,7},{7,6},{8,9},{9,8},{10,11... | collective-permute-start | bytes 3145736 | tf_op jit(solution)/shard_map/ppermute | solution.py:575
  18.8 56.0 %collective-permute-start.15 = (f32[256,8,128]{2,1,0:T(8,128)}, f32[256,8,128]{2,1,0:T(8,128)S(1)}, u32[]{:S(2)}, u32[]{:S(2)}) collective-permute-start(f32[256,8,128]{2,1,0:T(8,128)} %get-tuple-element.71), channel_id=1, source_target_pairs={{0,1},{1,0},{2,3},{3,2},{4,5},{5,4},{6,7},{7,6},{8,9},{9,8},{10,11... | collective-permute-start | bytes 3145736 | tf_op jit(solution)/shard_map/ppermute | solution.py:575
  19.0 4.1 %copy-start.2 = (f32[320,8,128]{2,1,0:T(8,128)S(1)}, f32[320,8,128]{2,1,0:T(8,128)}, u32[]{:S(2)}) copy-start(f32[320,8,128]{2,1,0:T(8,128)} %get-tuple-element.52) | copy-start | bytes 3932164
  20.4 5.3 %copy-start.3 = (f32[256,8,128]{2,1,0:T(8,128)S(1)}, f32[256,8,128]{2,1,0:T(8,128)}, u32[]{:S(2)}) copy-start(f32[256,8,128]{2,1,0:T(8,128)} %get-tuple-element.61) | copy-start | bytes 3145732
  20.7 14.6 %collective-permute-start.4 = (f32[128,8,128]{2,1,0:T(8,128)S(1)}, f32[128,8,128]{2,1,0:T(8,128)S(1)}, u32[]{:S(2)}, u32[]{:S(2)}) collective-permute-start(f32[128,8,128]{2,1,0:T(8,128)S(1)} %pad_maximum_fusion), channel_id=1, source_target_pairs={{0,4},{2,6},{4,0},{6,2},{8,12},{10,14},{12,8},{14,10},{1,5},{3,7},... | collective-permute-start | bytes 1572872 | tf_op jit(solution)/shard_map/ppermute | solution.py:578
  23.0 2.8 %copy-start.9 = (f32[256,8,128]{2,1,0:T(8,128)S(1)}, f32[256,8,128]{2,1,0:T(8,128)}, u32[]{:S(2)}) copy-start(f32[256,8,128]{2,1,0:T(8,128)} %get-tuple-element.66) | copy-start | bytes 3145732
  23.1 2.8 %copy-start.6 = (f32[256,8,128]{2,1,0:T(8,128)S(1)}, f32[256,8,128]{2,1,0:T(8,128)}, u32[]{:S(2)}) copy-start(f32[256,8,128]{2,1,0:T(8,128)} %get-tuple-element.54) | copy-start | bytes 3145732
  23.1 18.1 %collective-permute-start.1 = (f32[160,8,128]{2,1,0:T(8,128)S(1)}, f32[160,8,128]{2,1,0:T(8,128)S(1)}, u32[]{:S(2)}, u32[]{:S(2)}) collective-permute-start(f32[160,8,128]{2,1,0:T(8,128)S(1)} %slice_add_fusion), channel_id=1, source_target_pairs={{0,2},{2,0},{4,6},{6,4},{8,10},{10,8},{12,14},{14,12},{1,3},{3,1},... | collective-permute-start | bytes 1966088 | tf_op jit(solution)/shard_map/ppermute | solution.py:578
  25.8 28.2 %collective-permute-start.11 = (f32[256,8,128]{2,1,0:T(8,128)S(1)}, f32[256,8,128]{2,1,0:T(8,128)S(1)}, u32[]{:S(2)}, u32[]{:S(2)}) collective-permute-start(f32[256,8,128]{2,1,0:T(8,128)S(1)} %copy-done.9), channel_id=1, source_target_pairs={{0,1},{1,0},{2,3},{3,2},{4,5},{5,4},{6,7},{7,6},{8,9},{9,8},{10,11... | collective-permute-start | bytes 3145736 | tf_op jit(solution)/shard_map/ppermute | solution.py:575
  26.0 16.7 %copy-start.7 = (f32[256,8,128]{2,1,0:T(8,128)S(1)}, f32[256,8,128]{2,1,0:T(8,128)}, u32[]{:S(2)}) copy-start(f32[256,8,128]{2,1,0:T(8,128)} %get-tuple-element.59) | copy-start | bytes 3145732
  35.3 17.2 %collective-permute-start.8 = (f32[128,8,128]{2,1,0:T(8,128)S(1)}, f32[128,8,128]{2,1,0:T(8,128)S(1)}, u32[]{:S(2)}, u32[]{:S(2)}) collective-permute-start(f32[128,8,128]{2,1,0:T(8,128)S(1)} %slice_add_fusion.3), channel_id=1, source_target_pairs={{0,2},{2,0},{4,6},{6,4},{8,10},{10,8},{12,14},{14,12},{1,3},{3,1},... | collective-permute-start | bytes 1572872 | tf_op jit(solution)/shard_map/ppermute | solution.py:578
  41.3 11.2 %collective-permute-start.5 = (f32[80,8,128]{2,1,0:T(8,128)S(1)}, f32[80,8,128]{2,1,0:T(8,128)S(1)}, u32[]{:S(2)}, u32[]{:S(2)}) collective-permute-start(f32[80,8,128]{2,1,0:T(8,128)S(1)} %slice_add_fusion.6), channel_id=1, source_target_pairs={{0,4},{2,6},{4,0},{6,2},{8,12},{10,14},{12,8},{14,10},{1,5},{3,7},... | collective-permute-start | bytes 983048 | tf_op jit(solution)/shard_map/ppermute | solution.py:578
  42.8 11.2 %copy-start.4 = (f32[256,8,128]{2,1,0:T(8,128)S(1)}, f32[256,8,128]{2,1,0:T(8,128)}, u32[]{:S(2)}) copy-start(f32[256,8,128]{2,1,0:T(8,128)} %get-tuple-element.65) | copy-start | bytes 3145732
  42.8 20.2 %collective-permute-start.12 = (f32[128,8,128]{2,1,0:T(8,128)S(1)}, f32[128,8,128]{2,1,0:T(8,128)S(1)}, u32[]{:S(2)}, u32[]{:S(2)}) collective-permute-start(f32[128,8,128]{2,1,0:T(8,128)S(1)} %slice_add_fusion.5), channel_id=1, source_target_pairs={{0,2},{2,0},{4,6},{6,4},{8,10},{10,8},{12,14},{14,12},{1,3},{3,1},... | collective-permute-start | bytes 1572872 | tf_op jit(solution)/shard_map/ppermute | solution.py:578
  52.6 12.3 %collective-permute-start.10 = (f32[64,8,128]{2,1,0:T(8,128)S(1)}, f32[64,8,128]{2,1,0:T(8,128)S(1)}, u32[]{:S(2)}, u32[]{:S(2)}) collective-permute-start(f32[64,8,128]{2,1,0:T(8,128)S(1)} %slice_add_fusion.16), channel_id=1, source_target_pairs={{0,4},{2,6},{4,0},{6,2},{8,12},{10,14},{12,8},{14,10},{1,5},{3,7},... | collective-permute-start | bytes 786440 | tf_op jit(solution)/shard_map/ppermute | solution.py:578
  54.0 20.8 %copy-start.5 = (f32[256,8,128]{2,1,0:T(8,128)S(1)}, f32[256,8,128]{2,1,0:T(8,128)}, u32[]{:S(2)}) copy-start(f32[256,8,128]{2,1,0:T(8,128)} %get-tuple-element.70) | copy-start | bytes 3145732
  54.1 20.8 %collective-permute-start.17 = (f32[64,8,128]{2,1,0:T(8,128)S(1)}, f32[64,8,128]{2,1,0:T(8,128)S(1)}, u32[]{:S(2)}, u32[]{:S(2)}) collective-permute-start(f32[64,8,128]{2,1,0:T(8,128)S(1)} %maximum_add_fusion), channel_id=1, source_target_pairs={{0,8},{2,10},{4,12},{6,14},{8,0},{10,2},{12,4},{14,6},{1,9},{3,11}... | collective-permute-start | bytes 786440 | tf_op jit(solution)/shard_map/ppermute | solution.py:578
  56.4 18.4 %collective-permute-start.9 = (f32[40,8,128]{2,1,0:T(8,128)S(1)}, f32[40,8,128]{2,1,0:T(8,128)S(1)}, u32[]{:S(2)}, u32[]{:S(2)}) collective-permute-start(f32[40,8,128]{2,1,0:T(8,128)S(1)} %slice_add_fusion.18), channel_id=1, source_target_pairs={{0,8},{2,10},{4,12},{6,14},{8,0},{10,2},{12,4},{14,6},{1,9},{3,11}... | collective-permute-start | bytes 491528 | tf_op jit(solution)/shard_map/ppermute | solution.py:578
  63.0 21.5 %collective-permute-start.16 = (f32[128,8,128]{2,1,0:T(8,128)S(1)}, f32[128,8,128]{2,1,0:T(8,128)S(1)}, u32[]{:S(2)}, u32[]{:S(2)}) collective-permute-start(f32[128,8,128]{2,1,0:T(8,128)S(1)} %slice_add_fusion.4), channel_id=1, source_target_pairs={{0,2},{2,0},{4,6},{6,4},{8,10},{10,8},{12,14},{14,12},{1,3},{3,1},... | collective-permute-start | bytes 1572872 | tf_op jit(solution)/shard_map/ppermute | solution.py:578
  74.8 9.6 %collective-permute-start.14 = (f32[64,8,128]{2,1,0:T(8,128)S(1)}, f32[64,8,128]{2,1,0:T(8,128)S(1)}, u32[]{:S(2)}, u32[]{:S(2)}) collective-permute-start(f32[64,8,128]{2,1,0:T(8,128)S(1)} %slice_add_fusion.14), channel_id=1, source_target_pairs={{0,4},{2,6},{4,0},{6,2},{8,12},{10,14},{12,8},{14,10},{1,5},{3,7},... | collective-permute-start | bytes 786440 | tf_op jit(solution)/shard_map/ppermute | solution.py:578
  75.8 8.7 %collective-permute-start.13 = (f32[32,8,128]{2,1,0:T(8,128)S(1)}, f32[32,8,128]{2,1,0:T(8,128)S(1)}, u32[]{:S(2)}, u32[]{:S(2)}) collective-permute-start(f32[32,8,128]{2,1,0:T(8,128)S(1)} %slice_add_fusion.54), channel_id=1, source_target_pairs={{0,8},{2,10},{4,12},{6,14},{8,0},{10,2},{12,4},{14,6},{1,9},{3,11}... | collective-permute-start | bytes 393224 | tf_op jit(solution)/shard_map/ppermute | solution.py:578
  78.8 14.9 %collective-permute-start.20 = (f32[128,8,128]{2,1,0:T(8,128)S(1)}, f32[128,8,128]{2,1,0:T(8,128)S(1)}, u32[]{:S(2)}, u32[]{:S(2)}) collective-permute-start(f32[128,8,128]{2,1,0:T(8,128)S(1)} %slice_add_fusion.2), channel_id=1, source_target_pairs={{0,2},{2,0},{4,6},{6,4},{8,10},{10,8},{12,14},{14,12},{1,3},{3,1},... | collective-permute-start | bytes 1572872 | tf_op jit(solution)/shard_map/ppermute | solution.py:578
  84.5 9.2 %collective-permute-start.19 = (f32[64,8,128]{2,1,0:T(8,128)S(1)}, f32[64,8,128]{2,1,0:T(8,128)S(1)}, u32[]{:S(2)}, u32[]{:S(2)}) collective-permute-start(f32[64,8,128]{2,1,0:T(8,128)S(1)} %slice_add_fusion.12), channel_id=1, source_target_pairs={{0,4},{2,6},{4,0},{6,2},{8,12},{10,14},{12,8},{14,10},{1,5},{3,7},... | collective-permute-start | bytes 786440 | tf_op jit(solution)/shard_map/ppermute | solution.py:578
  84.8 16.5 %collective-permute-start.23 = (f32[128,8,128]{2,1,0:T(8,128)S(1)}, f32[128,8,128]{2,1,0:T(8,128)S(1)}, u32[]{:S(2)}, u32[]{:S(2)}) collective-permute-start(f32[128,8,128]{2,1,0:T(8,128)S(1)} %slice_add_fusion.1), channel_id=1, source_target_pairs={{0,2},{2,0},{4,6},{6,4},{8,10},{10,8},{12,14},{14,12},{1,3},{3,1},... | collective-permute-start | bytes 1572872 | tf_op jit(solution)/shard_map/ppermute | solution.py:578
  86.5 8.1 %collective-permute-start.18 = (f32[32,8,128]{2,1,0:T(8,128)S(1)}, f32[32,8,128]{2,1,0:T(8,128)S(1)}, u32[]{:S(2)}, u32[]{:S(2)}) collective-permute-start(f32[32,8,128]{2,1,0:T(8,128)S(1)} %slice_add_fusion.48), channel_id=1, source_target_pairs={{0,8},{2,10},{4,12},{6,14},{8,0},{10,2},{12,4},{14,6},{1,9},{3,11}... | collective-permute-start | bytes 393224 | tf_op jit(solution)/shard_map/ppermute | solution.py:578
  94.7 10.0 %collective-permute-start.22 = (f32[64,8,128]{2,1,0:T(8,128)S(1)}, f32[64,8,128]{2,1,0:T(8,128)S(1)}, u32[]{:S(2)}, u32[]{:S(2)}) collective-permute-start(f32[64,8,128]{2,1,0:T(8,128)S(1)} %slice_add_fusion.10), channel_id=1, source_target_pairs={{0,4},{2,6},{4,0},{6,2},{8,12},{10,14},{12,8},{14,10},{1,5},{3,7},... | collective-permute-start | bytes 786440 | tf_op jit(solution)/shard_map/ppermute | solution.py:578
  94.7 10.0 %collective-permute-start.21 = (f32[32,8,128]{2,1,0:T(8,128)S(1)}, f32[32,8,128]{2,1,0:T(8,128)S(1)}, u32[]{:S(2)}, u32[]{:S(2)}) collective-permute-start(f32[32,8,128]{2,1,0:T(8,128)S(1)} %slice_add_fusion.39), channel_id=1, source_target_pairs={{0,8},{2,10},{4,12},{6,14},{8,0},{10,2},{12,4},{14,6},{1,9},{3,11}... | collective-permute-start | bytes 393224 | tf_op jit(solution)/shard_map/ppermute | solution.py:578
  104.7 9.0 %collective-permute-start.25 = (f32[64,8,128]{2,1,0:T(8,128)S(1)}, f32[64,8,128]{2,1,0:T(8,128)S(1)}, u32[]{:S(2)}, u32[]{:S(2)}) collective-permute-start(f32[64,8,128]{2,1,0:T(8,128)S(1)} %slice_add_fusion.8), channel_id=1, source_target_pairs={{0,4},{2,6},{4,0},{6,2},{8,12},{10,14},{12,8},{14,10},{1,5},{3,7},... | collective-permute-start | bytes 786440 | tf_op jit(solution)/shard_map/ppermute | solution.py:578
  107.3 10.1 %collective-permute-start.27 = (f32[32,8,128]{2,1,0:T(8,128)S(1)}, f32[32,8,128]{2,1,0:T(8,128)S(1)}, u32[]{:S(2)}, u32[]{:S(2)}) collective-permute-start(f32[32,8,128]{2,1,0:T(8,128)S(1)} %slice_add_fusion.45), channel_id=1, source_target_pairs={{0,2},{2,0},{4,6},{6,4},{8,10},{10,8},{12,14},{14,12},{1,3},{3,1},... | collective-permute-start | bytes 393224 | tf_op jit(solution)/shard_map/ppermute | solution.py:578
  107.6 7.0 %collective-permute-start.24 = (f32[32,8,128]{2,1,0:T(8,128)S(1)}, f32[32,8,128]{2,1,0:T(8,128)S(1)}, u32[]{:S(2)}, u32[]{:S(2)}) collective-permute-start(f32[32,8,128]{2,1,0:T(8,128)S(1)} %slice_add_fusion.33), channel_id=1, source_target_pairs={{0,8},{2,10},{4,12},{6,14},{8,0},{10,2},{12,4},{14,6},{1,9},{3,11}... | collective-permute-start | bytes 393224 | tf_op jit(solution)/shard_map/ppermute | solution.py:578
  114.6 6.8 %collective-permute-start.26 = (f32[32,8,128]{2,1,0:T(8,128)S(1)}, f32[32,8,128]{2,1,0:T(8,128)S(1)}, u32[]{:S(2)}, u32[]{:S(2)}) collective-permute-start(f32[32,8,128]{2,1,0:T(8,128)S(1)} %slice_add_fusion.27), channel_id=1, source_target_pairs={{0,8},{2,10},{4,12},{6,14},{8,0},{10,2},{12,4},{14,6},{1,9},{3,11}... | collective-permute-start | bytes 393224 | tf_op jit(solution)/shard_map/ppermute | solution.py:578
  118.5 3.7 %copy-start = (s32[32,128]{1,0:T(8,128)S(1)}, s32[32,128]{1,0:T(8,128)}, u32[]{:S(2)}) copy-start(s32[32,128]{1,0:T(8,128)} %refs_2_.3) | copy-start | bytes 49156
  118.5 3.6 %copy-start.1 = (s32[32]{0:T(128)S(1)}, s32[32]{0:T(128)}, u32[]{:S(2)}) copy-start(s32[32]{0:T(128)} %refs_1_.2) | copy-start | bytes 388
  123.7 9.8 %collective-permute-start.28 = (f32[30,8,128]{2,1,0:T(8,128)S(1)}, f32[30,8,128]{2,1,0:T(8,128)S(1)}, u32[]{:S(2)}, u32[]{:S(2)}) collective-permute-start(f32[30,8,128]{2,1,0:T(8,128)S(1)} %get-tuple-element.86), channel_id=1, source_target_pairs={{0,2},{2,0},{4,6},{6,4},{8,10},{10,8},{12,14},{14,12},{1,3},{3,1},... | collective-permute-start | bytes 368648 | tf_op jit(solution)/shard_map/ppermute | solution.py:649
  124.2 13.1 %collective-permute-start.29 = (f32[30,8,128]{2,1,0:T(8,128)S(1)}, f32[30,8,128]{2,1,0:T(8,128)S(1)}, u32[]{:S(2)}, u32[]{:S(2)}) collective-permute-start(f32[30,8,128]{2,1,0:T(8,128)S(1)} %get-tuple-element.88), channel_id=1, source_target_pairs={{0,4},{2,6},{4,0},{6,2},{8,12},{10,14},{12,8},{14,10},{1,5},{3,7},... | collective-permute-start | bytes 368648 | tf_op jit(solution)/shard_map/ppermute | solution.py:649
  127.7 13.4 %collective-permute-start.30 = (f32[30,8,128]{2,1,0:T(8,128)S(1)}, f32[30,8,128]{2,1,0:T(8,128)S(1)}, u32[]{:S(2)}, u32[]{:S(2)}) collective-permute-start(f32[30,8,128]{2,1,0:T(8,128)S(1)} %get-tuple-element.90), channel_id=1, source_target_pairs={{0,6},{2,4},{4,2},{6,0},{8,14},{10,12},{12,10},{14,8},{1,7},{3,5},... | collective-permute-start | bytes 368648 | tf_op jit(solution)/shard_map/ppermute | solution.py:649
  127.8 13.3 %collective-permute-start.31 = (f32[30,8,128]{2,1,0:T(8,128)S(1)}, f32[30,8,128]{2,1,0:T(8,128)S(1)}, u32[]{:S(2)}, u32[]{:S(2)}) collective-permute-start(f32[30,8,128]{2,1,0:T(8,128)S(1)} %get-tuple-element.92), channel_id=1, source_target_pairs={{0,8},{2,10},{4,12},{6,14},{8,0},{10,2},{12,4},{14,6},{1,9},{3,11}... | collective-permute-start | bytes 368648 | tf_op jit(solution)/shard_map/ppermute | solution.py:649
  133.3 7.8 %collective-permute-start.32 = (f32[30,8,128]{2,1,0:T(8,128)S(1)}, f32[30,8,128]{2,1,0:T(8,128)S(1)}, u32[]{:S(2)}, u32[]{:S(2)}) collective-permute-start(f32[30,8,128]{2,1,0:T(8,128)S(1)} %get-tuple-element.94), channel_id=1, source_target_pairs={{0,10},{2,8},{4,14},{6,12},{8,2},{10,0},{12,6},{14,4},{1,11},{3,9}... | collective-permute-start | bytes 368648 | tf_op jit(solution)/shard_map/ppermute | solution.py:649
  133.5 8.2 %collective-permute-start.33 = (f32[30,8,128]{2,1,0:T(8,128)S(1)}, f32[30,8,128]{2,1,0:T(8,128)S(1)}, u32[]{:S(2)}, u32[]{:S(2)}) collective-permute-start(f32[30,8,128]{2,1,0:T(8,128)S(1)} %get-tuple-element.96), channel_id=1, source_target_pairs={{0,12},{2,14},{4,8},{6,10},{8,4},{10,6},{12,0},{14,2},{1,13},{3,15... | collective-permute-start | bytes 368648 | tf_op jit(solution)/shard_map/ppermute | solution.py:649
  137.2 7.7 %collective-permute-start.34 = (f32[30,8,128]{2,1,0:T(8,128)S(1)}, f32[30,8,128]{2,1,0:T(8,128)S(1)}, u32[]{:S(2)}, u32[]{:S(2)}) collective-permute-start(f32[30,8,128]{2,1,0:T(8,128)S(1)} %get-tuple-element.98), channel_id=1, source_target_pairs={{0,14},{2,12},{4,10},{6,8},{8,6},{10,4},{12,2},{14,0},{1,15},{3,13... | collective-permute-start | bytes 368648 | tf_op jit(solution)/shard_map/ppermute | solution.py:649
  146.4 1.6 %collective-permute-start.35 = (f32[58,8,128]{2,1,0:T(8,128)S(1)}, f32[58,8,128]{2,1,0:T(8,128)S(1)}, u32[]{:S(2)}, u32[]{:S(2)}) collective-permute-start(f32[58,8,128]{2,1,0:T(8,128)S(1)} %get-tuple-element.101), channel_id=1, source_target_pairs={{0,1},{1,0},{2,3},{3,2},{4,5},{5,4},{6,7},{7,6},{8,9},{9,8},{10,11... | collective-permute-start | bytes 712712 | tf_op jit(solution)/shard_map/ppermute | solution.py:575
